TPU v7x, 32 devices: a whole 2x2x4 slice. The times are simulated.
32 devices in a mesh: groups: 2 (over y), ops: 16 (over z, x, core).
Axes of the slice: x: 2, y: 2, z: 4, core: 2. Of those that a mesh axis runs over, the one named last changes fastest.
Arguments:
- psi: bfloat16 [32, 128, 128], P(('groups', 'ops')), parts along dimension 0, may hold values from -6 to 6
- left_ops: bfloat16 [512, 128, 128], P(('groups', 'ops')), parts along dimension 0, may hold values from -0.5 to 0.5
- right_ops: bfloat16 [512, 128, 128], P(('groups', 'ops')), parts along dimension 0, may hold values from -0.125 to 0.125
- couplings: int32 [3, 12288], P(None, ('groups', 'ops')), parts along dimension 1, may hold values from 0 to 15, as said below
- live: int32 [32], P(('groups', 'ops')), parts along dimension 0, may hold values from 48 to 384, as said below
Outputs:
- sigma: float32 [32, 128, 128], P(('groups', 'ops')), parts along dimension 0
There are 2 independent parts, one for each index of `groups`. A program takes and returns all parts, laid end to end along the dimension named above; each array names one. Nothing has to cross between parts.
Inputs may be any that keep to these rules, and one draw needn't show every extreme that they name: `couplings`: row 0 lies in 0 to 15, rows 1 and 2 in 0 to 15. Some list has all 384 slots live, and some list only 48.
All inputs are finite; a program needn't handle non-finite values.
Results may differ from a plain program's by a relative error of at most 0.0029.
Values may be sent and summed in bfloat16 or wider, within the bound.
No kernel may reach another device: no remote copies, remote signals or barrier semaphores. Data moves between devices by JAX's collectives and lax.ppermute only.
A program may use at most 128 MiB of HBM per device.

v0:
```python
import jax
import jax.numpy as jnp
from jax import lax
from jax.experimental import pallas as pl
from jax.experimental.pallas import tpu as pltpu
from jax.sharding import PartitionSpec as P

VMEM = pl.BlockSpec(memory_space=pltpu.VMEM)
SMEM = pl.BlockSpec(memory_space=pltpu.SMEM)

BLOCKS, CELL_BLOCK, SUM, ENDS, ORDER_SIZE = 0, 384, 640, 896, 1024
COUNT_BITS = 10


def transposed_dot(a, b):
    return lax.dot_general(
        a, b, (((1,), (1,)), ((), ())), preferred_element_type=jnp.float32
    )


def iota(shape, axis):
    return lax.broadcasted_iota(jnp.int32, shape, axis)


def count(mask, axis):
    return jnp.sum(mask.astype(jnp.float32), axis=axis, keepdims=True).astype(jnp.int32)


def picked(mask, values, axis):
    kept = jnp.where(mask, values, 0).astype(jnp.float32)
    return jnp.sum(kept, axis=axis, keepdims=True).astype(jnp.int32)


def as_column(row):
    n = row.shape[1]
    return picked(iota((n, n), 0) == iota((n, n), 1), row, 1)


CHAINS = ((3, 2, 1), (1, 3, 2))
OPS = 16


def partners(step):
    return [(i, i ^ (1 << CHAINS[i & 1][step])) for i in range(OPS)]


def other_core(x):
    return lax.ppermute(x, "ops", [(i, i ^ 1) for i in range(OPS)])


def place(sector, me):
    near = sector ^ me
    spots = [
        sum(((near >> bit) & 1) << step for step, bit in enumerate(chain)) for chain in CHAINS
    ]
    return (near & 1) * (OPS // 2) + jnp.where(sector & 1 == 0, spots[0], spots[1])


def order_kernel(nops, coup_ref, out_ref):
    slots = coup_ref.shape[1]
    cells = OPS * nops
    me = lax.axis_index("ops").astype(jnp.int32)

    g = coup_ref[0:1, :]
    alive = iota((1, slots), 1) < coup_ref[3:4, :]
    cell = jnp.where(alive, place(coup_ref[2:3, :], me) * nops + g, cells)
    block = place(coup_ref[1:2, :], me) * nops + g
    cell_col = as_column(cell)
    block_col = as_column(block)
    square = (slots, slots)
    ahead = (cell < cell_col) | ((cell == cell_col) & (iota(square, 1) < iota(square, 0)))
    spot_col = count(ahead, 1)
    out_ref[:, BLOCKS : BLOCKS + slots] = picked(spot_col == iota(square, 1), block_col, 0)

    lane = iota((1, cells), 1)
    first = count(cell_col < lane, 0)
    here = cell_col == lane
    number = count(here, 0)
    only = picked(here, block_col, 0)
    few = (number <= 4).astype(jnp.int32) + (number <= 2).astype(jnp.int32)
    group = (lane < cells // 2).astype(jnp.int32) + (lane < cells // 4).astype(jnp.int32)
    kind = jnp.where(number < 2, 9, few + 3 * group)
    square = (cells, cells)
    kind_col = as_column(kind)
    ahead = (kind_col < kind) | ((kind_col == kind) & (iota(square, 0) < iota(square, 1)))
    spot = count(ahead, 0)
    cell_block = jnp.where(number == 0, cells, jnp.where(number == 1, only, cells + 1 + spot))
    chosen = as_column(spot) == iota(square, 1)
    out_ref[:, CELL_BLOCK : CELL_BLOCK + cells] = cell_block
    firsts = picked(chosen, as_column(first), 0)
    out_ref[:, SUM : SUM + cells] = (firsts << COUNT_BITS) + picked(chosen, as_column(number), 0)
    small = iota((1, 128), 1)
    ends = jnp.zeros((1, 128), jnp.int32)
    for k in range(9):
        ends = jnp.where(small == k, count(kind <= k, 1), ends)
    out_ref[:, ENDS : ENDS + 128] = ends


def params(limit):
    return pltpu.CompilerParams(vmem_limit_bytes=limit * 1024 * 1024)


def cost(flops):
    return pl.CostEstimate(flops=flops, bytes_accessed=1 << 20, transcendentals=0)


def order_slots(nops, couplings, live):
    slots = couplings.shape[1]
    rows = jnp.concatenate([couplings, jnp.broadcast_to(live[None], (1, slots))], axis=0)
    return pl.pallas_call(
        lambda *refs: order_kernel(nops, *refs),
        out_shape=jax.ShapeDtypeStruct((1, ORDER_SIZE), jnp.int32),
        in_specs=[VMEM],
        out_specs=VMEM,
        compiler_params=params(16),
        cost_estimate=cost(20 * slots * slots),
        name="order",
    )(rows)


def hold_kernel(psi_ref, left_ref, psi_out, left_out):
    psi_out[...] = psi_ref[...]
    left_out[...] = left_ref[...]


def hold(psi, left_ops):
    return pl.pallas_call(
        hold_kernel,
        out_shape=[jax.ShapeDtypeStruct(x.shape, x.dtype) for x in (psi, left_ops)],
        in_specs=[VMEM] * 2,
        out_specs=[VMEM] * 2,
        compiler_params=params(4),
        cost_estimate=cost(0),
        name="hold",
    )(psi, left_ops)


def turn_kernel(right_ref, turned_ref):
    nops, m, _ = right_ref.shape
    for g in range(nops):
        turned_ref[g * m : (g + 1) * m] = right_ref[g].T


def turn(right_ops):
    nops, m, _ = right_ops.shape
    return pl.pallas_call(
        turn_kernel,
        out_shape=jax.ShapeDtypeStruct((nops * m, m), jnp.bfloat16),
        in_specs=[VMEM],
        out_specs=VMEM,
        compiler_params=params(4),
        cost_estimate=cost(0),
        name="turn",
    )(right_ops)


def add_up(order, block_ref, cells, begin, ends):
    many, some, two = ends
    m = block_ref.shape[1]

    def cell(k):
        packed = order(SUM + k)
        return packed >> COUNT_BITS, packed & ((1 << COUNT_BITS) - 1)

    @pl.loop(begin, many)
    def _(k):
        first, number = cell(k)

        def add(j, total):
            return total + block_ref[order(BLOCKS + first + j)].astype(jnp.float32)

        total = lax.fori_loop(0, number, add, jnp.zeros((m, m), jnp.float32))
        block_ref[cells + 1 + k] = total.astype(jnp.bfloat16)

    @pl.loop(many, some)
    def _(k):
        first, number = cell(k)
        fourth = jnp.where(number == 4, order(BLOCKS + first + 3), cells)
        total = block_ref[order(BLOCKS + first)].astype(jnp.float32)
        total += block_ref[order(BLOCKS + first + 1)].astype(jnp.float32)
        total += block_ref[order(BLOCKS + first + 2)].astype(jnp.float32)
        total += block_ref[fourth].astype(jnp.float32)
        block_ref[cells + 1 + k] = total.astype(jnp.bfloat16)

    @pl.loop(some, two, step=2)
    def _(k):
        ks = (k, jnp.minimum(k + 1, two - 1))
        firsts = [cell(k)[0] for k in ks]
        totals = [
            block_ref[order(BLOCKS + first)] + block_ref[order(BLOCKS + first + 1)]
            for first in firsts
        ]
        for k, total in zip(ks, totals):
            block_ref[cells + 1 + k] = total


def multiply(order, block_ref, turned_ref, out_ref, offset, nops):
    half, m, _ = out_ref.shape
    for t in range(0, half, 2):
        rows = [
            jnp.concatenate(
                [
                    block_ref[order(CELL_BLOCK + (offset + t + i) * nops + g)]
                    for g in range(nops)
                ],
                axis=1,
            )
            for i in range(2)
        ]
        out = jnp.dot(
            jnp.concatenate(rows, axis=0), turned_ref[...], preferred_element_type=jnp.float32
        )
        out_ref[t : t + 2] = out.reshape(2, m, m)


def fill(psi_ref, left_ref, block_ref, offset):
    nops, m, _ = left_ref.shape
    step = 4
    for s in range(0, psi_ref.shape[0], 2):
        pair = jnp.concatenate([psi_ref[s], psi_ref[s + 1]], axis=1)
        for g in range(0, nops, step):
            rows = left_ref[g : g + step].reshape(step * m, m)
            both = jnp.dot(rows, pair, preferred_element_type=jnp.float32).astype(jnp.bfloat16)
            at = (offset + s) * nops + g
            block_ref[at : at + step] = both[:, :m].reshape(step, m, m)
            block_ref[at + nops : at + nops + step] = both[:, m:].reshape(step, m, m)


def early_kernel(psi_ref, left_ref, block_ref):
    nops, m, _ = left_ref.shape
    fill(psi_ref, left_ref, block_ref, 0)
    block_ref[OPS * nops] = jnp.zeros((m, m), jnp.bfloat16)


def early(psi, left, slots):
    nops, m, _ = left.shape
    cells = OPS * nops
    return pl.pallas_call(
        early_kernel,
        out_shape=jax.ShapeDtypeStruct((cells + 1 + slots // 2, m, m), jnp.bfloat16),
        in_specs=[VMEM] * 2,
        out_specs=VMEM,
        compiler_params=params(24),
        cost_estimate=cost(2 * psi.shape[0] * nops * m**3),
        name="early",
    )(psi, left)


def more(psi, left, blocks, offset):
    nops, m, _ = left.shape

    def kernel(psi_ref, left_ref, _, block_ref):
        fill(psi_ref, left_ref, block_ref, offset)

    return pl.pallas_call(
        kernel,
        out_shape=jax.ShapeDtypeStruct(blocks.shape, blocks.dtype),
        in_specs=[VMEM] * 3,
        out_specs=VMEM,
        input_output_aliases={2: 0},
        compiler_params=params(24),
        cost_estimate=cost(2 * psi.shape[0] * nops * m**3),
        name="more",
    )(psi, left, blocks)


def terms(order, turned, blocks, group, offset, number, psi=None, left=None):
    m = blocks.shape[1]
    nops = turned.shape[0] // m
    cells = OPS * nops
    extra = [] if psi is None else [psi, left]

    def kernel(order_in, turned_ref, *refs):
        block_ref, out_ref, order_ref, sem = refs[-4:]
        copy = pltpu.make_async_copy(order_in, order_ref, sem)
        copy.start()
        if extra:
            fill(refs[0], refs[1], block_ref, OPS // 2)
        copy.wait()

        def order(i):
            return order_ref[0, i]

        begin = order(ENDS + 3 * group - 1) if group else 0
        ends = [order(ENDS + 3 * group + k) for k in range(3)]
        add_up(order, block_ref, cells, begin, ends)
        multiply(order, block_ref, turned_ref, out_ref, offset, nops)

    return pl.pallas_call(
        kernel,
        out_shape=[
            jax.ShapeDtypeStruct(blocks.shape, blocks.dtype),
            jax.ShapeDtypeStruct((number, m, m), jnp.float32),
        ],
        in_specs=[VMEM] * (3 + len(extra)),
        out_specs=[VMEM] * 2,
        scratch_shapes=[pltpu.SMEM(order.shape, jnp.int32), pltpu.SemaphoreType.DMA],
        input_output_aliases={2 + len(extra): 0},
        compiler_params=params(24),
        cost_estimate=cost(2 * (number + len(extra) * 4) * nops * m**3),
        name=f"terms_{group}",
    )(order, turned, *extra, blocks)


def slot_kernel(live_ref, coup_ref, psi_ref, left_ref, right_ref, out_ref):
    out_ref[...] = jnp.zeros_like(out_ref)

    @pl.loop(0, live_ref[0])
    def _(c):
        g = coup_ref[0, c]
        half = jnp.dot(left_ref[g], psi_ref[coup_ref[1, c]], preferred_element_type=jnp.float32)
        out_ref[coup_ref[2, c]] += transposed_dot(half.astype(jnp.bfloat16), right_ref[g])


def by_slot(whole, left_ops, right_ops, couplings, live):
    return pl.pallas_call(
        slot_kernel,
        out_shape=jax.ShapeDtypeStruct(whole.shape, jnp.float32),
        in_specs=[SMEM] * 2 + [VMEM] * 3,
        out_specs=VMEM,
        compiler_params=pltpu.CompilerParams(vmem_limit_bytes=60 * 1024 * 1024),
        name="slots",
    )(live, couplings, whole, left_ops, right_ops)


def shards_small(psi, left_ops, right_ops, couplings, live):
    slots = couplings.shape[1]
    came = lax.ppermute(psi, "ops", partners(0))
    psi, left = hold(psi, left_ops)
    two, left = lax.optimization_barrier((jnp.concatenate([psi, came], axis=0), left))
    came = lax.ppermute(two, "ops", partners(1))
    order = order_slots(left_ops.shape[0], couplings, live)
    four, order = lax.optimization_barrier((jnp.concatenate([two, came], axis=0), order))
    came = lax.ppermute(four, "ops", partners(2))
    blocks = early(four, left, slots)
    turned = turn(right_ops)
    eight, turned, blocks = lax.optimization_barrier(
        (jnp.concatenate([four, came], axis=0), turned, blocks)
    )
    far = other_core(eight)
    blocks = more(came, left, blocks, 4)
    blocks, send = terms(order, turned, blocks, 0, 8, 8, far, left)
    came = other_core(send)
    blocks, next_four = terms(order, turned, blocks, 1, 4, 4)
    leaving = (next_four + came[4:]).astype(jnp.bfloat16)
    arrived = lax.ppermute(leaving, "ops", partners(2))
    _, last_four = terms(order, turned, blocks, 2, 0, 4)
    keep = last_four + came[:4]
    for step in (1, 0):
        half = keep.shape[0] // 2
        both = keep + arrived.astype(jnp.float32)
        keep, leaving = both[:half], both[half:].astype(jnp.bfloat16)
        arrived = lax.ppermute(leaving, "ops", partners(step))
    return keep + arrived.astype(jnp.float32)


def shards_large(psi, left_ops, right_ops, couplings, live):
    whole = lax.all_gather(psi, "ops", axis=0, tiled=True)
    total = by_slot(whole, left_ops, right_ops, couplings, live)
    return lax.psum_scatter(total, "ops", scatter_dimension=0, tiled=True)


def solution(mesh):
    ops = mesh.shape["ops"]
    placed = (
        P(("groups", "ops"), None, None),
        P(("groups", "ops"), None, None),
        P(("groups", "ops"), None, None),
        P(None, ("groups", "ops")),
        P(("groups", "ops")),
    )

    def shards(psi, *rest):
        if ops == OPS and psi.shape[0] == 1 and rest[0].shape[0] == 16 and rest[2].shape[1] == 384:
            return shards_small(psi, *rest)
        return shards_large(psi, *rest)

    return jax.shard_map(
        shards,
        mesh=mesh,
        in_specs=placed,
        out_specs=P(("groups", "ops"), None, None),
        check_vma=False,
    )
```

profile of v0, /device:TPU:0, one launch (start us, length us, event | category | flops | bytes accessed | tf_op | source)
XLA Modules:
  0.0 38.1 jit_solution(15032236917341964593)
XLA Ops:
  0.0 4.0 %collective-permute-start = (bf16[1,128,128]{2,1,0:T(8,128)(2,1)}, bf16[1,128,128]{2,1,0:T(8,128)(2,1)S(1)}, u32[]{:S(2)}, u32[]{:S(2)}) collective-permute-start(bf16[1,128,128]{2,1,0:T(8,128)(2,1)} %psi_ref.1), channel_id=1, source_target_pairs={{0,8},{1,3},{2,10},{3,1},{4,12},{5,7},{6,14},{7,5},{8,0},{9,11},{1... | collective-permute-start | bytes 98312 | tf_op jit(solution)/shard_map/ppermute | solution.py:328
  4.0 0.0 copy-start
  4.0 1.0 %copy-done = bf16[16,128,128]{2,1,0:T(8,128)(2,1)S(1)} copy-done((bf16[16,128,128]{2,1,0:T(8,128)(2,1)S(1)}, bf16[16,128,128]{2,1,0:T(8,128)(2,1)}, u32[]{:S(2)}) %copy-start) | copy-done | bytes 524312
  5.1 0.0 copy-start.2
  5.1 0.8 %copy-done.2 = bf16[1,128,128]{2,1,0:T(8,128)(2,1)S(1)} copy-done((bf16[1,128,128]{2,1,0:T(8,128)(2,1)S(1)}, bf16[1,128,128]{2,1,0:T(8,128)(2,1)}, u32[]{:S(2)}) %copy-start.2) | copy-done | bytes 32792
  5.9 0.3 collective-permute-done
  6.2 2.0 %collective-permute-start.1 = (bf16[2,128,128]{2,1,0:T(8,128)(2,1)S(1)}, bf16[2,128,128]{2,1,0:T(8,128)(2,1)S(1)}, u32[]{:S(2)}, u32[]{:S(2)}) collective-permute-start(bf16[2,128,128]{2,1,0:T(8,128)(2,1)S(1)} %pad_maximum_fusion.2), channel_id=1, source_target_pairs={{0,4},{1,9},{2,6},{3,11},{4,0},{5,13},{6,2},{7,15},{8,12},{9,1},{1... | collective-permute-start | bytes 196616 | tf_op jit(solution)/shard_map/ppermute | solution.py:331
  8.8 0.7 %concatenate.14.refs_0_ = s32[4,384]{1,0:T(4,128)S(1)} pad(s32[3,384]{1,0:T(4,128)} %param.8, s32[]{:T(128)} %bitcast.1), padding=0_1x0_0 | pad | bytes 10756 | tf_op jit(solution)/shard_map/concatenate | solution.py:109
  9.5 0.6 %order.1.order_in = s32[1,1024]{1,0:T(1,128)S(1)} custom-call(s32[4,384]{1,0:T(4,128)S(1)} %concatenate.14.refs_0_), custom_call_target="tpu_custom_call" | custom-call | flops 2949120 | bytes 1048576 | tf_op jit(solution)/shard_map/order/pallas_call | solution.py:110
  10.1 0.4 collective-permute-done.1
  10.5 1.9 %collective-permute-start.2 = (bf16[4,128,128]{2,1,0:T(8,128)(2,1)S(1)}, bf16[4,128,128]{2,1,0:T(8,128)(2,1)S(1)}, u32[]{:S(2)}, u32[]{:S(2)}) collective-permute-start(bf16[4,128,128]{2,1,0:T(8,128)(2,1)S(1)} %pad_maximum_fusion.1.psi_ref), channel_id=1, source_target_pairs={{0,2},{1,5},{2,0},{3,7},{4,6},{5,1},{6,4},{7,3},{8,10},{9,13},{10,... | collective-permute-start | bytes 393224 | tf_op jit(solution)/shard_map/ppermute | solution.py:334
  12.4 0.0 copy-start.1
  12.4 1.0 %copy-done.1 = bf16[16,128,128]{2,1,0:T(8,128)(2,1)S(1)} copy-done((bf16[16,128,128]{2,1,0:T(8,128)(2,1)S(1)}, bf16[16,128,128]{2,1,0:T(8,128)(2,1)}, u32[]{:S(2)}) %copy-start.1) | copy-done | bytes 524312
  13.4 0.2 turn.1.turned_ref
  13.6 0.7 %early.1._ = bf16[449,128,128]{2,1,0:T(8,128)(2,1)S(1)} custom-call(bf16[4,128,128]{2,1,0:T(8,128)(2,1)S(1)} %pad_maximum_fusion.1.psi_ref, bf16[16,128,128]{2,1,0:T(8,128)(2,1)S(1)} %get-tuple-element.24.left_ref.refs_1_), custom_call_target="tpu_custom_call" | custom-call | flops 268435456 | bytes 1048576 | tf_op jit(solution)/shard_map/early/pallas_call | solution.py:238
  14.3 1.2 %collective-permute-done.2.psi_ref = bf16[4,128,128]{2,1,0:T(8,128)(2,1)S(1)} collective-permute-done((bf16[4,128,128]{2,1,0:T(8,128)(2,1)S(1)}, bf16[4,128,128]{2,1,0:T(8,128)(2,1)S(1)}, u32[]{:S(2)}, u32[]{:S(2)}) %collective-permute-start.2) | collective-permute-done | bytes 131104 | tf_op jit(solution)/shard_map/ppermute | solution.py:334
  15.6 0.1 collective-permute-start.3
  15.6 0.7 %more.1.refs_2_ = bf16[449,128,128]{2,1,0:T(8,128)(2,1)S(1)} custom-call(bf16[4,128,128]{2,1,0:T(8,128)(2,1)S(1)} %collective-permute-done.2.psi_ref, bf16[16,128,128]{2,1,0:T(8,128)(2,1)S(1)} %get-tuple-element.24.left_ref.refs_1_, bf16[449,128,128]{2,1,0:T(8,128)(2,1)S(1)} %early.1._), custom_call_target="tpu_custom_call", output_to_operand_aliasing={{}: (2, {})} | custom-call | flops 268435456 | bytes 1048576 | tf_op jit(solution)/shard_map/more/pallas_call | solution.py:255
  16.3 0.8 %collective-permute-done.3.refs_0_ = bf16[8,128,128]{2,1,0:T(8,128)(2,1)S(1)} collective-permute-done((bf16[8,128,128]{2,1,0:T(8,128)(2,1)S(1)}, bf16[8,128,128]{2,1,0:T(8,128)(2,1)S(1)}, u32[]{:S(2)}, u32[]{:S(2)}) %collective-permute-start.3) | collective-permute-done | bytes 262176 | tf_op jit(solution)/shard_map/ppermute | solution.py:48
  17.2 2.6 %terms_0.1 = (bf16[449,128,128]{2,1,0:T(8,128)(2,1)S(1)}, f32[8,128,128]{2,1,0:T(8,128)S(1)}) custom-call(s32[1,1024]{1,0:T(1,128)S(1)} %order.1.order_in, bf16[2048,128]{1,0:T(8,128)(2,1)S(1)} %turn.1.turned_ref, bf16[8,128,128]{2,1,0:T(8,128)(2,1)S(1)} %collective-permute-done.3.refs_0_, ...), custom_call_target="tpu_custom_call", output_to_operand_aliasing={{0}: (4, {})} | custom-call | flops 1073741824 | bytes 1048576 | tf_op jit(solution)/shard_map/terms_0/pallas_call | solution.py:289
  19.8 1.0 %collective-permute-start.4 = (f32[8,128,128]{2,1,0:T(8,128)S(1)}, f32[8,128,128]{2,1,0:T(8,128)S(1)}, u32[]{:S(2)}, u32[]{:S(2)}) collective-permute-start(f32[8,128,128]{2,1,0:T(8,128)S(1)} %get-tuple-element.31), channel_id=1, source_target_pairs={{0,1},{1,0},{2,3},{3,2},{4,5},{5,4},{6,7},{7,6},{8,9},{9,8},{10,11... | collective-permute-start | bytes 1572872 | tf_op jit(solution)/shard_map/ppermute | solution.py:48
  20.8 1.4 %terms_1.1 = (bf16[449,128,128]{2,1,0:T(8,128)(2,1)S(1)}, f32[4,128,128]{2,1,0:T(8,128)S(1)}) custom-call(s32[1,1024]{1,0:T(1,128)S(1)} %order.1.order_in, bf16[2048,128]{1,0:T(8,128)(2,1)S(1)} %turn.1.turned_ref, bf16[449,128,128]{2,1,0:T(8,128)(2,1)S(1)} %get-tuple-element.28.refs_0_), custom_call_target="tpu_custom_call", output_to_operand_aliasing={{0}: (2, {})} | custom-call | flops 268435456 | bytes 1048576 | tf_op jit(solution)/shard_map/terms_1/pallas_call | solution.py:289
  22.2 0.2 collective-permute-done.4
  22.4 1.5 %collective-permute-start.5 = (bf16[4,128,128]{2,1,0:T(8,128)(2,1)S(1)}, bf16[4,128,128]{2,1,0:T(8,128)(2,1)S(1)}, u32[]{:S(2)}, u32[]{:S(2)}) collective-permute-start(bf16[4,128,128]{2,1,0:T(8,128)(2,1)S(1)} %fusion), channel_id=1, source_target_pairs={{0,2},{1,5},{2,0},{3,7},{4,6},{5,1},{6,4},{7,3},{8,10},{9,13},{10,... | collective-permute-start | bytes 393224 | tf_op jit(solution)/shard_map/ppermute | solution.py:346
  23.9 1.4 %terms_2.1 = (bf16[449,128,128]{2,1,0:T(8,128)(2,1)S(1)}, f32[4,128,128]{2,1,0:T(8,128)S(1)}) custom-call(s32[1,1024]{1,0:T(1,128)S(1)} %order.1.order_in, bf16[2048,128]{1,0:T(8,128)(2,1)S(1)} %turn.1.turned_ref, bf16[449,128,128]{2,1,0:T(8,128)(2,1)S(1)} %get-tuple-element.29.refs_0_), custom_call_target="tpu_custom_call", output_to_operand_aliasing={{0}: (2, {})} | custom-call | flops 268435456 | bytes 1048576 | tf_op jit(solution)/shard_map/terms_2/pallas_call | solution.py:289
  25.3 2.1 %collective-permute-done.5 = bf16[4,128,128]{2,1,0:T(8,128)(2,1)S(1)} collective-permute-done((bf16[4,128,128]{2,1,0:T(8,128)(2,1)S(1)}, bf16[4,128,128]{2,1,0:T(8,128)(2,1)S(1)}, u32[]{:S(2)}, u32[]{:S(2)}) %collective-permute-start.5) | collective-permute-done | bytes 131104 | tf_op jit(solution)/shard_map/ppermute | solution.py:346
  27.5 2.0 %collective-permute-start.6 = (bf16[2,128,128]{2,1,0:T(8,128)(2,1)S(1)}, bf16[2,128,128]{2,1,0:T(8,128)(2,1)S(1)}, u32[]{:S(2)}, u32[]{:S(2)}) collective-permute-start(bf16[2,128,128]{2,1,0:T(8,128)(2,1)S(1)} %slice.42), channel_id=1, source_target_pairs={{0,4},{1,9},{2,6},{3,11},{4,0},{5,13},{6,2},{7,15},{8,12},{9,1},{1... | collective-permute-start | bytes 196616 | tf_op jit(solution)/shard_map/ppermute | solution.py:353
  29.5 3.0 %collective-permute-done.6 = bf16[2,128,128]{2,1,0:T(8,128)(2,1)S(1)} collective-permute-done((bf16[2,128,128]{2,1,0:T(8,128)(2,1)S(1)}, bf16[2,128,128]{2,1,0:T(8,128)(2,1)S(1)}, u32[]{:S(2)}, u32[]{:S(2)}) %collective-permute-start.6) | collective-permute-done | bytes 65568 | tf_op jit(solution)/shard_map/ppermute | solution.py:353
  32.6 2.7 %collective-permute-start.7 = (bf16[1,128,128]{2,1,0:T(8,128)(2,1)S(1)}, bf16[1,128,128]{2,1,0:T(8,128)(2,1)S(1)}, u32[]{:S(2)}, u32[]{:S(2)}) collective-permute-start(bf16[1,128,128]{2,1,0:T(8,128)(2,1)S(1)} %slice.43), channel_id=1, source_target_pairs={{0,8},{1,3},{2,10},{3,1},{4,12},{5,7},{6,14},{7,5},{8,0},{9,11},{1... | collective-permute-start | bytes 98312 | tf_op jit(solution)/shard_map/ppermute | solution.py:353
  35.3 2.2 %collective-permute-done.7 = bf16[1,128,128]{2,1,0:T(8,128)(2,1)S(1)} collective-permute-done((bf16[1,128,128]{2,1,0:T(8,128)(2,1)S(1)}, bf16[1,128,128]{2,1,0:T(8,128)(2,1)S(1)}, u32[]{:S(2)}, u32[]{:S(2)}) %collective-permute-start.7) | collective-permute-done | bytes 32800 | tf_op jit(solution)/shard_map/ppermute | solution.py:353
  37.4 0.6 %slice_add_fusion.3 = f32[1,128,128]{2,1,0:T(8,128)} fusion(f32[2,128,128]{2,1,0:T(8,128)S(1)} %slice_add_fusion.2, bf16[1,128,128]{2,1,0:T(8,128)(2,1)S(1)} %collective-permute-done.7), kind=kLoop, calls=%fused_computation.9 | loop fusion | flops 32768 | bytes 163840 | tf_op jit(solution)/shard_map/add | solution.py:354
  (9 shorter events, 0.2 us)
Async XLA Ops:
  0.0 6.1 %collective-permute-start = (bf16[1,128,128]{2,1,0:T(8,128)(2,1)}, bf16[1,128,128]{2,1,0:T(8,128)(2,1)S(1)}, u32[]{:S(2)}, u32[]{:S(2)}) collective-permute-start(bf16[1,128,128]{2,1,0:T(8,128)(2,1)} %psi_ref.1), channel_id=1, source_target_pairs={{0,8},{1,3},{2,10},{3,1},{4,12},{5,7},{6,14},{7,5},{8,0},{9,11},{1... | collective-permute-start | bytes 98312 | tf_op jit(solution)/shard_map/ppermute | solution.py:328
  4.0 1.0 %copy-start = (bf16[16,128,128]{2,1,0:T(8,128)(2,1)S(1)}, bf16[16,128,128]{2,1,0:T(8,128)(2,1)}, u32[]{:S(2)}) copy-start(bf16[16,128,128]{2,1,0:T(8,128)(2,1)} %left_ref.1) | copy-start | bytes 1572868
  5.1 0.8 %copy-start.2 = (bf16[1,128,128]{2,1,0:T(8,128)(2,1)S(1)}, bf16[1,128,128]{2,1,0:T(8,128)(2,1)}, u32[]{:S(2)}) copy-start(bf16[1,128,128]{2,1,0:T(8,128)(2,1)} %psi_ref.1) | copy-start | bytes 98308
  6.2 4.3 %collective-permute-start.1 = (bf16[2,128,128]{2,1,0:T(8,128)(2,1)S(1)}, bf16[2,128,128]{2,1,0:T(8,128)(2,1)S(1)}, u32[]{:S(2)}, u32[]{:S(2)}) collective-permute-start(bf16[2,128,128]{2,1,0:T(8,128)(2,1)S(1)} %pad_maximum_fusion.2), channel_id=1, source_target_pairs={{0,4},{1,9},{2,6},{3,11},{4,0},{5,13},{6,2},{7,15},{8,12},{9,1},{1... | collective-permute-start | bytes 196616 | tf_op jit(solution)/shard_map/ppermute | solution.py:331
  10.5 5.0 %collective-permute-start.2 = (bf16[4,128,128]{2,1,0:T(8,128)(2,1)S(1)}, bf16[4,128,128]{2,1,0:T(8,128)(2,1)S(1)}, u32[]{:S(2)}, u32[]{:S(2)}) collective-permute-start(bf16[4,128,128]{2,1,0:T(8,128)(2,1)S(1)} %pad_maximum_fusion.1.psi_ref), channel_id=1, source_target_pairs={{0,2},{1,5},{2,0},{3,7},{4,6},{5,1},{6,4},{7,3},{8,10},{9,13},{10,... | collective-permute-start | bytes 393224 | tf_op jit(solution)/shard_map/ppermute | solution.py:334
  12.4 1.0 %copy-start.1 = (bf16[16,128,128]{2,1,0:T(8,128)(2,1)S(1)}, bf16[16,128,128]{2,1,0:T(8,128)(2,1)}, u32[]{:S(2)}) copy-start(bf16[16,128,128]{2,1,0:T(8,128)(2,1)} %right_ref.1) | copy-start | bytes 1572868
  15.6 1.6 %collective-permute-start.3 = (bf16[8,128,128]{2,1,0:T(8,128)(2,1)S(1)}, bf16[8,128,128]{2,1,0:T(8,128)(2,1)S(1)}, u32[]{:S(2)}, u32[]{:S(2)}) collective-permute-start(bf16[8,128,128]{2,1,0:T(8,128)(2,1)S(1)} %pad_maximum_fusion), channel_id=1, source_target_pairs={{0,1},{1,0},{2,3},{3,2},{4,5},{5,4},{6,7},{7,6},{8,9},{9,8},{10,11... | collective-permute-start | bytes 786440 | tf_op jit(solution)/shard_map/ppermute | solution.py:48
  19.8 2.6 %collective-permute-start.4 = (f32[8,128,128]{2,1,0:T(8,128)S(1)}, f32[8,128,128]{2,1,0:T(8,128)S(1)}, u32[]{:S(2)}, u32[]{:S(2)}) collective-permute-start(f32[8,128,128]{2,1,0:T(8,128)S(1)} %get-tuple-element.31), channel_id=1, source_target_pairs={{0,1},{1,0},{2,3},{3,2},{4,5},{5,4},{6,7},{7,6},{8,9},{9,8},{10,11... | collective-permute-start | bytes 1572872 | tf_op jit(solution)/shard_map/ppermute | solution.py:48
  22.4 5.0 %collective-permute-start.5 = (bf16[4,128,128]{2,1,0:T(8,128)(2,1)S(1)}, bf16[4,128,128]{2,1,0:T(8,128)(2,1)S(1)}, u32[]{:S(2)}, u32[]{:S(2)}) collective-permute-start(bf16[4,128,128]{2,1,0:T(8,128)(2,1)S(1)} %fusion), channel_id=1, source_target_pairs={{0,2},{1,5},{2,0},{3,7},{4,6},{5,1},{6,4},{7,3},{8,10},{9,13},{10,... | collective-permute-start | bytes 393224 | tf_op jit(solution)/shard_map/ppermute | solution.py:346
  27.5 5.0 %collective-permute-start.6 = (bf16[2,128,128]{2,1,0:T(8,128)(2,1)S(1)}, bf16[2,128,128]{2,1,0:T(8,128)(2,1)S(1)}, u32[]{:S(2)}, u32[]{:S(2)}) collective-permute-start(bf16[2,128,128]{2,1,0:T(8,128)(2,1)S(1)} %slice.42), channel_id=1, source_target_pairs={{0,4},{1,9},{2,6},{3,11},{4,0},{5,13},{6,2},{7,15},{8,12},{9,1},{1... | collective-permute-start | bytes 196616 | tf_op jit(solution)/shard_map/ppermute | solution.py:353
  32.6 4.9 %collective-permute-start.7 = (bf16[1,128,128]{2,1,0:T(8,128)(2,1)S(1)}, bf16[1,128,128]{2,1,0:T(8,128)(2,1)S(1)}, u32[]{:S(2)}, u32[]{:S(2)}) collective-permute-start(bf16[1,128,128]{2,1,0:T(8,128)(2,1)S(1)} %slice.43), channel_id=1, source_target_pairs={{0,8},{1,3},{2,10},{3,1},{4,12},{5,7},{6,14},{7,5},{8,0},{9,11},{1... | collective-permute-start | bytes 98312 | tf_op jit(solution)/shard_map/ppermute | solution.py:353
where the time goes:
time: 38.4 us; the launch traced here: 38.1 us
  starting transfers between devices  15.2 us (40%)
  waiting for transfers between devices  10.1 us (26%)
  Pallas kernels  7.66 us (20%)
  local copies, waits for them, and re-layouts  3.56 us (9%)
  other arithmetic  0.76 us (2%)
  between operations  0.76 us (2%)
    pallas_call x3, Pallas kernels, terms(): pl.pallas_call(kernel, out_shape=[jax.ShapeDtypeStruct(blocks.shape, bloc...  5.43 us
    ppermute x2, waiting for transfers between devices, shards_small(): arrived = lax.ppermute(leaving, 'ops', partners(step))  5.19 us
    ppermute x2, starting transfers between devices, shards_small(): arrived = lax.ppermute(leaving, 'ops', partners(step))  4.72 us
    ppermute x1, starting transfers between devices, shards_small(): came = lax.ppermute(psi, 'ops', partners(0))  4.04 us
    unnamed x6, local copies, waits for them, and re-layouts  2.84 us
    ppermute x1, waiting for transfers between devices, shards_small(): arrived = lax.ppermute(leaving, 'ops', partners(2))  2.11 us
    ppermute x1, starting transfers between devices, shards_small(): came = lax.ppermute(two, 'ops', partners(1))  1.97 us
    ppermute x1, starting transfers between devices, shards_small(): came = lax.ppermute(four, 'ops', partners(2))  1.89 us
  transfers between devices with their start and end apart: 8, of which 8 were waited for; matrix products, arithmetic and copies ran while one was open for 2% of the time, Pallas kernels for 13%

commit v1 on v0

--- a/solution.py
+++ b/solution.py
@@ -36,24 +36,22 @@
     return picked(iota((n, n), 0) == iota((n, n), 1), row, 1)
 
 
-CHAINS = ((3, 2, 1), (1, 3, 2))
+CHAIN = (3, 2, 1)
 OPS = 16
 
 
-def partners(step):
-    return [(i, i ^ (1 << CHAINS[i & 1][step])) for i in range(OPS)]
-
-
-def other_core(x):
-    return lax.ppermute(x, "ops", [(i, i ^ 1) for i in range(OPS)])
+def between_chips(x, step):
+    return lax.ppermute(x, "ops", [(i, i ^ (1 << CHAIN[step])) for i in range(1, OPS, 2)])
+
+
+def to_core(core, x):
+    return lax.ppermute(x, "ops", [(i ^ 1, i) for i in range(core, OPS, 2)])
 
 
 def place(sector, me):
     near = sector ^ me
-    spots = [
-        sum(((near >> bit) & 1) << step for step, bit in enumerate(chain)) for chain in CHAINS
-    ]
-    return (near & 1) * (OPS // 2) + jnp.where(sector & 1 == 0, spots[0], spots[1])
+    spot = sum(((near >> bit) & 1) << step for step, bit in enumerate(CHAIN))
+    return spot * 2 + (sector & 1)
 
 
 def order_kernel(nops, coup_ref, out_ref):
@@ -118,21 +116,20 @@
     )(rows)
 
 
-def hold_kernel(psi_ref, left_ref, psi_out, left_out):
-    psi_out[...] = psi_ref[...]
-    left_out[...] = left_ref[...]
-
-
-def hold(psi, left_ops):
+def hold_kernel(in_ref, out_ref):
+    out_ref[...] = in_ref[...]
+
+
+def hold(x):
     return pl.pallas_call(
         hold_kernel,
-        out_shape=[jax.ShapeDtypeStruct(x.shape, x.dtype) for x in (psi, left_ops)],
-        in_specs=[VMEM] * 2,
-        out_specs=[VMEM] * 2,
+        out_shape=jax.ShapeDtypeStruct(x.shape, x.dtype),
+        in_specs=[VMEM],
+        out_specs=VMEM,
         compiler_params=params(4),
         cost_estimate=cost(0),
         name="hold",
-    )(psi, left_ops)
+    )(x)
 
 
 def turn_kernel(right_ref, turned_ref):
@@ -325,33 +322,41 @@
 
 def shards_small(psi, left_ops, right_ops, couplings, live):
     slots = couplings.shape[1]
-    came = lax.ppermute(psi, "ops", partners(0))
-    psi, left = hold(psi, left_ops)
-    two, left = lax.optimization_barrier((jnp.concatenate([psi, came], axis=0), left))
-    came = lax.ppermute(two, "ops", partners(1))
+    first_core = lax.axis_index("ops") & 1 == 0
+
+    def shared(x):
+        return jnp.where(first_core, to_core(0, x), x)
+
+    came = lax.ppermute(psi, "ops", [(i, i ^ 1) for i in range(OPS)])
+    psi = hold(psi)
+    two = jnp.concatenate(
+        [jnp.where(first_core, psi, came), jnp.where(first_core, came, psi)], axis=0
+    )
+    came_two = between_chips(two, 0)
+    left = hold(left_ops)
+    four, left = lax.optimization_barrier((jnp.concatenate([two, came_two], axis=0), left))
+    came_four = between_chips(four, 1)
     order = order_slots(left_ops.shape[0], couplings, live)
-    four, order = lax.optimization_barrier((jnp.concatenate([two, came], axis=0), order))
-    came = lax.ppermute(four, "ops", partners(2))
-    blocks = early(four, left, slots)
+    eight, order = lax.optimization_barrier((jnp.concatenate([four, came_four], axis=0), order))
+    came_eight = between_chips(eight, 2)
+    blocks = early(jnp.concatenate([two, shared(came_two)], axis=0), left, slots)
+    blocks = more(shared(came_four), left, blocks, 4)
     turned = turn(right_ops)
-    eight, turned, blocks = lax.optimization_barrier(
-        (jnp.concatenate([four, came], axis=0), turned, blocks)
-    )
-    far = other_core(eight)
-    blocks = more(came, left, blocks, 4)
-    blocks, send = terms(order, turned, blocks, 0, 8, 8, far, left)
-    came = other_core(send)
+    came_eight, turned, blocks = lax.optimization_barrier((came_eight, turned, blocks))
+    blocks, leaving = terms(order, turned, blocks, 0, 8, 8, shared(came_eight), left)
+    others = to_core(1, leaving)
     blocks, next_four = terms(order, turned, blocks, 1, 4, 4)
-    leaving = (next_four + came[4:]).astype(jnp.bfloat16)
-    arrived = lax.ppermute(leaving, "ops", partners(2))
+    arrived = between_chips((leaving + others).astype(jnp.bfloat16), 2)
     _, last_four = terms(order, turned, blocks, 2, 0, 4)
-    keep = last_four + came[:4]
+    keep = jnp.concatenate([last_four, next_four], axis=0)
+    keep = keep + to_core(1, keep)
     for step in (1, 0):
         half = keep.shape[0] // 2
         both = keep + arrived.astype(jnp.float32)
-        keep, leaving = both[:half], both[half:].astype(jnp.bfloat16)
-        arrived = lax.ppermute(leaving, "ops", partners(step))
-    return keep + arrived.astype(jnp.float32)
+        keep = both[:half]
+        arrived = between_chips(both[half:].astype(jnp.bfloat16), step)
+    both = keep + arrived.astype(jnp.float32)
+    return jnp.where(first_core, to_core(0, both[:1]), both[1:])
 
 
 def shards_large(psi, left_ops, right_ops, couplings, live):

time: 38.4 us -> 61.2 us (1.59)
  waiting for transfers between devices: 10.1 us -> 34.9 us
  starting transfers between devices: 15.2 us -> 12.8 us
    ppermute x8 -> x13, waiting for transfers between devices: 10.1 us -> 34.9 us  [the longest x6 34.6 us: to_core(): return lax.ppermute(x, 'ops', [(i ^ 1, i) for i in range(core, OPS, 2)])]
    ppermute x8 -> x13, starting transfers between devices: 15.2 us -> 12.8 us  [the longest x6 8.35 us: to_core(): return lax.ppermute(x, 'ops', [(i ^ 1, i) for i in range(core, OPS, 2)])]
    select_n x0 -> x5, other arithmetic: none -> 0.7 us  [the longest x1 0.64 us: shards_small(): return jnp.where(first_core, to_core(0, both[:1]), both[1:])]
    add x1 -> x0, other arithmetic: 0.64 us -> none  [shards_small(): return keep + arrived.astype(jnp.float32)]
    unnamed x6 -> x7, local copies, waits for them, and re-layouts: 2.84 us -> 2.85 us
  transfers between devices with their start and end apart: 8 -> 13, of which waited for: 8 -> 6; matrix products, arithmetic and copies ran while one was open for 2% -> 1% of each run, Pallas kernels for 13% -> 9%
where the time goes in v1:
time: 61.2 us; the launch traced here: 61.4 us
  waiting for transfers between devices  34.9 us (57%)
  starting transfers between devices  12.8 us (21%)
  Pallas kernels  8.14 us (13%)
  local copies, waits for them, and re-layouts  3.61 us (6%)
  between operations  0.97 us (2%)
  other arithmetic  0.93 us (2%)
    ppermute x6, waiting for transfers between devices, to_core(): return lax.ppermute(x, 'ops', [(i ^ 1, i) for i in range(core, OPS, 2)])  34.6 us
    ppermute x6, starting transfers between devices, to_core(): return lax.ppermute(x, 'ops', [(i ^ 1, i) for i in range(core, OPS, 2)])  8.35 us
    pallas_call x3, Pallas kernels, terms(): pl.pallas_call(kernel, out_shape=[jax.ShapeDtypeStruct(blocks.shape, bloc...  5.91 us
    ppermute x6, starting transfers between devices, between_chips(): lax.ppermute(x, 'ops', [(i, i ^ 1 << CHAIN[step]) for i in range(1, OPS,...  4.02 us
    unnamed x7, local copies, waits for them, and re-layouts  2.85 us
  transfers between devices with their start and end apart: 13, of which 6 were waited for; matrix products, arithmetic and copies ran while one was open for 1% of the time, Pallas kernels for 9%

profile of v1, /device:TPU:0, one launch (start us, length us, event | category | flops | bytes accessed | tf_op | source)
XLA Modules:
  0.0 61.4 jit_solution(16944314307318510091)
XLA Ops:
  0.0 0.5 collective-permute-start
  0.5 0.8 %copy-done.2 = bf16[1,128,128]{2,1,0:T(8,128)(2,1)S(1)} copy-done((bf16[1,128,128]{2,1,0:T(8,128)(2,1)S(1)}, bf16[1,128,128]{2,1,0:T(8,128)(2,1)}, u32[]{:S(2)}) %copy-start.2) | copy-done | bytes 32792
  1.2 0.3 collective-permute-done
  1.6 0.7 %collective-permute-start.1 = (bf16[2,128,128]{2,1,0:T(8,128)(2,1)S(1)}, bf16[2,128,128]{2,1,0:T(8,128)(2,1)S(1)}, u32[]{:S(2)}, u32[]{:S(2)}) collective-permute-start(bf16[2,128,128]{2,1,0:T(8,128)(2,1)S(1)} %pad_maximum_fusion.4), channel_id=1, source_target_pairs={{1,9},{3,11},{5,13},{7,15},{9,1},{11,3},{13,5},{15,7},{17,25},{19,... | collective-permute-start | bytes 196616 | tf_op jit(solution)/shard_map/ppermute | solution.py:44
  2.2 1.3 %collective-permute-start.5 = (bf16[2,128,128]{2,1,0:T(8,128)(2,1)S(1)}, bf16[2,128,128]{2,1,0:T(8,128)(2,1)S(1)}, u32[]{:S(2)}, u32[]{:S(2)}) collective-permute-start(bf16[2,128,128]{2,1,0:T(8,128)(2,1)S(1)} %collective-permute-done.1), channel_id=1, source_target_pairs={{1,0},{3,2},{5,4},{7,6},{9,8},{11,10},{13,12},{15,14},{17,16},{19,... | collective-permute-start | bytes 196616 | tf_op jit(solution)/shard_map/ppermute | solution.py:48
  3.5 1.0 %copy-done = bf16[16,128,128]{2,1,0:T(8,128)(2,1)S(1)} copy-done((bf16[16,128,128]{2,1,0:T(8,128)(2,1)S(1)}, bf16[16,128,128]{2,1,0:T(8,128)(2,1)}, u32[]{:S(2)}) %copy-start) | copy-done | bytes 524312
  4.6 6.3 %collective-permute-done.5 = bf16[2,128,128]{2,1,0:T(8,128)(2,1)S(1)} collective-permute-done((bf16[2,128,128]{2,1,0:T(8,128)(2,1)S(1)}, bf16[2,128,128]{2,1,0:T(8,128)(2,1)S(1)}, u32[]{:S(2)}, u32[]{:S(2)}) %collective-permute-start.5) | collective-permute-done | bytes 65568 | tf_op jit(solution)/shard_map/ppermute | solution.py:48
  11.0 0.7 %collective-permute-start.2 = (bf16[4,128,128]{2,1,0:T(8,128)(2,1)S(1)}, bf16[4,128,128]{2,1,0:T(8,128)(2,1)S(1)}, u32[]{:S(2)}, u32[]{:S(2)}) collective-permute-start(bf16[4,128,128]{2,1,0:T(8,128)(2,1)S(1)} %get-tuple-element.17), channel_id=1, source_target_pairs={{1,5},{3,7},{5,1},{7,3},{9,13},{11,15},{13,9},{15,11},{17,21},{19,... | collective-permute-start | bytes 393224 | tf_op jit(solution)/shard_map/ppermute | solution.py:44
  12.3 1.0 %copy-done.1 = bf16[16,128,128]{2,1,0:T(8,128)(2,1)S(1)} copy-done((bf16[16,128,128]{2,1,0:T(8,128)(2,1)S(1)}, bf16[16,128,128]{2,1,0:T(8,128)(2,1)}, u32[]{:S(2)}) %copy-start.1) | copy-done | bytes 524312
  13.4 0.2 turn.1.turned_ref
  13.5 0.7 %concatenate.23.refs_0_ = s32[4,384]{1,0:T(4,128)S(1)} pad(s32[3,384]{1,0:T(4,128)} %param.8, s32[]{:T(128)} %bitcast.1), padding=0_1x0_0 | pad | bytes 10756 | tf_op jit(solution)/shard_map/concatenate | solution.py:107
  14.2 0.6 %order.1.order_in = s32[1,1024]{1,0:T(1,128)S(1)} custom-call(s32[4,384]{1,0:T(4,128)S(1)} %concatenate.23.refs_0_), custom_call_target="tpu_custom_call" | custom-call | flops 2949120 | bytes 1048576 | tf_op jit(solution)/shard_map/order/pallas_call | solution.py:108
  14.9 1.3 %collective-permute-start.4 = (bf16[4,128,128]{2,1,0:T(8,128)(2,1)S(1)}, bf16[4,128,128]{2,1,0:T(8,128)(2,1)S(1)}, u32[]{:S(2)}, u32[]{:S(2)}) collective-permute-start(bf16[4,128,128]{2,1,0:T(8,128)(2,1)S(1)} %collective-permute-done.2), channel_id=1, source_target_pairs={{1,0},{3,2},{5,4},{7,6},{9,8},{11,10},{13,12},{15,14},{17,16},{19,... | collective-permute-start | bytes 393224 | tf_op jit(solution)/shard_map/ppermute | solution.py:48
  16.2 0.7 %collective-permute-start.3 = (bf16[8,128,128]{2,1,0:T(8,128)(2,1)S(1)}, bf16[8,128,128]{2,1,0:T(8,128)(2,1)S(1)}, u32[]{:S(2)}, u32[]{:S(2)}) collective-permute-start(bf16[8,128,128]{2,1,0:T(8,128)(2,1)S(1)} %pad_maximum_fusion), channel_id=1, source_target_pairs={{1,3},{3,1},{5,7},{7,5},{9,11},{11,9},{13,15},{15,13},{17,19},{19,... | collective-permute-start | bytes 786440 | tf_op jit(solution)/shard_map/ppermute | solution.py:44
  16.9 0.7 %early.1._ = bf16[449,128,128]{2,1,0:T(8,128)(2,1)S(1)} custom-call(bf16[4,128,128]{2,1,0:T(8,128)(2,1)S(1)} %get-tuple-element.29.psi_ref, bf16[16,128,128]{2,1,0:T(8,128)(2,1)S(1)} %hold.3.left_ref.refs_1_), custom_call_target="tpu_custom_call" | custom-call | flops 268435456 | bytes 1048576 | tf_op jit(solution)/shard_map/early/pallas_call | solution.py:235
  17.6 2.5 %collective-permute-done.4 = bf16[4,128,128]{2,1,0:T(8,128)(2,1)S(1)} collective-permute-done((bf16[4,128,128]{2,1,0:T(8,128)(2,1)S(1)}, bf16[4,128,128]{2,1,0:T(8,128)(2,1)S(1)}, u32[]{:S(2)}, u32[]{:S(2)}) %collective-permute-start.4) | collective-permute-done | bytes 131104 | tf_op jit(solution)/shard_map/ppermute | solution.py:48
  20.1 0.7 %more.1.refs_2_ = bf16[449,128,128]{2,1,0:T(8,128)(2,1)S(1)} custom-call(bf16[4,128,128]{2,1,0:T(8,128)(2,1)S(1)} %broadcast_select_fusion.1.psi_ref, bf16[16,128,128]{2,1,0:T(8,128)(2,1)S(1)} %hold.3.left_ref.refs_1_, bf16[449,128,128]{2,1,0:T(8,128)(2,1)S(1)} %early.1._), custom_call_target="tpu_custom_call", output_to_operand_aliasing={{}: (2, {})} | custom-call | flops 268435456 | bytes 1048576 | tf_op jit(solution)/shard_map/more/pallas_call | solution.py:252
  20.8 1.3 %collective-permute-start.6 = (bf16[8,128,128]{2,1,0:T(8,128)(2,1)S(1)}, bf16[8,128,128]{2,1,0:T(8,128)(2,1)S(1)}, u32[]{:S(2)}, u32[]{:S(2)}) collective-permute-start(bf16[8,128,128]{2,1,0:T(8,128)(2,1)S(1)} %collective-permute-done.3), channel_id=1, source_target_pairs={{1,0},{3,2},{5,4},{7,6},{9,8},{11,10},{13,12},{15,14},{17,16},{19,... | collective-permute-start | bytes 786440 | tf_op jit(solution)/shard_map/ppermute | solution.py:48
  22.1 6.6 %collective-permute-done.6 = bf16[8,128,128]{2,1,0:T(8,128)(2,1)S(1)} collective-permute-done((bf16[8,128,128]{2,1,0:T(8,128)(2,1)S(1)}, bf16[8,128,128]{2,1,0:T(8,128)(2,1)S(1)}, u32[]{:S(2)}, u32[]{:S(2)}) %collective-permute-start.6) | collective-permute-done | bytes 262176 | tf_op jit(solution)/shard_map/ppermute | solution.py:48
  28.7 2.8 %terms_0.1 = (bf16[449,128,128]{2,1,0:T(8,128)(2,1)S(1)}, f32[8,128,128]{2,1,0:T(8,128)S(1)}) custom-call(s32[1,1024]{1,0:T(1,128)S(1)} %order.1.order_in, bf16[2048,128]{1,0:T(8,128)(2,1)S(1)} %turn.1.turned_ref, bf16[8,128,128]{2,1,0:T(8,128)(2,1)S(1)} %broadcast_select_fusion.refs_0_, ...), custom_call_target="tpu_custom_call", output_to_operand_aliasing={{0}: (4, {})} | custom-call | flops 1073741824 | bytes 1048576 | tf_op jit(solution)/shard_map/terms_0/pallas_call | solution.py:286
  31.5 1.9 %collective-permute-start.8 = (f32[8,128,128]{2,1,0:T(8,128)S(1)}, f32[8,128,128]{2,1,0:T(8,128)S(1)}, u32[]{:S(2)}, u32[]{:S(2)}) collective-permute-start(f32[8,128,128]{2,1,0:T(8,128)S(1)} %get-tuple-element.28), channel_id=1, source_target_pairs={{0,1},{2,3},{4,5},{6,7},{8,9},{10,11},{12,13},{14,15},{16,17},{18,... | collective-permute-start | bytes 1572872 | tf_op jit(solution)/shard_map/ppermute | solution.py:48
  33.4 1.5 %terms_1.1 = (bf16[449,128,128]{2,1,0:T(8,128)(2,1)S(1)}, f32[4,128,128]{2,1,0:T(8,128)S(1)}) custom-call(s32[1,1024]{1,0:T(1,128)S(1)} %order.1.order_in, bf16[2048,128]{1,0:T(8,128)(2,1)S(1)} %turn.1.turned_ref, bf16[449,128,128]{2,1,0:T(8,128)(2,1)S(1)} %get-tuple-element.24.refs_0_), custom_call_target="tpu_custom_call", output_to_operand_aliasing={{0}: (2, {})} | custom-call | flops 268435456 | bytes 1048576 | tf_op jit(solution)/shard_map/terms_1/pallas_call | solution.py:286
  35.0 1.6 %terms_2.1 = (bf16[449,128,128]{2,1,0:T(8,128)(2,1)S(1)}, f32[4,128,128]{2,1,0:T(8,128)S(1)}) custom-call(s32[1,1024]{1,0:T(1,128)S(1)} %order.1.order_in, bf16[2048,128]{1,0:T(8,128)(2,1)S(1)} %turn.1.turned_ref, bf16[449,128,128]{2,1,0:T(8,128)(2,1)S(1)} %get-tuple-element.25.refs_0_), custom_call_target="tpu_custom_call", output_to_operand_aliasing={{0}: (2, {})} | custom-call | flops 268435456 | bytes 1048576 | tf_op jit(solution)/shard_map/terms_2/pallas_call | solution.py:286
  36.6 1.3 %collective-permute-start.7 = (f32[8,128,128]{2,1,0:T(8,128)S(1)}, f32[8,128,128]{2,1,0:T(8,128)S(1)}, u32[]{:S(2)}, u32[]{:S(2)}) collective-permute-start(f32[8,128,128]{2,1,0:T(8,128)S(1)} %constant_dynamic-update-slice_fusion), channel_id=1, source_target_pairs={{0,1},{2,3},{4,5},{6,7},{8,9},{10,11},{12,13},{14,15},{16,17},{18,... | collective-permute-start | bytes 1572872 | tf_op jit(solution)/shard_map/ppermute | solution.py:48
  38.0 0.7 %collective-permute-start.9 = (bf16[8,128,128]{2,1,0:T(8,128)(2,1)S(1)}, bf16[8,128,128]{2,1,0:T(8,128)(2,1)S(1)}, u32[]{:S(2)}, u32[]{:S(2)}) collective-permute-start(bf16[8,128,128]{2,1,0:T(8,128)(2,1)S(1)} %add_convert_fusion), channel_id=1, source_target_pairs={{1,3},{3,1},{5,7},{7,5},{9,11},{11,9},{13,15},{15,13},{17,19},{19,... | collective-permute-start | bytes 786440 | tf_op jit(solution)/shard_map/ppermute | solution.py:44
  38.7 0.7 %collective-permute-done.7 = f32[8,128,128]{2,1,0:T(8,128)S(1)} collective-permute-done((f32[8,128,128]{2,1,0:T(8,128)S(1)}, f32[8,128,128]{2,1,0:T(8,128)S(1)}, u32[]{:S(2)}, u32[]{:S(2)}) %collective-permute-start.7) | collective-permute-done | bytes 524320 | tf_op jit(solution)/shard_map/ppermute | solution.py:48
  39.4 0.1 convert_add_fusion
  39.5 0.7 %collective-permute-start.10 = (bf16[4,128,128]{2,1,0:T(8,128)(2,1)S(1)}, bf16[4,128,128]{2,1,0:T(8,128)(2,1)S(1)}, u32[]{:S(2)}, u32[]{:S(2)}) collective-permute-start(bf16[4,128,128]{2,1,0:T(8,128)(2,1)S(1)} %slice.37), channel_id=1, source_target_pairs={{1,5},{3,7},{5,1},{7,3},{9,13},{11,15},{13,9},{15,11},{17,21},{19,... | collective-permute-start | bytes 393224 | tf_op jit(solution)/shard_map/ppermute | solution.py:44
  40.2 0.7 %collective-permute-start.11 = (bf16[2,128,128]{2,1,0:T(8,128)(2,1)S(1)}, bf16[2,128,128]{2,1,0:T(8,128)(2,1)S(1)}, u32[]{:S(2)}, u32[]{:S(2)}) collective-permute-start(bf16[2,128,128]{2,1,0:T(8,128)(2,1)S(1)} %slice.38), channel_id=1, source_target_pairs={{1,9},{3,11},{5,13},{7,15},{9,1},{11,3},{13,5},{15,7},{17,25},{19,... | collective-permute-start | bytes 196616 | tf_op jit(solution)/shard_map/ppermute | solution.py:44
  41.0 1.3 %collective-permute-start.12 = (f32[1,128,128]{2,1,0:T(8,128)S(1)}, f32[1,128,128]{2,1,0:T(8,128)S(1)}, u32[]{:S(2)}, u32[]{:S(2)}) collective-permute-start(f32[1,128,128]{2,1,0:T(8,128)S(1)} %slice.30), channel_id=1, source_target_pairs={{1,0},{3,2},{5,4},{7,6},{9,8},{11,10},{13,12},{15,14},{17,16},{19,... | collective-permute-start | bytes 196616 | tf_op jit(solution)/shard_map/ppermute | solution.py:48
  42.3 18.5 %collective-permute-done.12 = f32[1,128,128]{2,1,0:T(8,128)S(1)} collective-permute-done((f32[1,128,128]{2,1,0:T(8,128)S(1)}, f32[1,128,128]{2,1,0:T(8,128)S(1)}, u32[]{:S(2)}, u32[]{:S(2)}) %collective-permute-start.12) | collective-permute-done | bytes 65568 | tf_op jit(solution)/shard_map/ppermute | solution.py:48
  60.7 0.6 %slice_select_fusion = f32[1,128,128]{2,1,0:T(8,128)} fusion(f32[1,128,128]{2,1,0:T(8,128)S(1)} %collective-permute-done.12, f32[2,128,128]{2,1,0:T(8,128)S(1)} %slice_add_fusion.1, pred[]{:T(512)S(6)} %eq.3), kind=kLoop, calls=%fused_computation.12 | loop fusion | flops 16384 | bytes 196609 | tf_op jit(solution)/shard_map/jit(_where)/select_n | solution.py:359
  (27 shorter events, 0.4 us)
Async XLA Ops:
  0.0 1.5 %collective-permute-start = (bf16[1,128,128]{2,1,0:T(8,128)(2,1)}, bf16[1,128,128]{2,1,0:T(8,128)(2,1)S(1)}, u32[]{:S(2)}, u32[]{:S(2)}) collective-permute-start(bf16[1,128,128]{2,1,0:T(8,128)(2,1)} %in_ref.2), channel_id=1, source_target_pairs={{0,1},{1,0},{2,3},{3,2},{4,5},{5,4},{6,7},{7,6},{8,9},{9,8},{10,11... | collective-permute-start | bytes 98312 | tf_op jit(solution)/shard_map/ppermute | solution.py:330
  0.5 0.8 %copy-start.2 = (bf16[1,128,128]{2,1,0:T(8,128)(2,1)S(1)}, bf16[1,128,128]{2,1,0:T(8,128)(2,1)}, u32[]{:S(2)}) copy-start(bf16[1,128,128]{2,1,0:T(8,128)(2,1)} %in_ref.2) | copy-start | bytes 98308
  1.6 0.7 %collective-permute-start.1 = (bf16[2,128,128]{2,1,0:T(8,128)(2,1)S(1)}, bf16[2,128,128]{2,1,0:T(8,128)(2,1)S(1)}, u32[]{:S(2)}, u32[]{:S(2)}) collective-permute-start(bf16[2,128,128]{2,1,0:T(8,128)(2,1)S(1)} %pad_maximum_fusion.4), channel_id=1, source_target_pairs={{1,9},{3,11},{5,13},{7,15},{9,1},{11,3},{13,5},{15,7},{17,25},{19,... | collective-permute-start | bytes 196616 | tf_op jit(solution)/shard_map/ppermute | solution.py:44
  2.2 8.7 %collective-permute-start.5 = (bf16[2,128,128]{2,1,0:T(8,128)(2,1)S(1)}, bf16[2,128,128]{2,1,0:T(8,128)(2,1)S(1)}, u32[]{:S(2)}, u32[]{:S(2)}) collective-permute-start(bf16[2,128,128]{2,1,0:T(8,128)(2,1)S(1)} %collective-permute-done.1), channel_id=1, source_target_pairs={{1,0},{3,2},{5,4},{7,6},{9,8},{11,10},{13,12},{15,14},{17,16},{19,... | collective-permute-start | bytes 196616 | tf_op jit(solution)/shard_map/ppermute | solution.py:48
  3.5 1.0 %copy-start = (bf16[16,128,128]{2,1,0:T(8,128)(2,1)S(1)}, bf16[16,128,128]{2,1,0:T(8,128)(2,1)}, u32[]{:S(2)}) copy-start(bf16[16,128,128]{2,1,0:T(8,128)(2,1)} %in_ref.3) | copy-start | bytes 1572868
  11.0 3.9 %collective-permute-start.2 = (bf16[4,128,128]{2,1,0:T(8,128)(2,1)S(1)}, bf16[4,128,128]{2,1,0:T(8,128)(2,1)S(1)}, u32[]{:S(2)}, u32[]{:S(2)}) collective-permute-start(bf16[4,128,128]{2,1,0:T(8,128)(2,1)S(1)} %get-tuple-element.17), channel_id=1, source_target_pairs={{1,5},{3,7},{5,1},{7,3},{9,13},{11,15},{13,9},{15,11},{17,21},{19,... | collective-permute-start | bytes 393224 | tf_op jit(solution)/shard_map/ppermute | solution.py:44
  12.3 1.0 %copy-start.1 = (bf16[16,128,128]{2,1,0:T(8,128)(2,1)S(1)}, bf16[16,128,128]{2,1,0:T(8,128)(2,1)}, u32[]{:S(2)}) copy-start(bf16[16,128,128]{2,1,0:T(8,128)(2,1)} %right_ref.1) | copy-start | bytes 1572868
  14.9 5.2 %collective-permute-start.4 = (bf16[4,128,128]{2,1,0:T(8,128)(2,1)S(1)}, bf16[4,128,128]{2,1,0:T(8,128)(2,1)S(1)}, u32[]{:S(2)}, u32[]{:S(2)}) collective-permute-start(bf16[4,128,128]{2,1,0:T(8,128)(2,1)S(1)} %collective-permute-done.2), channel_id=1, source_target_pairs={{1,0},{3,2},{5,4},{7,6},{9,8},{11,10},{13,12},{15,14},{17,16},{19,... | collective-permute-start | bytes 393224 | tf_op jit(solution)/shard_map/ppermute | solution.py:48
  16.2 4.5 %collective-permute-start.3 = (bf16[8,128,128]{2,1,0:T(8,128)(2,1)S(1)}, bf16[8,128,128]{2,1,0:T(8,128)(2,1)S(1)}, u32[]{:S(2)}, u32[]{:S(2)}) collective-permute-start(bf16[8,128,128]{2,1,0:T(8,128)(2,1)S(1)} %pad_maximum_fusion), channel_id=1, source_target_pairs={{1,3},{3,1},{5,7},{7,5},{9,11},{11,9},{13,15},{15,13},{17,19},{19,... | collective-permute-start | bytes 786440 | tf_op jit(solution)/shard_map/ppermute | solution.py:44
  20.8 7.9 %collective-permute-start.6 = (bf16[8,128,128]{2,1,0:T(8,128)(2,1)S(1)}, bf16[8,128,128]{2,1,0:T(8,128)(2,1)S(1)}, u32[]{:S(2)}, u32[]{:S(2)}) collective-permute-start(bf16[8,128,128]{2,1,0:T(8,128)(2,1)S(1)} %collective-permute-done.3), channel_id=1, source_target_pairs={{1,0},{3,2},{5,4},{7,6},{9,8},{11,10},{13,12},{15,14},{17,16},{19,... | collective-permute-start | bytes 786440 | tf_op jit(solution)/shard_map/ppermute | solution.py:48
  31.5 6.4 %collective-permute-start.8 = (f32[8,128,128]{2,1,0:T(8,128)S(1)}, f32[8,128,128]{2,1,0:T(8,128)S(1)}, u32[]{:S(2)}, u32[]{:S(2)}) collective-permute-start(f32[8,128,128]{2,1,0:T(8,128)S(1)} %get-tuple-element.28), channel_id=1, source_target_pairs={{0,1},{2,3},{4,5},{6,7},{8,9},{10,11},{12,13},{14,15},{16,17},{18,... | collective-permute-start | bytes 1572872 | tf_op jit(solution)/shard_map/ppermute | solution.py:48
  36.6 2.8 %collective-permute-start.7 = (f32[8,128,128]{2,1,0:T(8,128)S(1)}, f32[8,128,128]{2,1,0:T(8,128)S(1)}, u32[]{:S(2)}, u32[]{:S(2)}) collective-permute-start(f32[8,128,128]{2,1,0:T(8,128)S(1)} %constant_dynamic-update-slice_fusion), channel_id=1, source_target_pairs={{0,1},{2,3},{4,5},{6,7},{8,9},{10,11},{12,13},{14,15},{16,17},{18,... | collective-permute-start | bytes 1572872 | tf_op jit(solution)/shard_map/ppermute | solution.py:48
  38.0 1.4 %collective-permute-start.9 = (bf16[8,128,128]{2,1,0:T(8,128)(2,1)S(1)}, bf16[8,128,128]{2,1,0:T(8,128)(2,1)S(1)}, u32[]{:S(2)}, u32[]{:S(2)}) collective-permute-start(bf16[8,128,128]{2,1,0:T(8,128)(2,1)S(1)} %add_convert_fusion), channel_id=1, source_target_pairs={{1,3},{3,1},{5,7},{7,5},{9,11},{11,9},{13,15},{15,13},{17,19},{19,... | collective-permute-start | bytes 786440 | tf_op jit(solution)/shard_map/ppermute | solution.py:44
  39.5 0.7 %collective-permute-start.10 = (bf16[4,128,128]{2,1,0:T(8,128)(2,1)S(1)}, bf16[4,128,128]{2,1,0:T(8,128)(2,1)S(1)}, u32[]{:S(2)}, u32[]{:S(2)}) collective-permute-start(bf16[4,128,128]{2,1,0:T(8,128)(2,1)S(1)} %slice.37), channel_id=1, source_target_pairs={{1,5},{3,7},{5,1},{7,3},{9,13},{11,15},{13,9},{15,11},{17,21},{19,... | collective-permute-start | bytes 393224 | tf_op jit(solution)/shard_map/ppermute | solution.py:44
  40.2 0.7 %collective-permute-start.11 = (bf16[2,128,128]{2,1,0:T(8,128)(2,1)S(1)}, bf16[2,128,128]{2,1,0:T(8,128)(2,1)S(1)}, u32[]{:S(2)}, u32[]{:S(2)}) collective-permute-start(bf16[2,128,128]{2,1,0:T(8,128)(2,1)S(1)} %slice.38), channel_id=1, source_target_pairs={{1,9},{3,11},{5,13},{7,15},{9,1},{11,3},{13,5},{15,7},{17,25},{19,... | collective-permute-start | bytes 196616 | tf_op jit(solution)/shard_map/ppermute | solution.py:44
  41.0 19.8 %collective-permute-start.12 = (f32[1,128,128]{2,1,0:T(8,128)S(1)}, f32[1,128,128]{2,1,0:T(8,128)S(1)}, u32[]{:S(2)}, u32[]{:S(2)}) collective-permute-start(f32[1,128,128]{2,1,0:T(8,128)S(1)} %slice.30), channel_id=1, source_target_pairs={{1,0},{3,2},{5,4},{7,6},{9,8},{11,10},{13,12},{15,14},{17,16},{19,... | collective-permute-start | bytes 196616 | tf_op jit(solution)/shard_map/ppermute | solution.py:48

commit v2 on v1

--- a/solution.py
+++ b/solution.py
@@ -41,11 +41,11 @@
 
 
 def between_chips(x, step):
-    return lax.ppermute(x, "ops", [(i, i ^ (1 << CHAIN[step])) for i in range(1, OPS, 2)])
-
-
-def to_core(core, x):
-    return lax.ppermute(x, "ops", [(i ^ 1, i) for i in range(core, OPS, 2)])
+    return lax.ppermute(x, "ops", [(i, i ^ ((i & 1) << CHAIN[step])) for i in range(OPS)])
+
+
+def other_core(x):
+    return lax.ppermute(x, "ops", [(i, i ^ 1) for i in range(OPS)])
 
 
 def place(sector, me):
@@ -325,9 +325,9 @@
     first_core = lax.axis_index("ops") & 1 == 0
 
     def shared(x):
-        return jnp.where(first_core, to_core(0, x), x)
-
-    came = lax.ppermute(psi, "ops", [(i, i ^ 1) for i in range(OPS)])
+        return jnp.where(first_core, other_core(x), x)
+
+    came = other_core(psi)
     psi = hold(psi)
     two = jnp.concatenate(
         [jnp.where(first_core, psi, came), jnp.where(first_core, came, psi)], axis=0
@@ -344,19 +344,19 @@
     turned = turn(right_ops)
     came_eight, turned, blocks = lax.optimization_barrier((came_eight, turned, blocks))
     blocks, leaving = terms(order, turned, blocks, 0, 8, 8, shared(came_eight), left)
-    others = to_core(1, leaving)
+    others = other_core(leaving)
     blocks, next_four = terms(order, turned, blocks, 1, 4, 4)
     arrived = between_chips((leaving + others).astype(jnp.bfloat16), 2)
     _, last_four = terms(order, turned, blocks, 2, 0, 4)
     keep = jnp.concatenate([last_four, next_four], axis=0)
-    keep = keep + to_core(1, keep)
+    keep = keep + other_core(keep)
     for step in (1, 0):
         half = keep.shape[0] // 2
         both = keep + arrived.astype(jnp.float32)
         keep = both[:half]
         arrived = between_chips(both[half:].astype(jnp.bfloat16), step)
     both = keep + arrived.astype(jnp.float32)
-    return jnp.where(first_core, to_core(0, both[:1]), both[1:])
+    return jnp.where(first_core, other_core(both[:1]), both[1:])
 
 
 def shards_large(psi, left_ops, right_ops, couplings, live):

time: 61.2 us -> 54.7 us (0.89); the launches traced: 61.4 us -> 53.9 us
  waiting for transfers between devices: 34.9 us -> 3.18 us
  starting transfers between devices: 12.8 us -> 37.9 us
  Pallas kernels: 8.14 us -> 7.43 us
    ppermute x13, waiting for transfers between devices: 34.9 us -> 3.18 us  [the longest x7 3.17 us: other_core(): return lax.ppermute(x, 'ops', [(i, i ^ 1) for i in range(OPS)])]
    ppermute x13, starting transfers between devices: 12.8 us -> 37.9 us  [the longest x7 33.8 us: other_core(): return lax.ppermute(x, 'ops', [(i, i ^ 1) for i in range(OPS)])]
    pallas_call x3, Pallas kernels: 5.91 us -> 5.2 us  [terms(): pl.pallas_call(kernel, out_shape=[jax.ShapeDtypeStruct(blocks.shape, bloc...]
  transfers between devices with their start and end apart: 13 -> 13, of which waited for: 6 -> 4; matrix products, arithmetic and copies ran while one was open for 1% -> 2% of each run, Pallas kernels for 9% -> 9%
where the time goes in v2:
time: 54.7 us; the launch traced here: 53.9 us
  starting transfers between devices  37.9 us (69%)
  Pallas kernels  7.43 us (14%)
  local copies, waits for them, and re-layouts  3.61 us (7%)
  waiting for transfers between devices  3.18 us (6%)
  other arithmetic  0.93 us (2%)
  between operations  0.92 us (2%)
    ppermute x7, starting transfers between devices, other_core(): return lax.ppermute(x, 'ops', [(i, i ^ 1) for i in range(OPS)])  33.8 us
    pallas_call x3, Pallas kernels, terms(): pl.pallas_call(kernel, out_shape=[jax.ShapeDtypeStruct(blocks.shape, bloc...  5.2 us
    ppermute x6, starting transfers between devices, between_chips(): lax.ppermute(x, 'ops', [(i, i ^ (i & 1) << CHAIN[step]) for i in range(OP...  4.02 us
    ppermute x7, waiting for transfers between devices, other_core(): return lax.ppermute(x, 'ops', [(i, i ^ 1) for i in range(OPS)])  3.17 us
    unnamed x7, local copies, waits for them, and re-layouts  2.85 us
  transfers between devices with their start and end apart: 13, of which 4 were waited for; matrix products, arithmetic and copies ran while one was open for 2% of the time, Pallas kernels for 9%

profile of v2, /device:TPU:0, one launch (start us, length us, event | category | flops | bytes accessed | tf_op | source)
XLA Modules:
  0.0 53.9 jit_solution(3902798116058722882)
XLA Ops:
  0.0 0.5 collective-permute-start
  0.5 0.8 %copy-done.2 = bf16[1,128,128]{2,1,0:T(8,128)(2,1)S(1)} copy-done((bf16[1,128,128]{2,1,0:T(8,128)(2,1)S(1)}, bf16[1,128,128]{2,1,0:T(8,128)(2,1)}, u32[]{:S(2)}) %copy-start.2) | copy-done | bytes 32792
  1.2 0.3 collective-permute-done
  1.6 0.7 %collective-permute-start.1 = (bf16[2,128,128]{2,1,0:T(8,128)(2,1)S(1)}, bf16[2,128,128]{2,1,0:T(8,128)(2,1)S(1)}, u32[]{:S(2)}, u32[]{:S(2)}) collective-permute-start(bf16[2,128,128]{2,1,0:T(8,128)(2,1)S(1)} %pad_maximum_fusion.4), channel_id=1, source_target_pairs={{0,0},{1,9},{2,2},{3,11},{4,4},{5,13},{6,6},{7,15},{8,8},{9,1},{10... | collective-permute-start | bytes 196616 | tf_op jit(solution)/shard_map/ppermute | solution.py:44
  2.2 6.7 %collective-permute-start.5 = (bf16[2,128,128]{2,1,0:T(8,128)(2,1)S(1)}, bf16[2,128,128]{2,1,0:T(8,128)(2,1)S(1)}, u32[]{:S(2)}, u32[]{:S(2)}) collective-permute-start(bf16[2,128,128]{2,1,0:T(8,128)(2,1)S(1)} %collective-permute-done.1), channel_id=1, source_target_pairs={{0,1},{1,0},{2,3},{3,2},{4,5},{5,4},{6,7},{7,6},{8,9},{9,8},{10,11... | collective-permute-start | bytes 196616 | tf_op jit(solution)/shard_map/ppermute | solution.py:48
  8.9 1.0 %copy-done = bf16[16,128,128]{2,1,0:T(8,128)(2,1)S(1)} copy-done((bf16[16,128,128]{2,1,0:T(8,128)(2,1)S(1)}, bf16[16,128,128]{2,1,0:T(8,128)(2,1)}, u32[]{:S(2)}) %copy-start) | copy-done | bytes 524312
  10.1 0.7 %collective-permute-start.2 = (bf16[4,128,128]{2,1,0:T(8,128)(2,1)S(1)}, bf16[4,128,128]{2,1,0:T(8,128)(2,1)S(1)}, u32[]{:S(2)}, u32[]{:S(2)}) collective-permute-start(bf16[4,128,128]{2,1,0:T(8,128)(2,1)S(1)} %get-tuple-element.17), channel_id=1, source_target_pairs={{0,0},{1,5},{2,2},{3,7},{4,4},{5,1},{6,6},{7,3},{8,8},{9,13},{10,1... | collective-permute-start | bytes 393224 | tf_op jit(solution)/shard_map/ppermute | solution.py:44
  11.4 0.0 copy-start.1
  11.4 1.0 %copy-done.1 = bf16[16,128,128]{2,1,0:T(8,128)(2,1)S(1)} copy-done((bf16[16,128,128]{2,1,0:T(8,128)(2,1)S(1)}, bf16[16,128,128]{2,1,0:T(8,128)(2,1)}, u32[]{:S(2)}) %copy-start.1) | copy-done | bytes 524312
  12.4 0.2 turn.1.turned_ref
  12.6 0.7 %concatenate.23.refs_0_ = s32[4,384]{1,0:T(4,128)S(1)} pad(s32[3,384]{1,0:T(4,128)} %param.8, s32[]{:T(128)} %bitcast.1), padding=0_1x0_0 | pad | bytes 10756 | tf_op jit(solution)/shard_map/concatenate | solution.py:107
  13.3 0.6 %order.1.order_in = s32[1,1024]{1,0:T(1,128)S(1)} custom-call(s32[4,384]{1,0:T(4,128)S(1)} %concatenate.23.refs_0_), custom_call_target="tpu_custom_call" | custom-call | flops 2949120 | bytes 1048576 | tf_op jit(solution)/shard_map/order/pallas_call | solution.py:108
  14.0 2.9 %collective-permute-start.4 = (bf16[4,128,128]{2,1,0:T(8,128)(2,1)S(1)}, bf16[4,128,128]{2,1,0:T(8,128)(2,1)S(1)}, u32[]{:S(2)}, u32[]{:S(2)}) collective-permute-start(bf16[4,128,128]{2,1,0:T(8,128)(2,1)S(1)} %collective-permute-done.2), channel_id=1, source_target_pairs={{0,1},{1,0},{2,3},{3,2},{4,5},{5,4},{6,7},{7,6},{8,9},{9,8},{10,11... | collective-permute-start | bytes 393224 | tf_op jit(solution)/shard_map/ppermute | solution.py:48
  16.9 0.7 %collective-permute-start.3 = (bf16[8,128,128]{2,1,0:T(8,128)(2,1)S(1)}, bf16[8,128,128]{2,1,0:T(8,128)(2,1)S(1)}, u32[]{:S(2)}, u32[]{:S(2)}) collective-permute-start(bf16[8,128,128]{2,1,0:T(8,128)(2,1)S(1)} %pad_maximum_fusion), channel_id=1, source_target_pairs={{0,0},{1,3},{2,2},{3,1},{4,4},{5,7},{6,6},{7,5},{8,8},{9,11},{10,1... | collective-permute-start | bytes 786440 | tf_op jit(solution)/shard_map/ppermute | solution.py:44
  17.6 0.7 %early.1._ = bf16[449,128,128]{2,1,0:T(8,128)(2,1)S(1)} custom-call(bf16[4,128,128]{2,1,0:T(8,128)(2,1)S(1)} %get-tuple-element.29.psi_ref, bf16[16,128,128]{2,1,0:T(8,128)(2,1)S(1)} %hold.3.left_ref.refs_1_), custom_call_target="tpu_custom_call" | custom-call | flops 268435456 | bytes 1048576 | tf_op jit(solution)/shard_map/early/pallas_call | solution.py:235
  18.3 0.7 %more.1.refs_2_ = bf16[449,128,128]{2,1,0:T(8,128)(2,1)S(1)} custom-call(bf16[4,128,128]{2,1,0:T(8,128)(2,1)S(1)} %broadcast_select_fusion.1.psi_ref, bf16[16,128,128]{2,1,0:T(8,128)(2,1)S(1)} %hold.3.left_ref.refs_1_, bf16[449,128,128]{2,1,0:T(8,128)(2,1)S(1)} %early.1._), custom_call_target="tpu_custom_call", output_to_operand_aliasing={{}: (2, {})} | custom-call | flops 268435456 | bytes 1048576 | tf_op jit(solution)/shard_map/more/pallas_call | solution.py:252
  19.0 5.0 %collective-permute-start.6 = (bf16[8,128,128]{2,1,0:T(8,128)(2,1)S(1)}, bf16[8,128,128]{2,1,0:T(8,128)(2,1)S(1)}, u32[]{:S(2)}, u32[]{:S(2)}) collective-permute-start(bf16[8,128,128]{2,1,0:T(8,128)(2,1)S(1)} %collective-permute-done.3), channel_id=1, source_target_pairs={{0,1},{1,0},{2,3},{3,2},{4,5},{5,4},{6,7},{7,6},{8,9},{9,8},{10,11... | collective-permute-start | bytes 786440 | tf_op jit(solution)/shard_map/ppermute | solution.py:48
  24.0 1.2 %collective-permute-done.6 = bf16[8,128,128]{2,1,0:T(8,128)(2,1)S(1)} collective-permute-done((bf16[8,128,128]{2,1,0:T(8,128)(2,1)S(1)}, bf16[8,128,128]{2,1,0:T(8,128)(2,1)S(1)}, u32[]{:S(2)}, u32[]{:S(2)}) %collective-permute-start.6) | collective-permute-done | bytes 262176 | tf_op jit(solution)/shard_map/ppermute | solution.py:48
  25.2 2.5 %terms_0.1 = (bf16[449,128,128]{2,1,0:T(8,128)(2,1)S(1)}, f32[8,128,128]{2,1,0:T(8,128)S(1)}) custom-call(s32[1,1024]{1,0:T(1,128)S(1)} %order.1.order_in, bf16[2048,128]{1,0:T(8,128)(2,1)S(1)} %turn.1.turned_ref, bf16[8,128,128]{2,1,0:T(8,128)(2,1)S(1)} %broadcast_select_fusion.refs_0_, ...), custom_call_target="tpu_custom_call", output_to_operand_aliasing={{0}: (4, {})} | custom-call | flops 1073741824 | bytes 1048576 | tf_op jit(solution)/shard_map/terms_0/pallas_call | solution.py:286
  27.8 1.3 %collective-permute-start.8 = (f32[8,128,128]{2,1,0:T(8,128)S(1)}, f32[8,128,128]{2,1,0:T(8,128)S(1)}, u32[]{:S(2)}, u32[]{:S(2)}) collective-permute-start(f32[8,128,128]{2,1,0:T(8,128)S(1)} %get-tuple-element.28), channel_id=1, source_target_pairs={{0,1},{1,0},{2,3},{3,2},{4,5},{5,4},{6,7},{7,6},{8,9},{9,8},{10,11... | collective-permute-start | bytes 1572872 | tf_op jit(solution)/shard_map/ppermute | solution.py:48
  29.1 1.3 %terms_1.1 = (bf16[449,128,128]{2,1,0:T(8,128)(2,1)S(1)}, f32[4,128,128]{2,1,0:T(8,128)S(1)}) custom-call(s32[1,1024]{1,0:T(1,128)S(1)} %order.1.order_in, bf16[2048,128]{1,0:T(8,128)(2,1)S(1)} %turn.1.turned_ref, bf16[449,128,128]{2,1,0:T(8,128)(2,1)S(1)} %get-tuple-element.24.refs_0_), custom_call_target="tpu_custom_call", output_to_operand_aliasing={{0}: (2, {})} | custom-call | flops 268435456 | bytes 1048576 | tf_op jit(solution)/shard_map/terms_1/pallas_call | solution.py:286
  30.5 1.3 %terms_2.1 = (bf16[449,128,128]{2,1,0:T(8,128)(2,1)S(1)}, f32[4,128,128]{2,1,0:T(8,128)S(1)}) custom-call(s32[1,1024]{1,0:T(1,128)S(1)} %order.1.order_in, bf16[2048,128]{1,0:T(8,128)(2,1)S(1)} %turn.1.turned_ref, bf16[449,128,128]{2,1,0:T(8,128)(2,1)S(1)} %get-tuple-element.25.refs_0_), custom_call_target="tpu_custom_call", output_to_operand_aliasing={{0}: (2, {})} | custom-call | flops 268435456 | bytes 1048576 | tf_op jit(solution)/shard_map/terms_2/pallas_call | solution.py:286
  31.9 1.0 %collective-permute-start.7 = (f32[8,128,128]{2,1,0:T(8,128)S(1)}, f32[8,128,128]{2,1,0:T(8,128)S(1)}, u32[]{:S(2)}, u32[]{:S(2)}) collective-permute-start(f32[8,128,128]{2,1,0:T(8,128)S(1)} %constant_dynamic-update-slice_fusion), channel_id=1, source_target_pairs={{0,1},{1,0},{2,3},{3,2},{4,5},{5,4},{6,7},{7,6},{8,9},{9,8},{10,11... | collective-permute-start | bytes 1572872 | tf_op jit(solution)/shard_map/ppermute | solution.py:48
  32.8 0.1 add_convert_fusion
  32.9 0.7 %collective-permute-start.9 = (bf16[8,128,128]{2,1,0:T(8,128)(2,1)S(1)}, bf16[8,128,128]{2,1,0:T(8,128)(2,1)S(1)}, u32[]{:S(2)}, u32[]{:S(2)}) collective-permute-start(bf16[8,128,128]{2,1,0:T(8,128)(2,1)S(1)} %add_convert_fusion), channel_id=1, source_target_pairs={{0,0},{1,3},{2,2},{3,1},{4,4},{5,7},{6,6},{7,5},{8,8},{9,11},{10,1... | collective-permute-start | bytes 786440 | tf_op jit(solution)/shard_map/ppermute | solution.py:44
  33.6 0.8 %collective-permute-done.7 = f32[8,128,128]{2,1,0:T(8,128)S(1)} collective-permute-done((f32[8,128,128]{2,1,0:T(8,128)S(1)}, f32[8,128,128]{2,1,0:T(8,128)S(1)}, u32[]{:S(2)}, u32[]{:S(2)}) %collective-permute-start.7) | collective-permute-done | bytes 524320 | tf_op jit(solution)/shard_map/ppermute | solution.py:48
  34.4 0.1 convert_add_fusion
  34.5 0.7 %collective-permute-start.10 = (bf16[4,128,128]{2,1,0:T(8,128)(2,1)S(1)}, bf16[4,128,128]{2,1,0:T(8,128)(2,1)S(1)}, u32[]{:S(2)}, u32[]{:S(2)}) collective-permute-start(bf16[4,128,128]{2,1,0:T(8,128)(2,1)S(1)} %slice.37), channel_id=1, source_target_pairs={{0,0},{1,5},{2,2},{3,7},{4,4},{5,1},{6,6},{7,3},{8,8},{9,13},{10,1... | collective-permute-start | bytes 393224 | tf_op jit(solution)/shard_map/ppermute | solution.py:44
  35.2 0.7 %collective-permute-start.11 = (bf16[2,128,128]{2,1,0:T(8,128)(2,1)S(1)}, bf16[2,128,128]{2,1,0:T(8,128)(2,1)S(1)}, u32[]{:S(2)}, u32[]{:S(2)}) collective-permute-start(bf16[2,128,128]{2,1,0:T(8,128)(2,1)S(1)} %slice.38), channel_id=1, source_target_pairs={{0,0},{1,9},{2,2},{3,11},{4,4},{5,13},{6,6},{7,15},{8,8},{9,1},{10... | collective-permute-start | bytes 196616 | tf_op jit(solution)/shard_map/ppermute | solution.py:44
  35.9 16.5 %collective-permute-start.12 = (f32[1,128,128]{2,1,0:T(8,128)S(1)}, f32[1,128,128]{2,1,0:T(8,128)S(1)}, u32[]{:S(2)}, u32[]{:S(2)}) collective-permute-start(f32[1,128,128]{2,1,0:T(8,128)S(1)} %slice.30), channel_id=1, source_target_pairs={{0,1},{1,0},{2,3},{3,2},{4,5},{5,4},{6,7},{7,6},{8,9},{9,8},{10,11... | collective-permute-start | bytes 196616 | tf_op jit(solution)/shard_map/ppermute | solution.py:48
  52.4 0.9 %collective-permute-done.12 = f32[1,128,128]{2,1,0:T(8,128)S(1)} collective-permute-done((f32[1,128,128]{2,1,0:T(8,128)S(1)}, f32[1,128,128]{2,1,0:T(8,128)S(1)}, u32[]{:S(2)}, u32[]{:S(2)}) %collective-permute-start.12) | collective-permute-done | bytes 65568 | tf_op jit(solution)/shard_map/ppermute | solution.py:48
  53.3 0.6 %slice_select_fusion = f32[1,128,128]{2,1,0:T(8,128)} fusion(f32[1,128,128]{2,1,0:T(8,128)S(1)} %collective-permute-done.12, f32[2,128,128]{2,1,0:T(8,128)S(1)} %slice_add_fusion.1, pred[]{:T(512)S(6)} %eq.3), kind=kLoop, calls=%fused_computation.12 | loop fusion | flops 16384 | bytes 196609 | tf_op jit(solution)/shard_map/jit(_where)/select_n | solution.py:359
  (27 shorter events, 0.3 us)
Async XLA Ops:
  0.0 1.5 %collective-permute-start = (bf16[1,128,128]{2,1,0:T(8,128)(2,1)}, bf16[1,128,128]{2,1,0:T(8,128)(2,1)S(1)}, u32[]{:S(2)}, u32[]{:S(2)}) collective-permute-start(bf16[1,128,128]{2,1,0:T(8,128)(2,1)} %in_ref.2), channel_id=1, source_target_pairs={{0,1},{1,0},{2,3},{3,2},{4,5},{5,4},{6,7},{7,6},{8,9},{9,8},{10,11... | collective-permute-start | bytes 98312 | tf_op jit(solution)/shard_map/ppermute | solution.py:48
  0.5 0.8 %copy-start.2 = (bf16[1,128,128]{2,1,0:T(8,128)(2,1)S(1)}, bf16[1,128,128]{2,1,0:T(8,128)(2,1)}, u32[]{:S(2)}) copy-start(bf16[1,128,128]{2,1,0:T(8,128)(2,1)} %in_ref.2) | copy-start | bytes 98308
  1.6 0.7 %collective-permute-start.1 = (bf16[2,128,128]{2,1,0:T(8,128)(2,1)S(1)}, bf16[2,128,128]{2,1,0:T(8,128)(2,1)S(1)}, u32[]{:S(2)}, u32[]{:S(2)}) collective-permute-start(bf16[2,128,128]{2,1,0:T(8,128)(2,1)S(1)} %pad_maximum_fusion.4), channel_id=1, source_target_pairs={{0,0},{1,9},{2,2},{3,11},{4,4},{5,13},{6,6},{7,15},{8,8},{9,1},{10... | collective-permute-start | bytes 196616 | tf_op jit(solution)/shard_map/ppermute | solution.py:44
  2.2 7.8 %collective-permute-start.5 = (bf16[2,128,128]{2,1,0:T(8,128)(2,1)S(1)}, bf16[2,128,128]{2,1,0:T(8,128)(2,1)S(1)}, u32[]{:S(2)}, u32[]{:S(2)}) collective-permute-start(bf16[2,128,128]{2,1,0:T(8,128)(2,1)S(1)} %collective-permute-done.1), channel_id=1, source_target_pairs={{0,1},{1,0},{2,3},{3,2},{4,5},{5,4},{6,7},{7,6},{8,9},{9,8},{10,11... | collective-permute-start | bytes 196616 | tf_op jit(solution)/shard_map/ppermute | solution.py:48
  8.9 1.0 %copy-start = (bf16[16,128,128]{2,1,0:T(8,128)(2,1)S(1)}, bf16[16,128,128]{2,1,0:T(8,128)(2,1)}, u32[]{:S(2)}) copy-start(bf16[16,128,128]{2,1,0:T(8,128)(2,1)} %in_ref.3) | copy-start | bytes 1572868
  10.1 3.9 %collective-permute-start.2 = (bf16[4,128,128]{2,1,0:T(8,128)(2,1)S(1)}, bf16[4,128,128]{2,1,0:T(8,128)(2,1)S(1)}, u32[]{:S(2)}, u32[]{:S(2)}) collective-permute-start(bf16[4,128,128]{2,1,0:T(8,128)(2,1)S(1)} %get-tuple-element.17), channel_id=1, source_target_pairs={{0,0},{1,5},{2,2},{3,7},{4,4},{5,1},{6,6},{7,3},{8,8},{9,13},{10,1... | collective-permute-start | bytes 393224 | tf_op jit(solution)/shard_map/ppermute | solution.py:44
  11.4 1.0 %copy-start.1 = (bf16[16,128,128]{2,1,0:T(8,128)(2,1)S(1)}, bf16[16,128,128]{2,1,0:T(8,128)(2,1)}, u32[]{:S(2)}) copy-start(bf16[16,128,128]{2,1,0:T(8,128)(2,1)} %right_ref.1) | copy-start | bytes 1572868
  14.0 4.3 %collective-permute-start.4 = (bf16[4,128,128]{2,1,0:T(8,128)(2,1)S(1)}, bf16[4,128,128]{2,1,0:T(8,128)(2,1)S(1)}, u32[]{:S(2)}, u32[]{:S(2)}) collective-permute-start(bf16[4,128,128]{2,1,0:T(8,128)(2,1)S(1)} %collective-permute-done.2), channel_id=1, source_target_pairs={{0,1},{1,0},{2,3},{3,2},{4,5},{5,4},{6,7},{7,6},{8,9},{9,8},{10,11... | collective-permute-start | bytes 393224 | tf_op jit(solution)/shard_map/ppermute | solution.py:48
  16.9 2.1 %collective-permute-start.3 = (bf16[8,128,128]{2,1,0:T(8,128)(2,1)S(1)}, bf16[8,128,128]{2,1,0:T(8,128)(2,1)S(1)}, u32[]{:S(2)}, u32[]{:S(2)}) collective-permute-start(bf16[8,128,128]{2,1,0:T(8,128)(2,1)S(1)} %pad_maximum_fusion), channel_id=1, source_target_pairs={{0,0},{1,3},{2,2},{3,1},{4,4},{5,7},{6,6},{7,5},{8,8},{9,11},{10,1... | collective-permute-start | bytes 786440 | tf_op jit(solution)/shard_map/ppermute | solution.py:44
  19.0 6.2 %collective-permute-start.6 = (bf16[8,128,128]{2,1,0:T(8,128)(2,1)S(1)}, bf16[8,128,128]{2,1,0:T(8,128)(2,1)S(1)}, u32[]{:S(2)}, u32[]{:S(2)}) collective-permute-start(bf16[8,128,128]{2,1,0:T(8,128)(2,1)S(1)} %collective-permute-done.3), channel_id=1, source_target_pairs={{0,1},{1,0},{2,3},{3,2},{4,5},{5,4},{6,7},{7,6},{8,9},{9,8},{10,11... | collective-permute-start | bytes 786440 | tf_op jit(solution)/shard_map/ppermute | solution.py:48
  27.8 5.1 %collective-permute-start.8 = (f32[8,128,128]{2,1,0:T(8,128)S(1)}, f32[8,128,128]{2,1,0:T(8,128)S(1)}, u32[]{:S(2)}, u32[]{:S(2)}) collective-permute-start(f32[8,128,128]{2,1,0:T(8,128)S(1)} %get-tuple-element.28), channel_id=1, source_target_pairs={{0,1},{1,0},{2,3},{3,2},{4,5},{5,4},{6,7},{7,6},{8,9},{9,8},{10,11... | collective-permute-start | bytes 1572872 | tf_op jit(solution)/shard_map/ppermute | solution.py:48
  31.9 2.5 %collective-permute-start.7 = (f32[8,128,128]{2,1,0:T(8,128)S(1)}, f32[8,128,128]{2,1,0:T(8,128)S(1)}, u32[]{:S(2)}, u32[]{:S(2)}) collective-permute-start(f32[8,128,128]{2,1,0:T(8,128)S(1)} %constant_dynamic-update-slice_fusion), channel_id=1, source_target_pairs={{0,1},{1,0},{2,3},{3,2},{4,5},{5,4},{6,7},{7,6},{8,9},{9,8},{10,11... | collective-permute-start | bytes 1572872 | tf_op jit(solution)/shard_map/ppermute | solution.py:48
  32.9 1.5 %collective-permute-start.9 = (bf16[8,128,128]{2,1,0:T(8,128)(2,1)S(1)}, bf16[8,128,128]{2,1,0:T(8,128)(2,1)S(1)}, u32[]{:S(2)}, u32[]{:S(2)}) collective-permute-start(bf16[8,128,128]{2,1,0:T(8,128)(2,1)S(1)} %add_convert_fusion), channel_id=1, source_target_pairs={{0,0},{1,3},{2,2},{3,1},{4,4},{5,7},{6,6},{7,5},{8,8},{9,11},{10,1... | collective-permute-start | bytes 786440 | tf_op jit(solution)/shard_map/ppermute | solution.py:44
  34.5 0.7 %collective-permute-start.10 = (bf16[4,128,128]{2,1,0:T(8,128)(2,1)S(1)}, bf16[4,128,128]{2,1,0:T(8,128)(2,1)S(1)}, u32[]{:S(2)}, u32[]{:S(2)}) collective-permute-start(bf16[4,128,128]{2,1,0:T(8,128)(2,1)S(1)} %slice.37), channel_id=1, source_target_pairs={{0,0},{1,5},{2,2},{3,7},{4,4},{5,1},{6,6},{7,3},{8,8},{9,13},{10,1... | collective-permute-start | bytes 393224 | tf_op jit(solution)/shard_map/ppermute | solution.py:44
  35.2 0.7 %collective-permute-start.11 = (bf16[2,128,128]{2,1,0:T(8,128)(2,1)S(1)}, bf16[2,128,128]{2,1,0:T(8,128)(2,1)S(1)}, u32[]{:S(2)}, u32[]{:S(2)}) collective-permute-start(bf16[2,128,128]{2,1,0:T(8,128)(2,1)S(1)} %slice.38), channel_id=1, source_target_pairs={{0,0},{1,9},{2,2},{3,11},{4,4},{5,13},{6,6},{7,15},{8,8},{9,1},{10... | collective-permute-start | bytes 196616 | tf_op jit(solution)/shard_map/ppermute | solution.py:44
  35.9 17.4 %collective-permute-start.12 = (f32[1,128,128]{2,1,0:T(8,128)S(1)}, f32[1,128,128]{2,1,0:T(8,128)S(1)}, u32[]{:S(2)}, u32[]{:S(2)}) collective-permute-start(f32[1,128,128]{2,1,0:T(8,128)S(1)} %slice.30), channel_id=1, source_target_pairs={{0,1},{1,0},{2,3},{3,2},{4,5},{5,4},{6,7},{7,6},{8,9},{9,8},{10,11... | collective-permute-start | bytes 196616 | tf_op jit(solution)/shard_map/ppermute | solution.py:48

commit v3 on v0

--- a/solution.py
+++ b/solution.py
@@ -48,7 +48,12 @@
     return lax.ppermute(x, "ops", [(i, i ^ 1) for i in range(OPS)])
 
 
-def place(sector, me):
+def between_chips(x):
+    same_core = [list(range(core, OPS, 2)) for core in range(2)]
+    return lax.all_to_all(x, "ops", 0, 0, axis_index_groups=same_core, tiled=True)
+
+
+def source_place(sector, me):
     near = sector ^ me
     spots = [
         sum(((near >> bit) & 1) << step for step, bit in enumerate(chain)) for chain in CHAINS
@@ -56,6 +61,10 @@
     return (near & 1) * (OPS // 2) + jnp.where(sector & 1 == 0, spots[0], spots[1])
 
 
+def target_place(sector, me):
+    return ((sector ^ me) & 1) * (OPS // 2) + (sector >> 1)
+
+
 def order_kernel(nops, coup_ref, out_ref):
     slots = coup_ref.shape[1]
     cells = OPS * nops
@@ -63,8 +72,8 @@
 
     g = coup_ref[0:1, :]
     alive = iota((1, slots), 1) < coup_ref[3:4, :]
-    cell = jnp.where(alive, place(coup_ref[2:3, :], me) * nops + g, cells)
-    block = place(coup_ref[1:2, :], me) * nops + g
+    cell = jnp.where(alive, target_place(coup_ref[2:3, :], me) * nops + g, cells)
+    block = source_place(coup_ref[1:2, :], me) * nops + g
     cell_col = as_column(cell)
     block_col = as_column(block)
     square = (slots, slots)
@@ -78,8 +87,7 @@
     number = count(here, 0)
     only = picked(here, block_col, 0)
     few = (number <= 4).astype(jnp.int32) + (number <= 2).astype(jnp.int32)
-    group = (lane < cells // 2).astype(jnp.int32) + (lane < cells // 4).astype(jnp.int32)
-    kind = jnp.where(number < 2, 9, few + 3 * group)
+    kind = jnp.where(number < 2, 6, few + jnp.where(lane < cells // 2, 3, 0))
     square = (cells, cells)
     kind_col = as_column(kind)
     ahead = (kind_col < kind) | ((kind_col == kind) & (iota(square, 0) < iota(square, 1)))
@@ -91,7 +99,7 @@
     out_ref[:, SUM : SUM + cells] = (firsts << COUNT_BITS) + picked(chosen, as_column(number), 0)
     small = iota((1, 128), 1)
     ends = jnp.zeros((1, 128), jnp.int32)
-    for k in range(9):
+    for k in range(6):
         ends = jnp.where(small == k, count(kind <= k, 1), ends)
     out_ref[:, ENDS : ENDS + 128] = ends
 
@@ -275,7 +283,7 @@
         copy = pltpu.make_async_copy(order_in, order_ref, sem)
         copy.start()
         if extra:
-            fill(refs[0], refs[1], block_ref, OPS // 2)
+            fill(refs[0], refs[1], block_ref, OPS - psi.shape[0])
         copy.wait()
 
         def order(i):
@@ -332,26 +340,18 @@
     order = order_slots(left_ops.shape[0], couplings, live)
     four, order = lax.optimization_barrier((jnp.concatenate([two, came], axis=0), order))
     came = lax.ppermute(four, "ops", partners(2))
-    blocks = early(four, left, slots)
+    four, blocks = lax.optimization_barrier((four, early(four, left, slots)))
+    far_four = other_core(four)
     turned = turn(right_ops)
-    eight, turned, blocks = lax.optimization_barrier(
-        (jnp.concatenate([four, came], axis=0), turned, blocks)
-    )
-    far = other_core(eight)
+    blocks = more(far_four, left, blocks, 8)
+    came, turned, blocks = lax.optimization_barrier((came, turned, blocks))
+    far_four = other_core(came)
     blocks = more(came, left, blocks, 4)
-    blocks, send = terms(order, turned, blocks, 0, 8, 8, far, left)
+    blocks, send = terms(order, turned, blocks, 0, 8, 8, far_four, left)
     came = other_core(send)
-    blocks, next_four = terms(order, turned, blocks, 1, 4, 4)
-    leaving = (next_four + came[4:]).astype(jnp.bfloat16)
-    arrived = lax.ppermute(leaving, "ops", partners(2))
-    _, last_four = terms(order, turned, blocks, 2, 0, 4)
-    keep = last_four + came[:4]
-    for step in (1, 0):
-        half = keep.shape[0] // 2
-        both = keep + arrived.astype(jnp.float32)
-        keep, leaving = both[:half], both[half:].astype(jnp.bfloat16)
-        arrived = lax.ppermute(leaving, "ops", partners(step))
-    return keep + arrived.astype(jnp.float32)
+    _, keep = terms(order, turned, blocks, 1, 0, 8)
+    parts = between_chips((keep + came).astype(jnp.bfloat16))
+    return jnp.sum(parts.astype(jnp.float32), axis=0, keepdims=True)
 
 
 def shards_large(psi, left_ops, right_ops, couplings, live):

time: 38.4 us -> 39.5 us (1.029)
  blocking collectives: 0 us -> 15.3 us
  starting transfers between devices: 15.2 us -> 8.05 us
  waiting for transfers between devices: 10.1 us -> 3.53 us
  local copies, waits for them, and re-layouts: 3.56 us -> 2.5 us
  Pallas kernels: 7.66 us -> 8.1 us
    all_to_all x0 -> x1, blocking collectives: none -> 15.3 us  [between_chips(): lax.all_to_all(x, 'ops', 0, 0, axis_index_groups=same_core, tiled=True)]
    ppermute x3 -> x0, waiting for transfers between devices: 7.29 us -> none  [the longest x2 5.19 us: shards_small(): arrived = lax.ppermute(leaving, 'ops', partners(step))]
    ppermute x3 -> x0, starting transfers between devices: 6.24 us -> none  [the longest x2 4.72 us: shards_small(): arrived = lax.ppermute(leaving, 'ops', partners(step))]
    unnamed x6, local copies, waits for them, and re-layouts: 2.84 us -> 1.8 us
    ppermute x1, waiting for transfers between devices: 1.21 us -> 2.24 us  [shards_small(): came = lax.ppermute(four, 'ops', partners(2))]
    ppermute x2 -> x3, starting transfers between devices: 1.1 us -> 0.14 us  [other_core(): return lax.ppermute(x, 'ops', [(i, i ^ 1) for i in range(OPS)])]
    pallas_call x1 -> x2, Pallas kernels: 0.69 us -> 1.37 us  [more(): pl.pallas_call(kernel, out_shape=jax.ShapeDtypeStruct(blocks.shape, block...]
    add x3 -> x0, other arithmetic: 0.69 us -> none  [the longest x1 0.64 us: shards_small(): return keep + arrived.astype(jnp.float32)]
  transfers between devices with their start and end apart: 8 -> 6, of which waited for: 8 -> 4; matrix products, arithmetic and copies ran while one was open for 2% -> 2% of each run, Pallas kernels for 13% -> 12%
where the time goes in v3:
time: 39.5 us; the launch traced here: 38.9 us
  blocking collectives  15.3 us (39%)
  Pallas kernels  8.1 us (21%)
  starting transfers between devices  8.05 us (20%)
  waiting for transfers between devices  3.53 us (9%)
  local copies, waits for them, and re-layouts  2.5 us (6%)
  between operations  0.76 us (2%)
  other arithmetic  0.74 us (2%)
    all_to_all x1, blocking collectives, between_chips(): lax.all_to_all(x, 'ops', 0, 0, axis_index_groups=same_core, tiled=True)  15.3 us
    pallas_call x2, Pallas kernels, terms(): pl.pallas_call(kernel, out_shape=[jax.ShapeDtypeStruct(blocks.shape, bloc...  5.19 us
    ppermute x1, starting transfers between devices, shards_small(): came = lax.ppermute(psi, 'ops', partners(0))  4.04 us
    ppermute x1, waiting for transfers between devices, shards_small(): came = lax.ppermute(four, 'ops', partners(2))  2.24 us
    ppermute x1, starting transfers between devices, shards_small(): came = lax.ppermute(two, 'ops', partners(1))  1.97 us
    ppermute x1, starting transfers between devices, shards_small(): came = lax.ppermute(four, 'ops', partners(2))  1.89 us
    unnamed x6, local copies, waits for them, and re-layouts  1.8 us
    pallas_call x2, Pallas kernels, more(): pl.pallas_call(kernel, out_shape=jax.ShapeDtypeStruct(blocks.shape, block...  1.37 us
  transfers between devices with their start and end apart: 6, of which 4 were waited for; matrix products, arithmetic and copies ran while one was open for 2% of the time, Pallas kernels for 12%

profile of v3, /device:TPU:0, one launch (start us, length us, event | category | flops | bytes accessed | tf_op | source)
XLA Modules:
  0.0 38.9 jit_solution(17099612386276200533)
XLA Ops:
  0.0 4.0 %collective-permute-start = (bf16[1,128,128]{2,1,0:T(8,128)(2,1)}, bf16[1,128,128]{2,1,0:T(8,128)(2,1)S(1)}, u32[]{:S(2)}, u32[]{:S(2)}) collective-permute-start(bf16[1,128,128]{2,1,0:T(8,128)(2,1)} %psi_ref.1), channel_id=1, source_target_pairs={{0,8},{1,3},{2,10},{3,1},{4,12},{5,7},{6,14},{7,5},{8,0},{9,11},{1... | collective-permute-start | bytes 98312 | tf_op jit(solution)/shard_map/ppermute | solution.py:336
  4.0 0.0 copy-start
  4.0 1.0 %copy-done = bf16[16,128,128]{2,1,0:T(8,128)(2,1)S(1)} copy-done((bf16[16,128,128]{2,1,0:T(8,128)(2,1)S(1)}, bf16[16,128,128]{2,1,0:T(8,128)(2,1)}, u32[]{:S(2)}) %copy-start) | copy-done | bytes 524312
  5.1 0.0 copy-start.2
  5.1 0.8 %copy-done.2 = bf16[1,128,128]{2,1,0:T(8,128)(2,1)S(1)} copy-done((bf16[1,128,128]{2,1,0:T(8,128)(2,1)S(1)}, bf16[1,128,128]{2,1,0:T(8,128)(2,1)}, u32[]{:S(2)}) %copy-start.2) | copy-done | bytes 32792
  5.8 0.0 copy-start.1
  5.9 0.3 collective-permute-done
  6.2 2.0 %collective-permute-start.1 = (bf16[2,128,128]{2,1,0:T(8,128)(2,1)S(1)}, bf16[2,128,128]{2,1,0:T(8,128)(2,1)S(1)}, u32[]{:S(2)}, u32[]{:S(2)}) collective-permute-start(bf16[2,128,128]{2,1,0:T(8,128)(2,1)S(1)} %pad_maximum_fusion.1), channel_id=1, source_target_pairs={{0,4},{1,9},{2,6},{3,11},{4,0},{5,13},{6,2},{7,15},{8,12},{9,1},{1... | collective-permute-start | bytes 196616 | tf_op jit(solution)/shard_map/ppermute | solution.py:339
  8.8 0.7 %concatenate.11.refs_0_ = s32[4,384]{1,0:T(4,128)S(1)} pad(s32[3,384]{1,0:T(4,128)} %param.8, s32[]{:T(128)} %bitcast.2), padding=0_1x0_0 | pad | bytes 10756 | tf_op jit(solution)/shard_map/concatenate | solution.py:117
  9.5 0.6 %order.1.order_in = s32[1,1024]{1,0:T(1,128)S(1)} custom-call(s32[4,384]{1,0:T(4,128)S(1)} %concatenate.11.refs_0_), custom_call_target="tpu_custom_call" | custom-call | flops 2949120 | bytes 1048576 | tf_op jit(solution)/shard_map/order/pallas_call | solution.py:118
  10.1 0.4 collective-permute-done.1
  10.5 0.7 %early.1._ = bf16[449,128,128]{2,1,0:T(8,128)(2,1)S(1)} custom-call(bf16[4,128,128]{2,1,0:T(8,128)(2,1)S(1)} %pad_maximum_fusion.psi_ref, bf16[16,128,128]{2,1,0:T(8,128)(2,1)S(1)} %get-tuple-element.24.left_ref.refs_1_), custom_call_target="tpu_custom_call" | custom-call | flops 268435456 | bytes 1048576 | tf_op jit(solution)/shard_map/early/pallas_call | solution.py:246
  11.2 0.1 collective-permute-start.3
  11.3 1.9 %collective-permute-start.2 = (bf16[4,128,128]{2,1,0:T(8,128)(2,1)S(1)}, bf16[4,128,128]{2,1,0:T(8,128)(2,1)S(1)}, u32[]{:S(2)}, u32[]{:S(2)}) collective-permute-start(bf16[4,128,128]{2,1,0:T(8,128)(2,1)S(1)} %pad_maximum_fusion.psi_ref), channel_id=1, source_target_pairs={{0,2},{1,5},{2,0},{3,7},{4,6},{5,1},{6,4},{7,3},{8,10},{9,13},{10,... | collective-permute-start | bytes 393224 | tf_op jit(solution)/shard_map/ppermute | solution.py:342
  13.2 0.0 copy-done.1
  13.2 0.2 turn.1.turned_ref
  13.4 0.0 collective-permute-done.3.psi_ref
  13.4 0.7 %more.2._ = bf16[449,128,128]{2,1,0:T(8,128)(2,1)S(1)} custom-call(bf16[4,128,128]{2,1,0:T(8,128)(2,1)S(1)} %collective-permute-done.3.psi_ref, bf16[16,128,128]{2,1,0:T(8,128)(2,1)S(1)} %get-tuple-element.24.left_ref.refs_1_, bf16[449,128,128]{2,1,0:T(8,128)(2,1)S(1)} %early.1._), custom_call_target="tpu_custom_call", output_to_operand_aliasing={{}: (2, {})} | custom-call | flops 268435456 | bytes 1048576 | tf_op jit(solution)/shard_map/more/pallas_call | solution.py:263
  14.1 2.2 %collective-permute-done.2.psi_ref = bf16[4,128,128]{2,1,0:T(8,128)(2,1)S(1)} collective-permute-done((bf16[4,128,128]{2,1,0:T(8,128)(2,1)S(1)}, bf16[4,128,128]{2,1,0:T(8,128)(2,1)S(1)}, u32[]{:S(2)}, u32[]{:S(2)}) %collective-permute-start.2) | collective-permute-done | bytes 131104 | tf_op jit(solution)/shard_map/ppermute | solution.py:342
  16.3 0.0 collective-permute-start.4
  16.3 0.7 %more.3.refs_2_ = bf16[449,128,128]{2,1,0:T(8,128)(2,1)S(1)} custom-call(bf16[4,128,128]{2,1,0:T(8,128)(2,1)S(1)} %collective-permute-done.2.psi_ref, bf16[16,128,128]{2,1,0:T(8,128)(2,1)S(1)} %get-tuple-element.24.left_ref.refs_1_, bf16[449,128,128]{2,1,0:T(8,128)(2,1)S(1)} %more.2._), custom_call_target="tpu_custom_call", output_to_operand_aliasing={{}: (2, {})} | custom-call | flops 268435456 | bytes 1048576 | tf_op jit(solution)/shard_map/more/pallas_call | solution.py:263
  17.0 0.7 %collective-permute-done.4.refs_0_ = bf16[4,128,128]{2,1,0:T(8,128)(2,1)S(1)} collective-permute-done((bf16[4,128,128]{2,1,0:T(8,128)(2,1)S(1)}, bf16[4,128,128]{2,1,0:T(8,128)(2,1)S(1)}, u32[]{:S(2)}, u32[]{:S(2)}) %collective-permute-start.4) | collective-permute-done | bytes 131104 | tf_op jit(solution)/shard_map/ppermute | solution.py:48
  17.7 2.7 %terms_0.1 = (bf16[449,128,128]{2,1,0:T(8,128)(2,1)S(1)}, f32[8,128,128]{2,1,0:T(8,128)S(1)}) custom-call(s32[1,1024]{1,0:T(1,128)S(1)} %order.1.order_in, bf16[2048,128]{1,0:T(8,128)(2,1)S(1)} %turn.1.turned_ref, bf16[4,128,128]{2,1,0:T(8,128)(2,1)S(1)} %collective-permute-done.4.refs_0_, ...), custom_call_target="tpu_custom_call", output_to_operand_aliasing={{0}: (4, {})} | custom-call | flops 1073741824 | bytes 1048576 | tf_op jit(solution)/shard_map/terms_0/pallas_call | solution.py:297
  20.4 0.1 collective-permute-start.5
  20.5 2.5 %terms_1.1 = (bf16[449,128,128]{2,1,0:T(8,128)(2,1)S(1)}, f32[8,128,128]{2,1,0:T(8,128)S(1)}) custom-call(s32[1,1024]{1,0:T(1,128)S(1)} %order.1.order_in, bf16[2048,128]{1,0:T(8,128)(2,1)S(1)} %turn.1.turned_ref, bf16[449,128,128]{2,1,0:T(8,128)(2,1)S(1)} %get-tuple-element.30.refs_0_), custom_call_target="tpu_custom_call", output_to_operand_aliasing={{0}: (2, {})} | custom-call | flops 536870912 | bytes 1048576 | tf_op jit(solution)/shard_map/terms_1/pallas_call | solution.py:297
  22.9 0.0 collective-permute-done.5
  23.0 0.1 add_convert_fusion
  23.0 15.3 %all_to_all.5 = bf16[8,128,128]{2,1,0:T(8,128)(2,1)S(1)} all-to-all(bf16[8,128,128]{2,1,0:T(8,128)(2,1)S(1)} %add_convert_fusion), channel_id=1, replica_groups={{0,2,4,6,8,10,12,14},{1,3,5,7,9,11,13,15},{16,18,20,22,24,26,28,30},{17..., dimensions={0} | all-to-all | bytes 524288 | tf_op jit(solution)/shard_map/all_to_all | solution.py:53
  38.3 0.7 %convert_reduce_fusion = f32[128,128]{1,0:T(8,128)} fusion(bf16[8,128,128]{2,1,0:T(8,128)(2,1)S(1)} %all_to_all.5), kind=kLoop, calls=%fused_computation | loop fusion | flops 245760 | bytes 327680 | tf_op jit(solution)/shard_map/reduce_sum | solution.py:354
  (3 shorter events, 0.1 us)
Async XLA Ops:
  0.0 6.1 %collective-permute-start = (bf16[1,128,128]{2,1,0:T(8,128)(2,1)}, bf16[1,128,128]{2,1,0:T(8,128)(2,1)S(1)}, u32[]{:S(2)}, u32[]{:S(2)}) collective-permute-start(bf16[1,128,128]{2,1,0:T(8,128)(2,1)} %psi_ref.1), channel_id=1, source_target_pairs={{0,8},{1,3},{2,10},{3,1},{4,12},{5,7},{6,14},{7,5},{8,0},{9,11},{1... | collective-permute-start | bytes 98312 | tf_op jit(solution)/shard_map/ppermute | solution.py:336
  4.0 1.0 %copy-start = (bf16[16,128,128]{2,1,0:T(8,128)(2,1)S(1)}, bf16[16,128,128]{2,1,0:T(8,128)(2,1)}, u32[]{:S(2)}) copy-start(bf16[16,128,128]{2,1,0:T(8,128)(2,1)} %left_ref.1) | copy-start | bytes 1572868
  5.1 0.8 %copy-start.2 = (bf16[1,128,128]{2,1,0:T(8,128)(2,1)S(1)}, bf16[1,128,128]{2,1,0:T(8,128)(2,1)}, u32[]{:S(2)}) copy-start(bf16[1,128,128]{2,1,0:T(8,128)(2,1)} %psi_ref.1) | copy-start | bytes 98308
  5.8 7.3 %copy-start.1 = (bf16[16,128,128]{2,1,0:T(8,128)(2,1)S(1)}, bf16[16,128,128]{2,1,0:T(8,128)(2,1)}, u32[]{:S(2)}) copy-start(bf16[16,128,128]{2,1,0:T(8,128)(2,1)} %right_ref.1) | copy-start | bytes 1572868
  6.2 4.3 %collective-permute-start.1 = (bf16[2,128,128]{2,1,0:T(8,128)(2,1)S(1)}, bf16[2,128,128]{2,1,0:T(8,128)(2,1)S(1)}, u32[]{:S(2)}, u32[]{:S(2)}) collective-permute-start(bf16[2,128,128]{2,1,0:T(8,128)(2,1)S(1)} %pad_maximum_fusion.1), channel_id=1, source_target_pairs={{0,4},{1,9},{2,6},{3,11},{4,0},{5,13},{6,2},{7,15},{8,12},{9,1},{1... | collective-permute-start | bytes 196616 | tf_op jit(solution)/shard_map/ppermute | solution.py:339
  11.2 2.2 %collective-permute-start.3 = (bf16[4,128,128]{2,1,0:T(8,128)(2,1)S(1)}, bf16[4,128,128]{2,1,0:T(8,128)(2,1)S(1)}, u32[]{:S(2)}, u32[]{:S(2)}) collective-permute-start(bf16[4,128,128]{2,1,0:T(8,128)(2,1)S(1)} %pad_maximum_fusion.psi_ref), channel_id=1, source_target_pairs={{0,1},{1,0},{2,3},{3,2},{4,5},{5,4},{6,7},{7,6},{8,9},{9,8},{10,11... | collective-permute-start | bytes 393224 | tf_op jit(solution)/shard_map/ppermute | solution.py:48
  11.3 5.0 %collective-permute-start.2 = (bf16[4,128,128]{2,1,0:T(8,128)(2,1)S(1)}, bf16[4,128,128]{2,1,0:T(8,128)(2,1)S(1)}, u32[]{:S(2)}, u32[]{:S(2)}) collective-permute-start(bf16[4,128,128]{2,1,0:T(8,128)(2,1)S(1)} %pad_maximum_fusion.psi_ref), channel_id=1, source_target_pairs={{0,2},{1,5},{2,0},{3,7},{4,6},{5,1},{6,4},{7,3},{8,10},{9,13},{10,... | collective-permute-start | bytes 393224 | tf_op jit(solution)/shard_map/ppermute | solution.py:342
  16.3 1.3 %collective-permute-start.4 = (bf16[4,128,128]{2,1,0:T(8,128)(2,1)S(1)}, bf16[4,128,128]{2,1,0:T(8,128)(2,1)S(1)}, u32[]{:S(2)}, u32[]{:S(2)}) collective-permute-start(bf16[4,128,128]{2,1,0:T(8,128)(2,1)S(1)} %collective-permute-done.2.psi_ref), channel_id=1, source_target_pairs={{0,1},{1,0},{2,3},{3,2},{4,5},{5,4},{6,7},{7,6},{8,9},{9,8},{10,11... | collective-permute-start | bytes 393224 | tf_op jit(solution)/shard_map/ppermute | solution.py:48
  20.4 2.5 %collective-permute-start.5 = (f32[8,128,128]{2,1,0:T(8,128)S(1)}, f32[8,128,128]{2,1,0:T(8,128)S(1)}, u32[]{:S(2)}, u32[]{:S(2)}) collective-permute-start(f32[8,128,128]{2,1,0:T(8,128)S(1)} %get-tuple-element.32), channel_id=1, source_target_pairs={{0,1},{1,0},{2,3},{3,2},{4,5},{5,4},{6,7},{7,6},{8,9},{9,8},{10,11... | collective-permute-start | bytes 1572872 | tf_op jit(solution)/shard_map/ppermute | solution.py:48

commit v4 on v3

--- a/solution.py
+++ b/solution.py
@@ -340,14 +340,14 @@
     order = order_slots(left_ops.shape[0], couplings, live)
     four, order = lax.optimization_barrier((jnp.concatenate([two, came], axis=0), order))
     came = lax.ppermute(four, "ops", partners(2))
-    four, blocks = lax.optimization_barrier((four, early(four, left, slots)))
-    far_four = other_core(four)
+    blocks = early(four, left, slots)
     turned = turn(right_ops)
-    blocks = more(far_four, left, blocks, 8)
-    came, turned, blocks = lax.optimization_barrier((came, turned, blocks))
-    far_four = other_core(came)
+    eight, turned, blocks = lax.optimization_barrier(
+        (jnp.concatenate([four, came], axis=0), turned, blocks)
+    )
+    far = other_core(eight)
     blocks = more(came, left, blocks, 4)
-    blocks, send = terms(order, turned, blocks, 0, 8, 8, far_four, left)
+    blocks, send = terms(order, turned, blocks, 0, 8, 8, far, left)
     came = other_core(send)
     _, keep = terms(order, turned, blocks, 1, 0, 8)
     parts = between_chips((keep + came).astype(jnp.bfloat16))

time: 39.5 us -> 39 us (0.987)
  blocking collectives: 15.3 us -> 13.8 us
  local copies, waits for them, and re-layouts: 2.5 us -> 3.54 us
  Pallas kernels: 8.1 us -> 9.07 us
  waiting for transfers between devices: 3.53 us -> 2.68 us
    pallas_call x2, Pallas kernels: 5.19 us -> 6.85 us  [terms(): pl.pallas_call(kernel, out_shape=[jax.ShapeDtypeStruct(blocks.shape, bloc...]
    all_to_all x1, blocking collectives: 15.3 us -> 13.8 us  [between_chips(): lax.all_to_all(x, 'ops', 0, 0, axis_index_groups=same_core, tiled=True)]
    unnamed x6, local copies, waits for them, and re-layouts: 1.8 us -> 2.84 us
    ppermute x1, waiting for transfers between devices: 2.24 us -> 1.21 us  [shards_small(): came = lax.ppermute(four, 'ops', partners(2))]
    pallas_call x2 -> x1, Pallas kernels: 1.37 us -> 0.69 us  [more(): pl.pallas_call(kernel, out_shape=jax.ShapeDtypeStruct(blocks.shape, block...]
    ppermute x3 -> x2, waiting for transfers between devices: 0.66 us -> 0.83 us  [other_core(): return lax.ppermute(x, 'ops', [(i, i ^ 1) for i in range(OPS)])]
  transfers between devices with their start and end apart: 6 -> 5, of which waited for: 4 -> 4; matrix products, arithmetic and copies ran while one was open for 2% -> 2% of each run, Pallas kernels for 12% -> 14%
where the time goes in v4:
time: 39 us; the launch traced here: 38.6 us
  blocking collectives  13.8 us (35%)
  Pallas kernels  9.07 us (23%)
  starting transfers between devices  8.04 us (21%)
  local copies, waits for them, and re-layouts  3.54 us (9%)
  waiting for transfers between devices  2.68 us (7%)
  other arithmetic  0.78 us (2%)
  between operations  0.74 us (2%)
    all_to_all x1, blocking collectives, between_chips(): lax.all_to_all(x, 'ops', 0, 0, axis_index_groups=same_core, tiled=True)  13.8 us
    pallas_call x2, Pallas kernels, terms(): pl.pallas_call(kernel, out_shape=[jax.ShapeDtypeStruct(blocks.shape, bloc...  6.85 us
    ppermute x1, starting transfers between devices, shards_small(): came = lax.ppermute(psi, 'ops', partners(0))  4.04 us
    unnamed x6, local copies, waits for them, and re-layouts  2.84 us
    ppermute x1, starting transfers between devices, shards_small(): came = lax.ppermute(two, 'ops', partners(1))  1.97 us
    ppermute x1, starting transfers between devices, shards_small(): came = lax.ppermute(four, 'ops', partners(2))  1.89 us
    ppermute x1, waiting for transfers between devices, shards_small(): came = lax.ppermute(four, 'ops', partners(2))  1.21 us
    ppermute x2, waiting for transfers between devices, other_core(): return lax.ppermute(x, 'ops', [(i, i ^ 1) for i in range(OPS)])  0.83 us
  transfers between devices with their start and end apart: 5, of which 4 were waited for; matrix products, arithmetic and copies ran while one was open for 2% of the time, Pallas kernels for 14%

profile of v4, /device:TPU:0, one launch (start us, length us, event | category | flops | bytes accessed | tf_op | source)
XLA Modules:
  0.0 38.6 jit_solution(9112785502042302457)
XLA Ops:
  0.0 4.0 %collective-permute-start = (bf16[1,128,128]{2,1,0:T(8,128)(2,1)}, bf16[1,128,128]{2,1,0:T(8,128)(2,1)S(1)}, u32[]{:S(2)}, u32[]{:S(2)}) collective-permute-start(bf16[1,128,128]{2,1,0:T(8,128)(2,1)} %psi_ref.1), channel_id=1, source_target_pairs={{0,8},{1,3},{2,10},{3,1},{4,12},{5,7},{6,14},{7,5},{8,0},{9,11},{1... | collective-permute-start | bytes 98312 | tf_op jit(solution)/shard_map/ppermute | solution.py:336
  4.0 0.0 copy-start
  4.0 1.0 %copy-done = bf16[16,128,128]{2,1,0:T(8,128)(2,1)S(1)} copy-done((bf16[16,128,128]{2,1,0:T(8,128)(2,1)S(1)}, bf16[16,128,128]{2,1,0:T(8,128)(2,1)}, u32[]{:S(2)}) %copy-start) | copy-done | bytes 524312
  5.1 0.0 copy-start.2
  5.1 0.8 %copy-done.2 = bf16[1,128,128]{2,1,0:T(8,128)(2,1)S(1)} copy-done((bf16[1,128,128]{2,1,0:T(8,128)(2,1)S(1)}, bf16[1,128,128]{2,1,0:T(8,128)(2,1)}, u32[]{:S(2)}) %copy-start.2) | copy-done | bytes 32792
  5.9 0.3 collective-permute-done
  6.2 2.0 %collective-permute-start.1 = (bf16[2,128,128]{2,1,0:T(8,128)(2,1)S(1)}, bf16[2,128,128]{2,1,0:T(8,128)(2,1)S(1)}, u32[]{:S(2)}, u32[]{:S(2)}) collective-permute-start(bf16[2,128,128]{2,1,0:T(8,128)(2,1)S(1)} %pad_maximum_fusion.2), channel_id=1, source_target_pairs={{0,4},{1,9},{2,6},{3,11},{4,0},{5,13},{6,2},{7,15},{8,12},{9,1},{1... | collective-permute-start | bytes 196616 | tf_op jit(solution)/shard_map/ppermute | solution.py:339
  8.8 0.7 %concatenate.14.refs_0_ = s32[4,384]{1,0:T(4,128)S(1)} pad(s32[3,384]{1,0:T(4,128)} %param.8, s32[]{:T(128)} %bitcast.2), padding=0_1x0_0 | pad | bytes 10756 | tf_op jit(solution)/shard_map/concatenate | solution.py:117
  9.5 0.6 %order.1.order_in = s32[1,1024]{1,0:T(1,128)S(1)} custom-call(s32[4,384]{1,0:T(4,128)S(1)} %concatenate.14.refs_0_), custom_call_target="tpu_custom_call" | custom-call | flops 2949120 | bytes 1048576 | tf_op jit(solution)/shard_map/order/pallas_call | solution.py:118
  10.1 0.4 collective-permute-done.1
  10.5 1.9 %collective-permute-start.2 = (bf16[4,128,128]{2,1,0:T(8,128)(2,1)S(1)}, bf16[4,128,128]{2,1,0:T(8,128)(2,1)S(1)}, u32[]{:S(2)}, u32[]{:S(2)}) collective-permute-start(bf16[4,128,128]{2,1,0:T(8,128)(2,1)S(1)} %pad_maximum_fusion.1.psi_ref), channel_id=1, source_target_pairs={{0,2},{1,5},{2,0},{3,7},{4,6},{5,1},{6,4},{7,3},{8,10},{9,13},{10,... | collective-permute-start | bytes 393224 | tf_op jit(solution)/shard_map/ppermute | solution.py:342
  12.4 0.0 copy-start.1
  12.4 1.0 %copy-done.1 = bf16[16,128,128]{2,1,0:T(8,128)(2,1)S(1)} copy-done((bf16[16,128,128]{2,1,0:T(8,128)(2,1)S(1)}, bf16[16,128,128]{2,1,0:T(8,128)(2,1)}, u32[]{:S(2)}) %copy-start.1) | copy-done | bytes 524312
  13.4 0.2 turn.1.turned_ref
  13.6 0.7 %early.1._ = bf16[449,128,128]{2,1,0:T(8,128)(2,1)S(1)} custom-call(bf16[4,128,128]{2,1,0:T(8,128)(2,1)S(1)} %pad_maximum_fusion.1.psi_ref, bf16[16,128,128]{2,1,0:T(8,128)(2,1)S(1)} %get-tuple-element.22.left_ref.refs_1_), custom_call_target="tpu_custom_call" | custom-call | flops 268435456 | bytes 1048576 | tf_op jit(solution)/shard_map/early/pallas_call | solution.py:246
  14.3 1.2 %collective-permute-done.2.psi_ref = bf16[4,128,128]{2,1,0:T(8,128)(2,1)S(1)} collective-permute-done((bf16[4,128,128]{2,1,0:T(8,128)(2,1)S(1)}, bf16[4,128,128]{2,1,0:T(8,128)(2,1)S(1)}, u32[]{:S(2)}, u32[]{:S(2)}) %collective-permute-start.2) | collective-permute-done | bytes 131104 | tf_op jit(solution)/shard_map/ppermute | solution.py:342
  15.6 0.1 collective-permute-start.3
  15.6 0.7 %more.1.refs_2_ = bf16[449,128,128]{2,1,0:T(8,128)(2,1)S(1)} custom-call(bf16[4,128,128]{2,1,0:T(8,128)(2,1)S(1)} %collective-permute-done.2.psi_ref, bf16[16,128,128]{2,1,0:T(8,128)(2,1)S(1)} %get-tuple-element.22.left_ref.refs_1_, bf16[449,128,128]{2,1,0:T(8,128)(2,1)S(1)} %early.1._), custom_call_target="tpu_custom_call", output_to_operand_aliasing={{}: (2, {})} | custom-call | flops 268435456 | bytes 1048576 | tf_op jit(solution)/shard_map/more/pallas_call | solution.py:263
  16.3 0.8 %collective-permute-done.3.refs_0_ = bf16[8,128,128]{2,1,0:T(8,128)(2,1)S(1)} collective-permute-done((bf16[8,128,128]{2,1,0:T(8,128)(2,1)S(1)}, bf16[8,128,128]{2,1,0:T(8,128)(2,1)S(1)}, u32[]{:S(2)}, u32[]{:S(2)}) %collective-permute-start.3) | collective-permute-done | bytes 262176 | tf_op jit(solution)/shard_map/ppermute | solution.py:48
  17.2 3.7 %terms_0.1 = (bf16[449,128,128]{2,1,0:T(8,128)(2,1)S(1)}, f32[8,128,128]{2,1,0:T(8,128)S(1)}) custom-call(s32[1,1024]{1,0:T(1,128)S(1)} %order.1.order_in, bf16[2048,128]{1,0:T(8,128)(2,1)S(1)} %turn.1.turned_ref, bf16[8,128,128]{2,1,0:T(8,128)(2,1)S(1)} %collective-permute-done.3.refs_0_, ...), custom_call_target="tpu_custom_call", output_to_operand_aliasing={{0}: (4, {})} | custom-call | flops 1073741824 | bytes 1048576 | tf_op jit(solution)/shard_map/terms_0/pallas_call | solution.py:297
  20.9 0.1 collective-permute-start.4
  21.0 3.1 %terms_1.1 = (bf16[449,128,128]{2,1,0:T(8,128)(2,1)S(1)}, f32[8,128,128]{2,1,0:T(8,128)S(1)}) custom-call(s32[1,1024]{1,0:T(1,128)S(1)} %order.1.order_in, bf16[2048,128]{1,0:T(8,128)(2,1)S(1)} %turn.1.turned_ref, bf16[449,128,128]{2,1,0:T(8,128)(2,1)S(1)} %get-tuple-element.26.refs_0_), custom_call_target="tpu_custom_call", output_to_operand_aliasing={{0}: (2, {})} | custom-call | flops 536870912 | bytes 1048576 | tf_op jit(solution)/shard_map/terms_1/pallas_call | solution.py:297
  24.1 0.0 collective-permute-done.4
  24.1 0.1 add_convert_fusion
  24.2 13.8 %all_to_all.5 = bf16[8,128,128]{2,1,0:T(8,128)(2,1)S(1)} all-to-all(bf16[8,128,128]{2,1,0:T(8,128)(2,1)S(1)} %add_convert_fusion), channel_id=1, replica_groups={{0,2,4,6,8,10,12,14},{1,3,5,7,9,11,13,15},{16,18,20,22,24,26,28,30},{17..., dimensions={0} | all-to-all | bytes 524288 | tf_op jit(solution)/shard_map/all_to_all | solution.py:53
  38.0 0.7 %convert_reduce_fusion = f32[128,128]{1,0:T(8,128)} fusion(bf16[8,128,128]{2,1,0:T(8,128)(2,1)S(1)} %all_to_all.5), kind=kLoop, calls=%fused_computation | loop fusion | flops 245760 | bytes 327680 | tf_op jit(solution)/shard_map/reduce_sum | solution.py:354
  (4 shorter events, 0.1 us)
Async XLA Ops:
  0.0 6.1 %collective-permute-start = (bf16[1,128,128]{2,1,0:T(8,128)(2,1)}, bf16[1,128,128]{2,1,0:T(8,128)(2,1)S(1)}, u32[]{:S(2)}, u32[]{:S(2)}) collective-permute-start(bf16[1,128,128]{2,1,0:T(8,128)(2,1)} %psi_ref.1), channel_id=1, source_target_pairs={{0,8},{1,3},{2,10},{3,1},{4,12},{5,7},{6,14},{7,5},{8,0},{9,11},{1... | collective-permute-start | bytes 98312 | tf_op jit(solution)/shard_map/ppermute | solution.py:336
  4.0 1.0 %copy-start = (bf16[16,128,128]{2,1,0:T(8,128)(2,1)S(1)}, bf16[16,128,128]{2,1,0:T(8,128)(2,1)}, u32[]{:S(2)}) copy-start(bf16[16,128,128]{2,1,0:T(8,128)(2,1)} %left_ref.1) | copy-start | bytes 1572868
  5.1 0.8 %copy-start.2 = (bf16[1,128,128]{2,1,0:T(8,128)(2,1)S(1)}, bf16[1,128,128]{2,1,0:T(8,128)(2,1)}, u32[]{:S(2)}) copy-start(bf16[1,128,128]{2,1,0:T(8,128)(2,1)} %psi_ref.1) | copy-start | bytes 98308
  6.2 4.3 %collective-permute-start.1 = (bf16[2,128,128]{2,1,0:T(8,128)(2,1)S(1)}, bf16[2,128,128]{2,1,0:T(8,128)(2,1)S(1)}, u32[]{:S(2)}, u32[]{:S(2)}) collective-permute-start(bf16[2,128,128]{2,1,0:T(8,128)(2,1)S(1)} %pad_maximum_fusion.2), channel_id=1, source_target_pairs={{0,4},{1,9},{2,6},{3,11},{4,0},{5,13},{6,2},{7,15},{8,12},{9,1},{1... | collective-permute-start | bytes 196616 | tf_op jit(solution)/shard_map/ppermute | solution.py:339
  10.5 5.0 %collective-permute-start.2 = (bf16[4,128,128]{2,1,0:T(8,128)(2,1)S(1)}, bf16[4,128,128]{2,1,0:T(8,128)(2,1)S(1)}, u32[]{:S(2)}, u32[]{:S(2)}) collective-permute-start(bf16[4,128,128]{2,1,0:T(8,128)(2,1)S(1)} %pad_maximum_fusion.1.psi_ref), channel_id=1, source_target_pairs={{0,2},{1,5},{2,0},{3,7},{4,6},{5,1},{6,4},{7,3},{8,10},{9,13},{10,... | collective-permute-start | bytes 393224 | tf_op jit(solution)/shard_map/ppermute | solution.py:342
  12.4 1.0 %copy-start.1 = (bf16[16,128,128]{2,1,0:T(8,128)(2,1)S(1)}, bf16[16,128,128]{2,1,0:T(8,128)(2,1)}, u32[]{:S(2)}) copy-start(bf16[16,128,128]{2,1,0:T(8,128)(2,1)} %right_ref.1) | copy-start | bytes 1572868
  15.6 1.6 %collective-permute-start.3 = (bf16[8,128,128]{2,1,0:T(8,128)(2,1)S(1)}, bf16[8,128,128]{2,1,0:T(8,128)(2,1)S(1)}, u32[]{:S(2)}, u32[]{:S(2)}) collective-permute-start(bf16[8,128,128]{2,1,0:T(8,128)(2,1)S(1)} %pad_maximum_fusion), channel_id=1, source_target_pairs={{0,1},{1,0},{2,3},{3,2},{4,5},{5,4},{6,7},{7,6},{8,9},{9,8},{10,11... | collective-permute-start | bytes 786440 | tf_op jit(solution)/shard_map/ppermute | solution.py:48
  20.9 3.2 %collective-permute-start.4 = (f32[8,128,128]{2,1,0:T(8,128)S(1)}, f32[8,128,128]{2,1,0:T(8,128)S(1)}, u32[]{:S(2)}, u32[]{:S(2)}) collective-permute-start(f32[8,128,128]{2,1,0:T(8,128)S(1)} %get-tuple-element.28), channel_id=1, source_target_pairs={{0,1},{1,0},{2,3},{3,2},{4,5},{5,4},{6,7},{7,6},{8,9},{9,8},{10,11... | collective-permute-start | bytes 1572872 | tf_op jit(solution)/shard_map/ppermute | solution.py:48

commit v5 on v0

--- a/solution.py
+++ b/solution.py
@@ -36,24 +36,19 @@
     return picked(iota((n, n), 0) == iota((n, n), 1), row, 1)
 
 
-CHAINS = ((3, 2, 1), (1, 3, 2))
+ALONG_Z = (4, 8, 12)
+ALONG_X = 2
+OTHER_CORE = 1
 OPS = 16
 
 
-def partners(step):
-    return [(i, i ^ (1 << CHAINS[i & 1][step])) for i in range(OPS)]
-
-
-def other_core(x):
-    return lax.ppermute(x, "ops", [(i, i ^ 1) for i in range(OPS)])
+def exchange(x, apart):
+    return lax.ppermute(x, "ops", [(i, i ^ apart) for i in range(OPS)])
 
 
 def place(sector, me):
     near = sector ^ me
-    spots = [
-        sum(((near >> bit) & 1) << step for step, bit in enumerate(chain)) for chain in CHAINS
-    ]
-    return (near & 1) * (OPS // 2) + jnp.where(sector & 1 == 0, spots[0], spots[1])
+    return (near >> 2) | ((near & 2) << 1) | ((near & 1) << 3)
 
 
 def order_kernel(nops, coup_ref, out_ref):
@@ -325,33 +320,30 @@
 
 def shards_small(psi, left_ops, right_ops, couplings, live):
     slots = couplings.shape[1]
-    came = lax.ppermute(psi, "ops", partners(0))
+    came = [exchange(psi, apart) for apart in ALONG_Z]
     psi, left = hold(psi, left_ops)
-    two, left = lax.optimization_barrier((jnp.concatenate([psi, came], axis=0), left))
-    came = lax.ppermute(two, "ops", partners(1))
     order = order_slots(left_ops.shape[0], couplings, live)
-    four, order = lax.optimization_barrier((jnp.concatenate([two, came], axis=0), order))
-    came = lax.ppermute(four, "ops", partners(2))
+    four, left, order = lax.optimization_barrier(
+        (jnp.concatenate([psi, *came], axis=0), left, order)
+    )
+    came = exchange(four, ALONG_X)
     blocks = early(four, left, slots)
     turned = turn(right_ops)
     eight, turned, blocks = lax.optimization_barrier(
         (jnp.concatenate([four, came], axis=0), turned, blocks)
     )
-    far = other_core(eight)
+    far = exchange(eight, OTHER_CORE)
     blocks = more(came, left, blocks, 4)
     blocks, send = terms(order, turned, blocks, 0, 8, 8, far, left)
-    came = other_core(send)
+    came = exchange(send, OTHER_CORE)
     blocks, next_four = terms(order, turned, blocks, 1, 4, 4)
-    leaving = (next_four + came[4:]).astype(jnp.bfloat16)
-    arrived = lax.ppermute(leaving, "ops", partners(2))
+    arrived = exchange((next_four + came[4:]).astype(jnp.bfloat16), ALONG_X)
     _, last_four = terms(order, turned, blocks, 2, 0, 4)
-    keep = last_four + came[:4]
-    for step in (1, 0):
-        half = keep.shape[0] // 2
-        both = keep + arrived.astype(jnp.float32)
-        keep, leaving = both[:half], both[half:].astype(jnp.bfloat16)
-        arrived = lax.ppermute(leaving, "ops", partners(step))
-    return keep + arrived.astype(jnp.float32)
+    total = last_four + came[:4] + arrived.astype(jnp.float32)
+    parts = [
+        exchange(total[k + 1].astype(jnp.bfloat16), apart) for k, apart in enumerate(ALONG_Z)
+    ]
+    return sum((part.astype(jnp.float32) for part in parts), total[0])[None]
 
 
 def shards_large(psi, left_ops, right_ops, couplings, live):

time: 38.4 us -> 37.3 us (0.971)
  starting transfers between devices: 15.2 us -> 12.8 us
  Pallas kernels: 7.66 us -> 8.69 us
  waiting for transfers between devices: 10.1 us -> 10.8 us
    ppermute x8 -> x10, starting transfers between devices: 15.2 us -> 12.8 us  [exchange(): return lax.ppermute(x, 'ops', [(i, i ^ apart) for i in range(OPS)])]
    pallas_call x3, Pallas kernels: 5.43 us -> 6.46 us  [terms(): pl.pallas_call(kernel, out_shape=[jax.ShapeDtypeStruct(blocks.shape, bloc...]
    add x3 -> x0, other arithmetic: 0.69 us -> none  [the longest x1 0.64 us: shards_small(): return keep + arrived.astype(jnp.float32)]
    ppermute x8 -> x10, waiting for transfers between devices: 10.1 us -> 10.8 us  [exchange(): return lax.ppermute(x, 'ops', [(i, i ^ apart) for i in range(OPS)])]
    broadcast_in_dim x0 -> x1, other arithmetic: none -> 0.65 us  [shards_small(): return sum((part.astype(jnp.float32) for part in parts), total[0])[None]]
  transfers between devices with their start and end apart: 8 -> 10, of which waited for: 8 -> 8; matrix products, arithmetic and copies ran while one was open for 2% -> 2% of each run, Pallas kernels for 13% -> 15%
where the time goes in v5:
time: 37.3 us
  starting transfers between devices  12.8 us (34%)
  waiting for transfers between devices  10.8 us (29%)
  Pallas kernels  8.69 us (23%)
  local copies, waits for them, and re-layouts  3.54 us (9%)
  between operations  0.78 us (2%)
  other arithmetic  0.76 us (2%)
    ppermute x10, starting transfers between devices, exchange(): return lax.ppermute(x, 'ops', [(i, i ^ apart) for i in range(OPS)])  12.8 us
    ppermute x10, waiting for transfers between devices, exchange(): return lax.ppermute(x, 'ops', [(i, i ^ apart) for i in range(OPS)])  10.8 us
    pallas_call x3, Pallas kernels, terms(): pl.pallas_call(kernel, out_shape=[jax.ShapeDtypeStruct(blocks.shape, bloc...  6.46 us
    unnamed x6, local copies, waits for them, and re-layouts  2.83 us
  transfers between devices with their start and end apart: 10, of which 8 were waited for; matrix products, arithmetic and copies ran while one was open for 2% of the time, Pallas kernels for 15%

profile of v5, /device:TPU:0, one launch (start us, length us, event | category | flops | bytes accessed | tf_op | source)
XLA Modules:
  0.0 37.3 jit_solution(15851164351755490342)
XLA Ops:
  0.0 3.0 %collective-permute-start = (bf16[1,128,128]{2,1,0:T(8,128)(2,1)}, bf16[1,128,128]{2,1,0:T(8,128)(2,1)S(1)}, u32[]{:S(2)}, u32[]{:S(2)}) collective-permute-start(bf16[1,128,128]{2,1,0:T(8,128)(2,1)} %psi_ref.1), channel_id=1, source_target_pairs={{0,4},{1,5},{2,6},{3,7},{4,0},{5,1},{6,2},{7,3},{8,12},{9,13},{10,... | collective-permute-start | bytes 98312 | tf_op jit(solution)/shard_map/ppermute | solution.py:46
  3.0 2.5 %collective-permute-start.2 = (bf16[1,128,128]{2,1,0:T(8,128)(2,1)}, bf16[1,128,128]{2,1,0:T(8,128)(2,1)S(1)}, u32[]{:S(2)}, u32[]{:S(2)}) collective-permute-start(bf16[1,128,128]{2,1,0:T(8,128)(2,1)} %psi_ref.1), channel_id=1, source_target_pairs={{0,12},{1,13},{2,14},{3,15},{4,8},{5,9},{6,10},{7,11},{8,4},{9,5},... | collective-permute-start | bytes 98312 | tf_op jit(solution)/shard_map/ppermute | solution.py:46
  5.5 0.1 collective-permute-start.1
  6.3 1.0 %copy-done = bf16[16,128,128]{2,1,0:T(8,128)(2,1)S(1)} copy-done((bf16[16,128,128]{2,1,0:T(8,128)(2,1)S(1)}, bf16[16,128,128]{2,1,0:T(8,128)(2,1)}, u32[]{:S(2)}) %copy-start) | copy-done | bytes 524312
  7.3 0.8 %copy-done.2 = bf16[1,128,128]{2,1,0:T(8,128)(2,1)S(1)} copy-done((bf16[1,128,128]{2,1,0:T(8,128)(2,1)S(1)}, bf16[1,128,128]{2,1,0:T(8,128)(2,1)}, u32[]{:S(2)}) %copy-start.2) | copy-done | bytes 32792
  8.1 0.7 %concatenate.10.refs_0_ = s32[4,384]{1,0:T(4,128)S(1)} pad(s32[3,384]{1,0:T(4,128)} %param.8, s32[]{:T(128)} %bitcast.19), padding=0_1x0_0 | pad | bytes 10756 | tf_op jit(solution)/shard_map/concatenate | solution.py:104
  8.8 0.6 %order.1.order_in = s32[1,1024]{1,0:T(1,128)S(1)} custom-call(s32[4,384]{1,0:T(4,128)S(1)} %concatenate.10.refs_0_), custom_call_target="tpu_custom_call" | custom-call | flops 2949120 | bytes 1048576 | tf_op jit(solution)/shard_map/order/pallas_call | solution.py:105
  9.4 0.0 collective-permute-done
  9.5 0.0 collective-permute-done.2
  9.5 1.4 %collective-permute-done.1 = bf16[1,128,128]{2,1,0:T(8,128)(2,1)S(1)} collective-permute-done((bf16[1,128,128]{2,1,0:T(8,128)(2,1)}, bf16[1,128,128]{2,1,0:T(8,128)(2,1)S(1)}, u32[]{:S(2)}, u32[]{:S(2)}) %collective-permute-start.1) | collective-permute-done | bytes 32800 | tf_op jit(solution)/shard_map/ppermute | solution.py:46
  10.9 1.6 %collective-permute-start.3 = (bf16[4,128,128]{2,1,0:T(8,128)(2,1)S(1)}, bf16[4,128,128]{2,1,0:T(8,128)(2,1)S(1)}, u32[]{:S(2)}, u32[]{:S(2)}) collective-permute-start(bf16[4,128,128]{2,1,0:T(8,128)(2,1)S(1)} %pad_maximum_fusion.1.psi_ref), channel_id=1, source_target_pairs={{0,2},{1,3},{2,0},{3,1},{4,6},{5,7},{6,4},{7,5},{8,10},{9,11},{10,... | collective-permute-start | bytes 393224 | tf_op jit(solution)/shard_map/ppermute | solution.py:46
  12.5 1.0 %copy-done.1 = bf16[16,128,128]{2,1,0:T(8,128)(2,1)S(1)} copy-done((bf16[16,128,128]{2,1,0:T(8,128)(2,1)S(1)}, bf16[16,128,128]{2,1,0:T(8,128)(2,1)}, u32[]{:S(2)}) %copy-start.1) | copy-done | bytes 524312
  13.5 0.2 turn.1.turned_ref
  13.7 0.7 %early.1._ = bf16[449,128,128]{2,1,0:T(8,128)(2,1)S(1)} custom-call(bf16[4,128,128]{2,1,0:T(8,128)(2,1)S(1)} %pad_maximum_fusion.1.psi_ref, bf16[16,128,128]{2,1,0:T(8,128)(2,1)S(1)} %get-tuple-element.22.left_ref.refs_1_), custom_call_target="tpu_custom_call" | custom-call | flops 268435456 | bytes 1048576 | tf_op jit(solution)/shard_map/early/pallas_call | solution.py:233
  14.4 1.5 %collective-permute-done.3.psi_ref = bf16[4,128,128]{2,1,0:T(8,128)(2,1)S(1)} collective-permute-done((bf16[4,128,128]{2,1,0:T(8,128)(2,1)S(1)}, bf16[4,128,128]{2,1,0:T(8,128)(2,1)S(1)}, u32[]{:S(2)}, u32[]{:S(2)}) %collective-permute-start.3) | collective-permute-done | bytes 131104 | tf_op jit(solution)/shard_map/ppermute | solution.py:46
  16.0 0.1 collective-permute-start.4
  16.0 0.7 %more.1.refs_2_ = bf16[449,128,128]{2,1,0:T(8,128)(2,1)S(1)} custom-call(bf16[4,128,128]{2,1,0:T(8,128)(2,1)S(1)} %collective-permute-done.3.psi_ref, bf16[16,128,128]{2,1,0:T(8,128)(2,1)S(1)} %get-tuple-element.22.left_ref.refs_1_, bf16[449,128,128]{2,1,0:T(8,128)(2,1)S(1)} %early.1._), custom_call_target="tpu_custom_call", output_to_operand_aliasing={{}: (2, {})} | custom-call | flops 268435456 | bytes 1048576 | tf_op jit(solution)/shard_map/more/pallas_call | solution.py:250
  16.7 0.8 %collective-permute-done.4.refs_0_ = bf16[8,128,128]{2,1,0:T(8,128)(2,1)S(1)} collective-permute-done((bf16[8,128,128]{2,1,0:T(8,128)(2,1)S(1)}, bf16[8,128,128]{2,1,0:T(8,128)(2,1)S(1)}, u32[]{:S(2)}, u32[]{:S(2)}) %collective-permute-start.4) | collective-permute-done | bytes 262176 | tf_op jit(solution)/shard_map/ppermute | solution.py:46
  17.6 3.2 %terms_0.1 = (bf16[449,128,128]{2,1,0:T(8,128)(2,1)S(1)}, f32[8,128,128]{2,1,0:T(8,128)S(1)}) custom-call(s32[1,1024]{1,0:T(1,128)S(1)} %order.1.order_in, bf16[2048,128]{1,0:T(8,128)(2,1)S(1)} %turn.1.turned_ref, bf16[8,128,128]{2,1,0:T(8,128)(2,1)S(1)} %collective-permute-done.4.refs_0_, ...), custom_call_target="tpu_custom_call", output_to_operand_aliasing={{0}: (4, {})} | custom-call | flops 1073741824 | bytes 1048576 | tf_op jit(solution)/shard_map/terms_0/pallas_call | solution.py:284
  20.8 0.1 collective-permute-start.5
  20.8 1.7 %terms_1.1 = (bf16[449,128,128]{2,1,0:T(8,128)(2,1)S(1)}, f32[4,128,128]{2,1,0:T(8,128)S(1)}) custom-call(s32[1,1024]{1,0:T(1,128)S(1)} %order.1.order_in, bf16[2048,128]{1,0:T(8,128)(2,1)S(1)} %turn.1.turned_ref, bf16[449,128,128]{2,1,0:T(8,128)(2,1)S(1)} %get-tuple-element.26.refs_0_), custom_call_target="tpu_custom_call", output_to_operand_aliasing={{0}: (2, {})} | custom-call | flops 268435456 | bytes 1048576 | tf_op jit(solution)/shard_map/terms_1/pallas_call | solution.py:284
  22.5 0.2 collective-permute-done.5
  22.8 1.9 %collective-permute-start.6 = (bf16[4,128,128]{2,1,0:T(8,128)(2,1)S(1)}, bf16[4,128,128]{2,1,0:T(8,128)(2,1)S(1)}, u32[]{:S(2)}, u32[]{:S(2)}) collective-permute-start(bf16[4,128,128]{2,1,0:T(8,128)(2,1)S(1)} %fusion), channel_id=1, source_target_pairs={{0,2},{1,3},{2,0},{3,1},{4,6},{5,7},{6,4},{7,5},{8,10},{9,11},{10,... | collective-permute-start | bytes 393224 | tf_op jit(solution)/shard_map/ppermute | solution.py:46
  24.7 1.6 %terms_2.1 = (bf16[449,128,128]{2,1,0:T(8,128)(2,1)S(1)}, f32[4,128,128]{2,1,0:T(8,128)S(1)}) custom-call(s32[1,1024]{1,0:T(1,128)S(1)} %order.1.order_in, bf16[2048,128]{1,0:T(8,128)(2,1)S(1)} %turn.1.turned_ref, bf16[449,128,128]{2,1,0:T(8,128)(2,1)S(1)} %get-tuple-element.27.refs_0_), custom_call_target="tpu_custom_call", output_to_operand_aliasing={{0}: (2, {})} | custom-call | flops 268435456 | bytes 1048576 | tf_op jit(solution)/shard_map/terms_2/pallas_call | solution.py:284
  26.3 2.3 %collective-permute-done.6 = bf16[4,128,128]{2,1,0:T(8,128)(2,1)S(1)} collective-permute-done((bf16[4,128,128]{2,1,0:T(8,128)(2,1)S(1)}, bf16[4,128,128]{2,1,0:T(8,128)(2,1)S(1)}, u32[]{:S(2)}, u32[]{:S(2)}) %collective-permute-start.6) | collective-permute-done | bytes 131104 | tf_op jit(solution)/shard_map/ppermute | solution.py:46
  28.7 0.5 %collective-permute-start.7 = (bf16[128,128]{1,0:T(8,128)(2,1)S(1)}, bf16[128,128]{1,0:T(8,128)(2,1)S(1)}, u32[]{:S(2)}, u32[]{:S(2)}) collective-permute-start(bf16[128,128]{1,0:T(8,128)(2,1)S(1)} %get-tuple-element.33), channel_id=1, source_target_pairs={{0,4},{1,5},{2,6},{3,7},{4,0},{5,1},{6,2},{7,3},{8,12},{9,13},{10,... | collective-permute-start | bytes 98312 | tf_op jit(solution)/shard_map/ppermute | solution.py:46
  29.2 2.7 %collective-permute-start.9 = (bf16[128,128]{1,0:T(8,128)(2,1)S(1)}, bf16[128,128]{1,0:T(8,128)(2,1)S(1)}, u32[]{:S(2)}, u32[]{:S(2)}) collective-permute-start(bf16[128,128]{1,0:T(8,128)(2,1)S(1)} %get-tuple-element.34), channel_id=1, source_target_pairs={{0,12},{1,13},{2,14},{3,15},{4,8},{5,9},{6,10},{7,11},{8,4},{9,5},... | collective-permute-start | bytes 98312 | tf_op jit(solution)/shard_map/ppermute | solution.py:46
  31.9 0.3 collective-permute-start.8
  32.2 0.4 %collective-permute-done.7 = bf16[128,128]{1,0:T(8,128)(2,1)S(1)} collective-permute-done((bf16[128,128]{1,0:T(8,128)(2,1)S(1)}, bf16[128,128]{1,0:T(8,128)(2,1)S(1)}, u32[]{:S(2)}, u32[]{:S(2)}) %collective-permute-start.7) | collective-permute-done | bytes 32800 | tf_op jit(solution)/shard_map/ppermute | solution.py:46
  32.6 2.3 %collective-permute-done.9 = bf16[128,128]{1,0:T(8,128)(2,1)S(1)} collective-permute-done((bf16[128,128]{1,0:T(8,128)(2,1)S(1)}, bf16[128,128]{1,0:T(8,128)(2,1)S(1)}, u32[]{:S(2)}, u32[]{:S(2)}) %collective-permute-start.9) | collective-permute-done | bytes 32800 | tf_op jit(solution)/shard_map/ppermute | solution.py:46
  34.9 1.8 %collective-permute-done.8 = bf16[128,128]{1,0:T(8,128)(2,1)S(1)} collective-permute-done((bf16[128,128]{1,0:T(8,128)(2,1)S(1)}, bf16[128,128]{1,0:T(8,128)(2,1)S(1)}, u32[]{:S(2)}, u32[]{:S(2)}) %collective-permute-start.8) | collective-permute-done | bytes 32800 | tf_op jit(solution)/shard_map/ppermute | solution.py:46
  36.7 0.6 %fusion.5 = f32[1,128,128]{2,1,0:T(8,128)} fusion(f32[4,128,128]{2,1,0:T(8,128)S(1)} %get-tuple-element.32, bf16[128,128]{1,0:T(8,128)(2,1)S(1)} %collective-permute-done.9, bf16[128,128]{1,0:T(8,128)(2,1)S(1)} %collective-permute-done.8, bf16[128,128]{1,0:T(8,128)(2,1)S(1)} %collective-permute-done.7), kind=kLoop, calls=%fused_computation.10 | loop fusion | flops 98304 | bytes 229376 | tf_op jit(solution)/shard_map/broadcast_in_dim | solution.py:346
  (9 shorter events, 0.2 us)
Async XLA Ops:
  0.0 9.4 %collective-permute-start = (bf16[1,128,128]{2,1,0:T(8,128)(2,1)}, bf16[1,128,128]{2,1,0:T(8,128)(2,1)S(1)}, u32[]{:S(2)}, u32[]{:S(2)}) collective-permute-start(bf16[1,128,128]{2,1,0:T(8,128)(2,1)} %psi_ref.1), channel_id=1, source_target_pairs={{0,4},{1,5},{2,6},{3,7},{4,0},{5,1},{6,2},{7,3},{8,12},{9,13},{10,... | collective-permute-start | bytes 98312 | tf_op jit(solution)/shard_map/ppermute | solution.py:46
  3.0 6.4 %collective-permute-start.2 = (bf16[1,128,128]{2,1,0:T(8,128)(2,1)}, bf16[1,128,128]{2,1,0:T(8,128)(2,1)S(1)}, u32[]{:S(2)}, u32[]{:S(2)}) collective-permute-start(bf16[1,128,128]{2,1,0:T(8,128)(2,1)} %psi_ref.1), channel_id=1, source_target_pairs={{0,12},{1,13},{2,14},{3,15},{4,8},{5,9},{6,10},{7,11},{8,4},{9,5},... | collective-permute-start | bytes 98312 | tf_op jit(solution)/shard_map/ppermute | solution.py:46
  5.5 5.4 %collective-permute-start.1 = (bf16[1,128,128]{2,1,0:T(8,128)(2,1)}, bf16[1,128,128]{2,1,0:T(8,128)(2,1)S(1)}, u32[]{:S(2)}, u32[]{:S(2)}) collective-permute-start(bf16[1,128,128]{2,1,0:T(8,128)(2,1)} %psi_ref.1), channel_id=1, source_target_pairs={{0,8},{1,9},{2,10},{3,11},{4,12},{5,13},{6,14},{7,15},{8,0},{9,1},... | collective-permute-start | bytes 98312 | tf_op jit(solution)/shard_map/ppermute | solution.py:46
  6.3 1.0 %copy-start = (bf16[16,128,128]{2,1,0:T(8,128)(2,1)S(1)}, bf16[16,128,128]{2,1,0:T(8,128)(2,1)}, u32[]{:S(2)}) copy-start(bf16[16,128,128]{2,1,0:T(8,128)(2,1)} %left_ref.1) | copy-start | bytes 1572868
  7.3 0.8 %copy-start.2 = (bf16[1,128,128]{2,1,0:T(8,128)(2,1)S(1)}, bf16[1,128,128]{2,1,0:T(8,128)(2,1)}, u32[]{:S(2)}) copy-start(bf16[1,128,128]{2,1,0:T(8,128)(2,1)} %psi_ref.1) | copy-start | bytes 98308
  10.9 5.0 %collective-permute-start.3 = (bf16[4,128,128]{2,1,0:T(8,128)(2,1)S(1)}, bf16[4,128,128]{2,1,0:T(8,128)(2,1)S(1)}, u32[]{:S(2)}, u32[]{:S(2)}) collective-permute-start(bf16[4,128,128]{2,1,0:T(8,128)(2,1)S(1)} %pad_maximum_fusion.1.psi_ref), channel_id=1, source_target_pairs={{0,2},{1,3},{2,0},{3,1},{4,6},{5,7},{6,4},{7,5},{8,10},{9,11},{10,... | collective-permute-start | bytes 393224 | tf_op jit(solution)/shard_map/ppermute | solution.py:46
  12.5 1.0 %copy-start.1 = (bf16[16,128,128]{2,1,0:T(8,128)(2,1)S(1)}, bf16[16,128,128]{2,1,0:T(8,128)(2,1)}, u32[]{:S(2)}) copy-start(bf16[16,128,128]{2,1,0:T(8,128)(2,1)} %right_ref.1) | copy-start | bytes 1572868
  16.0 1.6 %collective-permute-start.4 = (bf16[8,128,128]{2,1,0:T(8,128)(2,1)S(1)}, bf16[8,128,128]{2,1,0:T(8,128)(2,1)S(1)}, u32[]{:S(2)}, u32[]{:S(2)}) collective-permute-start(bf16[8,128,128]{2,1,0:T(8,128)(2,1)S(1)} %pad_maximum_fusion), channel_id=1, source_target_pairs={{0,1},{1,0},{2,3},{3,2},{4,5},{5,4},{6,7},{7,6},{8,9},{9,8},{10,11... | collective-permute-start | bytes 786440 | tf_op jit(solution)/shard_map/ppermute | solution.py:46
  20.8 2.0 %collective-permute-start.5 = (f32[8,128,128]{2,1,0:T(8,128)S(1)}, f32[8,128,128]{2,1,0:T(8,128)S(1)}, u32[]{:S(2)}, u32[]{:S(2)}) collective-permute-start(f32[8,128,128]{2,1,0:T(8,128)S(1)} %get-tuple-element.29), channel_id=1, source_target_pairs={{0,1},{1,0},{2,3},{3,2},{4,5},{5,4},{6,7},{7,6},{8,9},{9,8},{10,11... | collective-permute-start | bytes 1572872 | tf_op jit(solution)/shard_map/ppermute | solution.py:46
  22.8 5.8 %collective-permute-start.6 = (bf16[4,128,128]{2,1,0:T(8,128)(2,1)S(1)}, bf16[4,128,128]{2,1,0:T(8,128)(2,1)S(1)}, u32[]{:S(2)}, u32[]{:S(2)}) collective-permute-start(bf16[4,128,128]{2,1,0:T(8,128)(2,1)S(1)} %fusion), channel_id=1, source_target_pairs={{0,2},{1,3},{2,0},{3,1},{4,6},{5,7},{6,4},{7,5},{8,10},{9,11},{10,... | collective-permute-start | bytes 393224 | tf_op jit(solution)/shard_map/ppermute | solution.py:46
  28.7 4.0 %collective-permute-start.7 = (bf16[128,128]{1,0:T(8,128)(2,1)S(1)}, bf16[128,128]{1,0:T(8,128)(2,1)S(1)}, u32[]{:S(2)}, u32[]{:S(2)}) collective-permute-start(bf16[128,128]{1,0:T(8,128)(2,1)S(1)} %get-tuple-element.33), channel_id=1, source_target_pairs={{0,4},{1,5},{2,6},{3,7},{4,0},{5,1},{6,2},{7,3},{8,12},{9,13},{10,... | collective-permute-start | bytes 98312 | tf_op jit(solution)/shard_map/ppermute | solution.py:46
  29.2 5.7 %collective-permute-start.9 = (bf16[128,128]{1,0:T(8,128)(2,1)S(1)}, bf16[128,128]{1,0:T(8,128)(2,1)S(1)}, u32[]{:S(2)}, u32[]{:S(2)}) collective-permute-start(bf16[128,128]{1,0:T(8,128)(2,1)S(1)} %get-tuple-element.34), channel_id=1, source_target_pairs={{0,12},{1,13},{2,14},{3,15},{4,8},{5,9},{6,10},{7,11},{8,4},{9,5},... | collective-permute-start | bytes 98312 | tf_op jit(solution)/shard_map/ppermute | solution.py:46
  31.9 4.8 %collective-permute-start.8 = (bf16[128,128]{1,0:T(8,128)(2,1)S(1)}, bf16[128,128]{1,0:T(8,128)(2,1)S(1)}, u32[]{:S(2)}, u32[]{:S(2)}) collective-permute-start(bf16[128,128]{1,0:T(8,128)(2,1)S(1)} %get-tuple-element.35), channel_id=1, source_target_pairs={{0,8},{1,9},{2,10},{3,11},{4,12},{5,13},{6,14},{7,15},{8,0},{9,1},... | collective-permute-start | bytes 98312 | tf_op jit(solution)/shard_map/ppermute | solution.py:46

commit v6 on v5

--- a/solution.py
+++ b/solution.py
@@ -46,9 +46,8 @@
     return lax.ppermute(x, "ops", [(i, i ^ apart) for i in range(OPS)])
 
 
-def place(sector, me):
-    near = sector ^ me
-    return (near >> 2) | ((near & 2) << 1) | ((near & 1) << 3)
+def place(near, along_z):
+    return (along_z >> 2) | ((near & 2) << 1) | ((near & 1) << 3)
 
 
 def order_kernel(nops, coup_ref, out_ref):
@@ -58,8 +57,8 @@
 
     g = coup_ref[0:1, :]
     alive = iota((1, slots), 1) < coup_ref[3:4, :]
-    cell = jnp.where(alive, place(coup_ref[2:3, :], me) * nops + g, cells)
-    block = place(coup_ref[1:2, :], me) * nops + g
+    cell = jnp.where(alive, place(coup_ref[2:3, :] ^ me, coup_ref[2:3, :]) * nops + g, cells)
+    block = place(coup_ref[1:2, :] ^ me, coup_ref[1:2, :] ^ me) * nops + g
     cell_col = as_column(cell)
     block_col = as_column(block)
     square = (slots, slots)
@@ -322,15 +321,13 @@
     slots = couplings.shape[1]
     came = [exchange(psi, apart) for apart in ALONG_Z]
     psi, left = hold(psi, left_ops)
+    four, left = lax.optimization_barrier((jnp.concatenate([psi, *came], axis=0), left))
+    came = exchange(four, ALONG_X)
     order = order_slots(left_ops.shape[0], couplings, live)
-    four, left, order = lax.optimization_barrier(
-        (jnp.concatenate([psi, *came], axis=0), left, order)
-    )
-    came = exchange(four, ALONG_X)
     blocks = early(four, left, slots)
     turned = turn(right_ops)
-    eight, turned, blocks = lax.optimization_barrier(
-        (jnp.concatenate([four, came], axis=0), turned, blocks)
+    eight, order, turned, blocks = lax.optimization_barrier(
+        (jnp.concatenate([four, came], axis=0), order, turned, blocks)
     )
     far = exchange(eight, OTHER_CORE)
     blocks = more(came, left, blocks, 4)
@@ -340,10 +337,11 @@
     arrived = exchange((next_four + came[4:]).astype(jnp.bfloat16), ALONG_X)
     _, last_four = terms(order, turned, blocks, 2, 0, 4)
     total = last_four + came[:4] + arrived.astype(jnp.float32)
-    parts = [
-        exchange(total[k + 1].astype(jnp.bfloat16), apart) for k, apart in enumerate(ALONG_Z)
-    ]
-    return sum((part.astype(jnp.float32) for part in parts), total[0])[None]
+    same_line = [[z * 4 + i for z in range(4)] for i in range(4)]
+    parts = lax.all_to_all(
+        total.astype(jnp.bfloat16), "ops", 0, 0, axis_index_groups=same_line, tiled=True
+    )
+    return jnp.sum(parts.astype(jnp.float32), axis=0, keepdims=True)
 
 
 def shards_large(psi, left_ops, right_ops, couplings, live):

time: 37.3 us -> 38.7 us (1.038)
  blocking collectives: 0 us -> 8.46 us
  starting transfers between devices: 12.8 us -> 8.38 us
  waiting for transfers between devices: 10.8 us -> 7.18 us
  Pallas kernels: 8.69 us -> 9.5 us
    all_to_all x0 -> x1, blocking collectives: none -> 8.46 us  [shards_small(): lax.all_to_all(total.astype(jnp.bfloat16), 'ops', 0, 0, axis_index_groups...]
    ppermute x10 -> x7, starting transfers between devices: 12.8 us -> 8.38 us  [exchange(): return lax.ppermute(x, 'ops', [(i, i ^ apart) for i in range(OPS)])]
    ppermute x10 -> x7, waiting for transfers between devices: 10.8 us -> 7.18 us  [exchange(): return lax.ppermute(x, 'ops', [(i, i ^ apart) for i in range(OPS)])]
    pallas_call x3, Pallas kernels: 6.46 us -> 7.27 us  [terms(): pl.pallas_call(kernel, out_shape=[jax.ShapeDtypeStruct(blocks.shape, bloc...]
    reduce_sum x0 -> x1, other arithmetic: none -> 0.65 us  [shards_small(): return jnp.sum(parts.astype(jnp.float32), axis=0, keepdims=True)]
    broadcast_in_dim x1 -> x0, other arithmetic: 0.65 us -> none  [shards_small(): return sum((part.astype(jnp.float32) for part in parts), total[0])[None]]
  transfers between devices with their start and end apart: 10 -> 7, of which waited for: 8 -> 4; matrix products, arithmetic and copies ran while one was open for 2% -> 2% of each run, Pallas kernels for 15% -> 15%
where the time goes in v6:
time: 38.7 us; the launch traced here: 38.6 us
  Pallas kernels  9.5 us (25%)
  blocking collectives  8.46 us (22%)
  starting transfers between devices  8.38 us (22%)
  waiting for transfers between devices  7.18 us (19%)
  local copies, waits for them, and re-layouts  3.53 us (9%)
  between operations  0.79 us (2%)
  other arithmetic  0.76 us (2%)
    all_to_all x1, blocking collectives, shards_small(): lax.all_to_all(total.astype(jnp.bfloat16), 'ops', 0, 0, axis_index_groups...  8.46 us
    ppermute x7, starting transfers between devices, exchange(): return lax.ppermute(x, 'ops', [(i, i ^ apart) for i in range(OPS)])  8.38 us
    pallas_call x3, Pallas kernels, terms(): pl.pallas_call(kernel, out_shape=[jax.ShapeDtypeStruct(blocks.shape, bloc...  7.27 us
    ppermute x7, waiting for transfers between devices, exchange(): return lax.ppermute(x, 'ops', [(i, i ^ apart) for i in range(OPS)])  7.18 us
    unnamed x6, local copies, waits for them, and re-layouts  2.84 us
  transfers between devices with their start and end apart: 7, of which 4 were waited for; matrix products, arithmetic and copies ran while one was open for 2% of the time, Pallas kernels for 15%

profile of v6, /device:TPU:0, one launch (start us, length us, event | category | flops | bytes accessed | tf_op | source)
XLA Modules:
  0.0 38.6 jit_solution(18126600690122452488)
XLA Ops:
  0.0 3.0 %collective-permute-start = (bf16[1,128,128]{2,1,0:T(8,128)(2,1)}, bf16[1,128,128]{2,1,0:T(8,128)(2,1)S(1)}, u32[]{:S(2)}, u32[]{:S(2)}) collective-permute-start(bf16[1,128,128]{2,1,0:T(8,128)(2,1)} %psi_ref.1), channel_id=1, source_target_pairs={{0,4},{1,5},{2,6},{3,7},{4,0},{5,1},{6,2},{7,3},{8,12},{9,13},{10,... | collective-permute-start | bytes 98312 | tf_op jit(solution)/shard_map/ppermute | solution.py:46
  3.0 2.5 %collective-permute-start.2 = (bf16[1,128,128]{2,1,0:T(8,128)(2,1)}, bf16[1,128,128]{2,1,0:T(8,128)(2,1)S(1)}, u32[]{:S(2)}, u32[]{:S(2)}) collective-permute-start(bf16[1,128,128]{2,1,0:T(8,128)(2,1)} %psi_ref.1), channel_id=1, source_target_pairs={{0,12},{1,13},{2,14},{3,15},{4,8},{5,9},{6,10},{7,11},{8,4},{9,5},... | collective-permute-start | bytes 98312 | tf_op jit(solution)/shard_map/ppermute | solution.py:46
  5.5 0.1 collective-permute-start.1
  5.6 0.0 copy-start
  5.6 1.0 %copy-done = bf16[16,128,128]{2,1,0:T(8,128)(2,1)S(1)} copy-done((bf16[16,128,128]{2,1,0:T(8,128)(2,1)S(1)}, bf16[16,128,128]{2,1,0:T(8,128)(2,1)}, u32[]{:S(2)}) %copy-start) | copy-done | bytes 524312
  6.7 0.0 copy-start.2
  6.7 0.8 %copy-done.2 = bf16[1,128,128]{2,1,0:T(8,128)(2,1)S(1)} copy-done((bf16[1,128,128]{2,1,0:T(8,128)(2,1)S(1)}, bf16[1,128,128]{2,1,0:T(8,128)(2,1)}, u32[]{:S(2)}) %copy-start.2) | copy-done | bytes 32792
  7.5 0.0 collective-permute-done
  7.5 1.9 %collective-permute-done.2 = bf16[1,128,128]{2,1,0:T(8,128)(2,1)S(1)} collective-permute-done((bf16[1,128,128]{2,1,0:T(8,128)(2,1)}, bf16[1,128,128]{2,1,0:T(8,128)(2,1)S(1)}, u32[]{:S(2)}, u32[]{:S(2)}) %collective-permute-start.2) | collective-permute-done | bytes 32800 | tf_op jit(solution)/shard_map/ppermute | solution.py:46
  9.4 1.5 %collective-permute-done.1 = bf16[1,128,128]{2,1,0:T(8,128)(2,1)S(1)} collective-permute-done((bf16[1,128,128]{2,1,0:T(8,128)(2,1)}, bf16[1,128,128]{2,1,0:T(8,128)(2,1)S(1)}, u32[]{:S(2)}, u32[]{:S(2)}) %collective-permute-start.1) | collective-permute-done | bytes 32800 | tf_op jit(solution)/shard_map/ppermute | solution.py:46
  10.9 1.6 %collective-permute-start.3 = (bf16[4,128,128]{2,1,0:T(8,128)(2,1)S(1)}, bf16[4,128,128]{2,1,0:T(8,128)(2,1)S(1)}, u32[]{:S(2)}, u32[]{:S(2)}) collective-permute-start(bf16[4,128,128]{2,1,0:T(8,128)(2,1)S(1)} %pad_maximum_fusion.1.psi_ref), channel_id=1, source_target_pairs={{0,2},{1,3},{2,0},{3,1},{4,6},{5,7},{6,4},{7,5},{8,10},{9,11},{10,... | collective-permute-start | bytes 393224 | tf_op jit(solution)/shard_map/ppermute | solution.py:46
  13.1 0.0 copy-start.1
  13.1 1.0 %copy-done.1 = bf16[16,128,128]{2,1,0:T(8,128)(2,1)S(1)} copy-done((bf16[16,128,128]{2,1,0:T(8,128)(2,1)S(1)}, bf16[16,128,128]{2,1,0:T(8,128)(2,1)}, u32[]{:S(2)}) %copy-start.1) | copy-done | bytes 524312
  14.2 0.2 turn.1.turned_ref
  14.3 0.7 %concatenate.11.refs_0_ = s32[4,384]{1,0:T(4,128)S(1)} pad(s32[3,384]{1,0:T(4,128)} %param.8, s32[]{:T(128)} %bitcast.2), padding=0_1x0_0 | pad | bytes 10756 | tf_op jit(solution)/shard_map/concatenate | solution.py:103
  15.0 0.6 %order.1.order_in = s32[1,1024]{1,0:T(1,128)S(1)} custom-call(s32[4,384]{1,0:T(4,128)S(1)} %concatenate.11.refs_0_), custom_call_target="tpu_custom_call" | custom-call | flops 2949120 | bytes 1048576 | tf_op jit(solution)/shard_map/order/pallas_call | solution.py:104
  15.7 0.7 %early.1._ = bf16[449,128,128]{2,1,0:T(8,128)(2,1)S(1)} custom-call(bf16[4,128,128]{2,1,0:T(8,128)(2,1)S(1)} %pad_maximum_fusion.1.psi_ref, bf16[16,128,128]{2,1,0:T(8,128)(2,1)S(1)} %get-tuple-element.21.left_ref.refs_1_), custom_call_target="tpu_custom_call" | custom-call | flops 268435456 | bytes 1048576 | tf_op jit(solution)/shard_map/early/pallas_call | solution.py:232
  16.4 0.0 collective-permute-done.3.psi_ref
  16.4 0.1 collective-permute-start.4
  16.5 0.7 %more.1.refs_2_ = bf16[449,128,128]{2,1,0:T(8,128)(2,1)S(1)} custom-call(bf16[4,128,128]{2,1,0:T(8,128)(2,1)S(1)} %collective-permute-done.3.psi_ref, bf16[16,128,128]{2,1,0:T(8,128)(2,1)S(1)} %get-tuple-element.21.left_ref.refs_1_, bf16[449,128,128]{2,1,0:T(8,128)(2,1)S(1)} %early.1._), custom_call_target="tpu_custom_call", output_to_operand_aliasing={{}: (2, {})} | custom-call | flops 268435456 | bytes 1048576 | tf_op jit(solution)/shard_map/more/pallas_call | solution.py:249
  17.2 0.8 %collective-permute-done.4.refs_0_ = bf16[8,128,128]{2,1,0:T(8,128)(2,1)S(1)} collective-permute-done((bf16[8,128,128]{2,1,0:T(8,128)(2,1)S(1)}, bf16[8,128,128]{2,1,0:T(8,128)(2,1)S(1)}, u32[]{:S(2)}, u32[]{:S(2)}) %collective-permute-start.4) | collective-permute-done | bytes 262176 | tf_op jit(solution)/shard_map/ppermute | solution.py:46
  18.0 3.5 %terms_0.1 = (bf16[449,128,128]{2,1,0:T(8,128)(2,1)S(1)}, f32[8,128,128]{2,1,0:T(8,128)S(1)}) custom-call(s32[1,1024]{1,0:T(1,128)S(1)} %order.1.order_in, bf16[2048,128]{1,0:T(8,128)(2,1)S(1)} %turn.1.turned_ref, bf16[8,128,128]{2,1,0:T(8,128)(2,1)S(1)} %collective-permute-done.4.refs_0_, ...), custom_call_target="tpu_custom_call", output_to_operand_aliasing={{0}: (4, {})} | custom-call | flops 1073741824 | bytes 1048576 | tf_op jit(solution)/shard_map/terms_0/pallas_call | solution.py:283
  21.6 0.1 collective-permute-start.5
  21.6 2.0 %terms_1.1 = (bf16[449,128,128]{2,1,0:T(8,128)(2,1)S(1)}, f32[4,128,128]{2,1,0:T(8,128)S(1)}) custom-call(s32[1,1024]{1,0:T(1,128)S(1)} %order.1.order_in, bf16[2048,128]{1,0:T(8,128)(2,1)S(1)} %turn.1.turned_ref, bf16[449,128,128]{2,1,0:T(8,128)(2,1)S(1)} %get-tuple-element.26.refs_0_), custom_call_target="tpu_custom_call", output_to_operand_aliasing={{0}: (2, {})} | custom-call | flops 268435456 | bytes 1048576 | tf_op jit(solution)/shard_map/terms_1/pallas_call | solution.py:283
  23.6 0.0 collective-permute-done.5
  23.7 1.1 %collective-permute-start.6 = (bf16[4,128,128]{2,1,0:T(8,128)(2,1)S(1)}, bf16[4,128,128]{2,1,0:T(8,128)(2,1)S(1)}, u32[]{:S(2)}, u32[]{:S(2)}) collective-permute-start(bf16[4,128,128]{2,1,0:T(8,128)(2,1)S(1)} %fusion), channel_id=1, source_target_pairs={{0,2},{1,3},{2,0},{3,1},{4,6},{5,7},{6,4},{7,5},{8,10},{9,11},{10,... | collective-permute-start | bytes 393224 | tf_op jit(solution)/shard_map/ppermute | solution.py:46
  24.7 1.8 %terms_2.1 = (bf16[449,128,128]{2,1,0:T(8,128)(2,1)S(1)}, f32[4,128,128]{2,1,0:T(8,128)S(1)}) custom-call(s32[1,1024]{1,0:T(1,128)S(1)} %order.1.order_in, bf16[2048,128]{1,0:T(8,128)(2,1)S(1)} %turn.1.turned_ref, bf16[449,128,128]{2,1,0:T(8,128)(2,1)S(1)} %get-tuple-element.27.refs_0_), custom_call_target="tpu_custom_call", output_to_operand_aliasing={{0}: (2, {})} | custom-call | flops 268435456 | bytes 1048576 | tf_op jit(solution)/shard_map/terms_2/pallas_call | solution.py:283
  26.5 2.9 %collective-permute-done.6 = bf16[4,128,128]{2,1,0:T(8,128)(2,1)S(1)} collective-permute-done((bf16[4,128,128]{2,1,0:T(8,128)(2,1)S(1)}, bf16[4,128,128]{2,1,0:T(8,128)(2,1)S(1)}, u32[]{:S(2)}, u32[]{:S(2)}) %collective-permute-start.6) | collective-permute-done | bytes 131104 | tf_op jit(solution)/shard_map/ppermute | solution.py:46
  29.5 8.5 %all_to_all.5 = bf16[4,128,128]{2,1,0:T(8,128)(2,1)S(1)} all-to-all(bf16[4,128,128]{2,1,0:T(8,128)(2,1)S(1)} %fusion.2), channel_id=1, replica_groups={{0,4,8,12},{1,5,9,13},{2,6,10,14},{3,7,11,15},{16,20,24,28},{17,21,25,2..., dimensions={0} | all-to-all | bytes 262144 | tf_op jit(solution)/shard_map/all_to_all | solution.py:341
  38.0 0.6 %convert_reduce_fusion = f32[128,128]{1,0:T(8,128)} fusion(bf16[4,128,128]{2,1,0:T(8,128)(2,1)S(1)} %all_to_all.5), kind=kLoop, calls=%fused_computation.6 | loop fusion | flops 114688 | bytes 196608 | tf_op jit(solution)/shard_map/reduce_sum | solution.py:344
  (5 shorter events, 0.2 us)
Async XLA Ops:
  0.0 7.5 %collective-permute-start = (bf16[1,128,128]{2,1,0:T(8,128)(2,1)}, bf16[1,128,128]{2,1,0:T(8,128)(2,1)S(1)}, u32[]{:S(2)}, u32[]{:S(2)}) collective-permute-start(bf16[1,128,128]{2,1,0:T(8,128)(2,1)} %psi_ref.1), channel_id=1, source_target_pairs={{0,4},{1,5},{2,6},{3,7},{4,0},{5,1},{6,2},{7,3},{8,12},{9,13},{10,... | collective-permute-start | bytes 98312 | tf_op jit(solution)/shard_map/ppermute | solution.py:46
  3.0 6.4 %collective-permute-start.2 = (bf16[1,128,128]{2,1,0:T(8,128)(2,1)}, bf16[1,128,128]{2,1,0:T(8,128)(2,1)S(1)}, u32[]{:S(2)}, u32[]{:S(2)}) collective-permute-start(bf16[1,128,128]{2,1,0:T(8,128)(2,1)} %psi_ref.1), channel_id=1, source_target_pairs={{0,12},{1,13},{2,14},{3,15},{4,8},{5,9},{6,10},{7,11},{8,4},{9,5},... | collective-permute-start | bytes 98312 | tf_op jit(solution)/shard_map/ppermute | solution.py:46
  5.5 5.4 %collective-permute-start.1 = (bf16[1,128,128]{2,1,0:T(8,128)(2,1)}, bf16[1,128,128]{2,1,0:T(8,128)(2,1)S(1)}, u32[]{:S(2)}, u32[]{:S(2)}) collective-permute-start(bf16[1,128,128]{2,1,0:T(8,128)(2,1)} %psi_ref.1), channel_id=1, source_target_pairs={{0,8},{1,9},{2,10},{3,11},{4,12},{5,13},{6,14},{7,15},{8,0},{9,1},... | collective-permute-start | bytes 98312 | tf_op jit(solution)/shard_map/ppermute | solution.py:46
  5.6 1.0 %copy-start = (bf16[16,128,128]{2,1,0:T(8,128)(2,1)S(1)}, bf16[16,128,128]{2,1,0:T(8,128)(2,1)}, u32[]{:S(2)}) copy-start(bf16[16,128,128]{2,1,0:T(8,128)(2,1)} %left_ref.1) | copy-start | bytes 1572868
  6.7 0.8 %copy-start.2 = (bf16[1,128,128]{2,1,0:T(8,128)(2,1)S(1)}, bf16[1,128,128]{2,1,0:T(8,128)(2,1)}, u32[]{:S(2)}) copy-start(bf16[1,128,128]{2,1,0:T(8,128)(2,1)} %psi_ref.1) | copy-start | bytes 98308
  10.9 5.5 %collective-permute-start.3 = (bf16[4,128,128]{2,1,0:T(8,128)(2,1)S(1)}, bf16[4,128,128]{2,1,0:T(8,128)(2,1)S(1)}, u32[]{:S(2)}, u32[]{:S(2)}) collective-permute-start(bf16[4,128,128]{2,1,0:T(8,128)(2,1)S(1)} %pad_maximum_fusion.1.psi_ref), channel_id=1, source_target_pairs={{0,2},{1,3},{2,0},{3,1},{4,6},{5,7},{6,4},{7,5},{8,10},{9,11},{10,... | collective-permute-start | bytes 393224 | tf_op jit(solution)/shard_map/ppermute | solution.py:46
  13.1 1.0 %copy-start.1 = (bf16[16,128,128]{2,1,0:T(8,128)(2,1)S(1)}, bf16[16,128,128]{2,1,0:T(8,128)(2,1)}, u32[]{:S(2)}) copy-start(bf16[16,128,128]{2,1,0:T(8,128)(2,1)} %right_ref.1) | copy-start | bytes 1572868
  16.4 1.6 %collective-permute-start.4 = (bf16[8,128,128]{2,1,0:T(8,128)(2,1)S(1)}, bf16[8,128,128]{2,1,0:T(8,128)(2,1)S(1)}, u32[]{:S(2)}, u32[]{:S(2)}) collective-permute-start(bf16[8,128,128]{2,1,0:T(8,128)(2,1)S(1)} %pad_maximum_fusion), channel_id=1, source_target_pairs={{0,1},{1,0},{2,3},{3,2},{4,5},{5,4},{6,7},{7,6},{8,9},{9,8},{10,11... | collective-permute-start | bytes 786440 | tf_op jit(solution)/shard_map/ppermute | solution.py:46
  21.6 2.1 %collective-permute-start.5 = (f32[8,128,128]{2,1,0:T(8,128)S(1)}, f32[8,128,128]{2,1,0:T(8,128)S(1)}, u32[]{:S(2)}, u32[]{:S(2)}) collective-permute-start(f32[8,128,128]{2,1,0:T(8,128)S(1)} %get-tuple-element.29), channel_id=1, source_target_pairs={{0,1},{1,0},{2,3},{3,2},{4,5},{5,4},{6,7},{7,6},{8,9},{9,8},{10,11... | collective-permute-start | bytes 1572872 | tf_op jit(solution)/shard_map/ppermute | solution.py:46
  23.7 5.8 %collective-permute-start.6 = (bf16[4,128,128]{2,1,0:T(8,128)(2,1)S(1)}, bf16[4,128,128]{2,1,0:T(8,128)(2,1)S(1)}, u32[]{:S(2)}, u32[]{:S(2)}) collective-permute-start(bf16[4,128,128]{2,1,0:T(8,128)(2,1)S(1)} %fusion), channel_id=1, source_target_pairs={{0,2},{1,3},{2,0},{3,1},{4,6},{5,7},{6,4},{7,5},{8,10},{9,11},{10,... | collective-permute-start | bytes 393224 | tf_op jit(solution)/shard_map/ppermute | solution.py:46

commit v7 on v5

--- a/solution.py
+++ b/solution.py
@@ -36,7 +36,7 @@
     return picked(iota((n, n), 0) == iota((n, n), 1), row, 1)
 
 
-ALONG_Z = (4, 8, 12)
+ALONG_Z = (12, 4, 8)
 ALONG_X = 2
 OTHER_CORE = 1
 OPS = 16
@@ -161,25 +161,35 @@
     def _(k):
         first, number = cell(k)
 
-        def add(j, total):
-            return total + block_ref[order(BLOCKS + first + j)].astype(jnp.float32)
-
-        total = lax.fori_loop(0, number, add, jnp.zeros((m, m), jnp.float32))
+        def add(i, total):
+            at = first + i * 4
+            for j in range(4):
+                block = jnp.where(i * 4 + j < number, order(BLOCKS + at + j), cells)
+                total = total + block_ref[block].astype(jnp.float32)
+            return total
+
+        chunks = (number + 3) >> 2
+        total = lax.fori_loop(0, chunks, add, jnp.zeros((m, m), jnp.float32))
         block_ref[cells + 1 + k] = total.astype(jnp.bfloat16)
 
-    @pl.loop(many, some)
+    @pl.loop(many, some, step=2)
     def _(k):
-        first, number = cell(k)
-        fourth = jnp.where(number == 4, order(BLOCKS + first + 3), cells)
-        total = block_ref[order(BLOCKS + first)].astype(jnp.float32)
-        total += block_ref[order(BLOCKS + first + 1)].astype(jnp.float32)
-        total += block_ref[order(BLOCKS + first + 2)].astype(jnp.float32)
-        total += block_ref[fourth].astype(jnp.float32)
-        block_ref[cells + 1 + k] = total.astype(jnp.bfloat16)
-
-    @pl.loop(some, two, step=2)
+        ks = (k, jnp.minimum(k + 1, some - 1))
+        totals = []
+        for k in ks:
+            first, number = cell(k)
+            fourth = jnp.where(number == 4, order(BLOCKS + first + 3), cells)
+            total = block_ref[order(BLOCKS + first)].astype(jnp.float32)
+            total += block_ref[order(BLOCKS + first + 1)].astype(jnp.float32)
+            total += block_ref[order(BLOCKS + first + 2)].astype(jnp.float32)
+            total += block_ref[fourth].astype(jnp.float32)
+            totals.append(total.astype(jnp.bfloat16))
+        for k, total in zip(ks, totals):
+            block_ref[cells + 1 + k] = total
+
+    @pl.loop(some, two, step=4)
     def _(k):
-        ks = (k, jnp.minimum(k + 1, two - 1))
+        ks = [jnp.minimum(k + i, two - 1) for i in range(4)]
         firsts = [cell(k)[0] for k in ks]
         totals = [
             block_ref[order(BLOCKS + first)] + block_ref[order(BLOCKS + first + 1)]
@@ -320,11 +330,11 @@
 
 def shards_small(psi, left_ops, right_ops, couplings, live):
     slots = couplings.shape[1]
-    came = [exchange(psi, apart) for apart in ALONG_Z]
+    came = {apart: exchange(psi, apart) for apart in ALONG_Z}
     psi, left = hold(psi, left_ops)
     order = order_slots(left_ops.shape[0], couplings, live)
     four, left, order = lax.optimization_barrier(
-        (jnp.concatenate([psi, *came], axis=0), left, order)
+        (jnp.concatenate([psi, came[4], came[8], came[12]], axis=0), left, order)
     )
     came = exchange(four, ALONG_X)
     blocks = early(four, left, slots)
@@ -341,7 +351,7 @@
     _, last_four = terms(order, turned, blocks, 2, 0, 4)
     total = last_four + came[:4] + arrived.astype(jnp.float32)
     parts = [
-        exchange(total[k + 1].astype(jnp.bfloat16), apart) for k, apart in enumerate(ALONG_Z)
+        exchange(total[apart // 4].astype(jnp.bfloat16), apart) for apart in ALONG_Z
     ]
     return sum((part.astype(jnp.float32) for part in parts), total[0])[None]
 

time: 37.3 us -> 36.3 us (0.973)
  waiting for transfers between devices: 10.8 us -> 9.01 us
  starting transfers between devices: 12.8 us -> 14.5 us
  Pallas kernels: 8.69 us -> 7.54 us
    ppermute x10, waiting for transfers between devices: 10.8 us -> 9.01 us  [exchange(): return lax.ppermute(x, 'ops', [(i, i ^ apart) for i in range(OPS)])]
    ppermute x10, starting transfers between devices: 12.8 us -> 14.5 us  [exchange(): return lax.ppermute(x, 'ops', [(i, i ^ apart) for i in range(OPS)])]
    pallas_call x3, Pallas kernels: 6.46 us -> 5.31 us  [terms(): pl.pallas_call(kernel, out_shape=[jax.ShapeDtypeStruct(blocks.shape, bloc...]
  transfers between devices with their start and end apart: 10 -> 10, of which waited for: 8 -> 7; matrix products, arithmetic and copies ran while one was open for 2% -> 2% of each run, Pallas kernels for 15% -> 14%
where the time goes in v7:
time: 36.3 us; the launch traced here: 36.1 us
  starting transfers between devices  14.5 us (40%)
  waiting for transfers between devices  9.01 us (25%)
  Pallas kernels  7.54 us (21%)
  local copies, waits for them, and re-layouts  3.54 us (10%)
  between operations  0.77 us (2%)
  other arithmetic  0.76 us (2%)
    ppermute x10, starting transfers between devices, exchange(): return lax.ppermute(x, 'ops', [(i, i ^ apart) for i in range(OPS)])  14.5 us
    ppermute x10, waiting for transfers between devices, exchange(): return lax.ppermute(x, 'ops', [(i, i ^ apart) for i in range(OPS)])  9.01 us
    pallas_call x3, Pallas kernels, terms(): pl.pallas_call(kernel, out_shape=[jax.ShapeDtypeStruct(blocks.shape, bloc...  5.31 us
    unnamed x6, local copies, waits for them, and re-layouts  2.83 us
  transfers between devices with their start and end apart: 10, of which 7 were waited for; matrix products, arithmetic and copies ran while one was open for 2% of the time, Pallas kernels for 14%

profile of v7, /device:TPU:0, one launch (start us, length us, event | category | flops | bytes accessed | tf_op | source)
XLA Modules:
  0.0 36.1 jit_solution(16483643314126561421)
XLA Ops:
  0.0 3.0 %collective-permute-start = (bf16[1,128,128]{2,1,0:T(8,128)(2,1)}, bf16[1,128,128]{2,1,0:T(8,128)(2,1)S(1)}, u32[]{:S(2)}, u32[]{:S(2)}) collective-permute-start(bf16[1,128,128]{2,1,0:T(8,128)(2,1)} %psi_ref.1), channel_id=1, source_target_pairs={{0,4},{1,5},{2,6},{3,7},{4,0},{5,1},{6,2},{7,3},{8,12},{9,13},{10,... | collective-permute-start | bytes 98312 | tf_op jit(solution)/shard_map/ppermute | solution.py:46
  3.0 2.5 %collective-permute-start.2 = (bf16[1,128,128]{2,1,0:T(8,128)(2,1)}, bf16[1,128,128]{2,1,0:T(8,128)(2,1)S(1)}, u32[]{:S(2)}, u32[]{:S(2)}) collective-permute-start(bf16[1,128,128]{2,1,0:T(8,128)(2,1)} %psi_ref.1), channel_id=1, source_target_pairs={{0,12},{1,13},{2,14},{3,15},{4,8},{5,9},{6,10},{7,11},{8,4},{9,5},... | collective-permute-start | bytes 98312 | tf_op jit(solution)/shard_map/ppermute | solution.py:46
  5.5 0.1 collective-permute-start.1
  6.3 1.0 %copy-done = bf16[16,128,128]{2,1,0:T(8,128)(2,1)S(1)} copy-done((bf16[16,128,128]{2,1,0:T(8,128)(2,1)S(1)}, bf16[16,128,128]{2,1,0:T(8,128)(2,1)}, u32[]{:S(2)}) %copy-start) | copy-done | bytes 524312
  7.3 0.8 %copy-done.2 = bf16[1,128,128]{2,1,0:T(8,128)(2,1)S(1)} copy-done((bf16[1,128,128]{2,1,0:T(8,128)(2,1)S(1)}, bf16[1,128,128]{2,1,0:T(8,128)(2,1)}, u32[]{:S(2)}) %copy-start.2) | copy-done | bytes 32792
  8.1 0.7 %concatenate.10.refs_0_ = s32[4,384]{1,0:T(4,128)S(1)} pad(s32[3,384]{1,0:T(4,128)} %param.8, s32[]{:T(128)} %bitcast.19), padding=0_1x0_0 | pad | bytes 10756 | tf_op jit(solution)/shard_map/concatenate | solution.py:104
  8.8 0.6 %order.1.order_in = s32[1,1024]{1,0:T(1,128)S(1)} custom-call(s32[4,384]{1,0:T(4,128)S(1)} %concatenate.10.refs_0_), custom_call_target="tpu_custom_call" | custom-call | flops 2949120 | bytes 1048576 | tf_op jit(solution)/shard_map/order/pallas_call | solution.py:105
  9.4 0.0 collective-permute-done
  9.5 0.0 collective-permute-done.2
  9.5 1.4 %collective-permute-done.1 = bf16[1,128,128]{2,1,0:T(8,128)(2,1)S(1)} collective-permute-done((bf16[1,128,128]{2,1,0:T(8,128)(2,1)}, bf16[1,128,128]{2,1,0:T(8,128)(2,1)S(1)}, u32[]{:S(2)}, u32[]{:S(2)}) %collective-permute-start.1) | collective-permute-done | bytes 32800 | tf_op jit(solution)/shard_map/ppermute | solution.py:46
  10.9 1.6 %collective-permute-start.3 = (bf16[4,128,128]{2,1,0:T(8,128)(2,1)S(1)}, bf16[4,128,128]{2,1,0:T(8,128)(2,1)S(1)}, u32[]{:S(2)}, u32[]{:S(2)}) collective-permute-start(bf16[4,128,128]{2,1,0:T(8,128)(2,1)S(1)} %pad_maximum_fusion.1.psi_ref), channel_id=1, source_target_pairs={{0,2},{1,3},{2,0},{3,1},{4,6},{5,7},{6,4},{7,5},{8,10},{9,11},{10,... | collective-permute-start | bytes 393224 | tf_op jit(solution)/shard_map/ppermute | solution.py:46
  12.5 1.0 %copy-done.1 = bf16[16,128,128]{2,1,0:T(8,128)(2,1)S(1)} copy-done((bf16[16,128,128]{2,1,0:T(8,128)(2,1)S(1)}, bf16[16,128,128]{2,1,0:T(8,128)(2,1)}, u32[]{:S(2)}) %copy-start.1) | copy-done | bytes 524312
  13.5 0.2 turn.1.turned_ref
  13.7 0.7 %early.1._ = bf16[449,128,128]{2,1,0:T(8,128)(2,1)S(1)} custom-call(bf16[4,128,128]{2,1,0:T(8,128)(2,1)S(1)} %pad_maximum_fusion.1.psi_ref, bf16[16,128,128]{2,1,0:T(8,128)(2,1)S(1)} %get-tuple-element.22.left_ref.refs_1_), custom_call_target="tpu_custom_call" | custom-call | flops 268435456 | bytes 1048576 | tf_op jit(solution)/shard_map/early/pallas_call | solution.py:243
  14.4 1.5 %collective-permute-done.3.psi_ref = bf16[4,128,128]{2,1,0:T(8,128)(2,1)S(1)} collective-permute-done((bf16[4,128,128]{2,1,0:T(8,128)(2,1)S(1)}, bf16[4,128,128]{2,1,0:T(8,128)(2,1)S(1)}, u32[]{:S(2)}, u32[]{:S(2)}) %collective-permute-start.3) | collective-permute-done | bytes 131104 | tf_op jit(solution)/shard_map/ppermute | solution.py:46
  16.0 0.1 collective-permute-start.4
  16.0 0.7 %more.1.refs_2_ = bf16[449,128,128]{2,1,0:T(8,128)(2,1)S(1)} custom-call(bf16[4,128,128]{2,1,0:T(8,128)(2,1)S(1)} %collective-permute-done.3.psi_ref, bf16[16,128,128]{2,1,0:T(8,128)(2,1)S(1)} %get-tuple-element.22.left_ref.refs_1_, bf16[449,128,128]{2,1,0:T(8,128)(2,1)S(1)} %early.1._), custom_call_target="tpu_custom_call", output_to_operand_aliasing={{}: (2, {})} | custom-call | flops 268435456 | bytes 1048576 | tf_op jit(solution)/shard_map/more/pallas_call | solution.py:260
  16.7 0.8 %collective-permute-done.4.refs_0_ = bf16[8,128,128]{2,1,0:T(8,128)(2,1)S(1)} collective-permute-done((bf16[8,128,128]{2,1,0:T(8,128)(2,1)S(1)}, bf16[8,128,128]{2,1,0:T(8,128)(2,1)S(1)}, u32[]{:S(2)}, u32[]{:S(2)}) %collective-permute-start.4) | collective-permute-done | bytes 262176 | tf_op jit(solution)/shard_map/ppermute | solution.py:46
  17.6 2.6 %terms_0.1 = (bf16[449,128,128]{2,1,0:T(8,128)(2,1)S(1)}, f32[8,128,128]{2,1,0:T(8,128)S(1)}) custom-call(s32[1,1024]{1,0:T(1,128)S(1)} %order.1.order_in, bf16[2048,128]{1,0:T(8,128)(2,1)S(1)} %turn.1.turned_ref, bf16[8,128,128]{2,1,0:T(8,128)(2,1)S(1)} %collective-permute-done.4.refs_0_, ...), custom_call_target="tpu_custom_call", output_to_operand_aliasing={{0}: (4, {})} | custom-call | flops 1073741824 | bytes 1048576 | tf_op jit(solution)/shard_map/terms_0/pallas_call | solution.py:294
  20.1 1.2 %collective-permute-start.5 = (f32[8,128,128]{2,1,0:T(8,128)S(1)}, f32[8,128,128]{2,1,0:T(8,128)S(1)}, u32[]{:S(2)}, u32[]{:S(2)}) collective-permute-start(f32[8,128,128]{2,1,0:T(8,128)S(1)} %get-tuple-element.29), channel_id=1, source_target_pairs={{0,1},{1,0},{2,3},{3,2},{4,5},{5,4},{6,7},{7,6},{8,9},{9,8},{10,11... | collective-permute-start | bytes 1572872 | tf_op jit(solution)/shard_map/ppermute | solution.py:46
  21.3 1.4 %terms_1.1 = (bf16[449,128,128]{2,1,0:T(8,128)(2,1)S(1)}, f32[4,128,128]{2,1,0:T(8,128)S(1)}) custom-call(s32[1,1024]{1,0:T(1,128)S(1)} %order.1.order_in, bf16[2048,128]{1,0:T(8,128)(2,1)S(1)} %turn.1.turned_ref, bf16[449,128,128]{2,1,0:T(8,128)(2,1)S(1)} %get-tuple-element.26.refs_0_), custom_call_target="tpu_custom_call", output_to_operand_aliasing={{0}: (2, {})} | custom-call | flops 268435456 | bytes 1048576 | tf_op jit(solution)/shard_map/terms_1/pallas_call | solution.py:294
  22.7 0.2 collective-permute-done.5
  22.9 1.6 %collective-permute-start.6 = (bf16[4,128,128]{2,1,0:T(8,128)(2,1)S(1)}, bf16[4,128,128]{2,1,0:T(8,128)(2,1)S(1)}, u32[]{:S(2)}, u32[]{:S(2)}) collective-permute-start(bf16[4,128,128]{2,1,0:T(8,128)(2,1)S(1)} %fusion), channel_id=1, source_target_pairs={{0,2},{1,3},{2,0},{3,1},{4,6},{5,7},{6,4},{7,5},{8,10},{9,11},{10,... | collective-permute-start | bytes 393224 | tf_op jit(solution)/shard_map/ppermute | solution.py:46
  24.5 1.4 %terms_2.1 = (bf16[449,128,128]{2,1,0:T(8,128)(2,1)S(1)}, f32[4,128,128]{2,1,0:T(8,128)S(1)}) custom-call(s32[1,1024]{1,0:T(1,128)S(1)} %order.1.order_in, bf16[2048,128]{1,0:T(8,128)(2,1)S(1)} %turn.1.turned_ref, bf16[449,128,128]{2,1,0:T(8,128)(2,1)S(1)} %get-tuple-element.27.refs_0_), custom_call_target="tpu_custom_call", output_to_operand_aliasing={{0}: (2, {})} | custom-call | flops 268435456 | bytes 1048576 | tf_op jit(solution)/shard_map/terms_2/pallas_call | solution.py:294
  25.9 2.8 %collective-permute-done.6 = bf16[4,128,128]{2,1,0:T(8,128)(2,1)S(1)} collective-permute-done((bf16[4,128,128]{2,1,0:T(8,128)(2,1)S(1)}, bf16[4,128,128]{2,1,0:T(8,128)(2,1)S(1)}, u32[]{:S(2)}, u32[]{:S(2)}) %collective-permute-start.6) | collective-permute-done | bytes 131104 | tf_op jit(solution)/shard_map/ppermute | solution.py:46
  28.8 1.4 %collective-permute-start.7 = (bf16[128,128]{1,0:T(8,128)(2,1)S(1)}, bf16[128,128]{1,0:T(8,128)(2,1)S(1)}, u32[]{:S(2)}, u32[]{:S(2)}) collective-permute-start(bf16[128,128]{1,0:T(8,128)(2,1)S(1)} %get-tuple-element.33), channel_id=1, source_target_pairs={{0,12},{1,13},{2,14},{3,15},{4,8},{5,9},{6,10},{7,11},{8,4},{9,5},... | collective-permute-start | bytes 98312 | tf_op jit(solution)/shard_map/ppermute | solution.py:46
  30.2 0.4 %collective-permute-start.9 = (bf16[128,128]{1,0:T(8,128)(2,1)S(1)}, bf16[128,128]{1,0:T(8,128)(2,1)S(1)}, u32[]{:S(2)}, u32[]{:S(2)}) collective-permute-start(bf16[128,128]{1,0:T(8,128)(2,1)S(1)} %get-tuple-element.34), channel_id=1, source_target_pairs={{0,8},{1,9},{2,10},{3,11},{4,12},{5,13},{6,14},{7,15},{8,0},{9,1},... | collective-permute-start | bytes 98312 | tf_op jit(solution)/shard_map/ppermute | solution.py:46
  30.7 2.6 %collective-permute-start.8 = (bf16[128,128]{1,0:T(8,128)(2,1)S(1)}, bf16[128,128]{1,0:T(8,128)(2,1)S(1)}, u32[]{:S(2)}, u32[]{:S(2)}) collective-permute-start(bf16[128,128]{1,0:T(8,128)(2,1)S(1)} %get-tuple-element.35), channel_id=1, source_target_pairs={{0,4},{1,5},{2,6},{3,7},{4,0},{5,1},{6,2},{7,3},{8,12},{9,13},{10,... | collective-permute-start | bytes 98312 | tf_op jit(solution)/shard_map/ppermute | solution.py:46
  33.2 1.6 %collective-permute-done.7 = bf16[128,128]{1,0:T(8,128)(2,1)S(1)} collective-permute-done((bf16[128,128]{1,0:T(8,128)(2,1)S(1)}, bf16[128,128]{1,0:T(8,128)(2,1)S(1)}, u32[]{:S(2)}, u32[]{:S(2)}) %collective-permute-start.7) | collective-permute-done | bytes 32800 | tf_op jit(solution)/shard_map/ppermute | solution.py:46
  34.8 0.7 %collective-permute-done.9 = bf16[128,128]{1,0:T(8,128)(2,1)S(1)} collective-permute-done((bf16[128,128]{1,0:T(8,128)(2,1)S(1)}, bf16[128,128]{1,0:T(8,128)(2,1)S(1)}, u32[]{:S(2)}, u32[]{:S(2)}) %collective-permute-start.9) | collective-permute-done | bytes 32800 | tf_op jit(solution)/shard_map/ppermute | solution.py:46
  35.5 0.0 collective-permute-done.8
  35.5 0.6 %fusion.5 = f32[1,128,128]{2,1,0:T(8,128)} fusion(f32[4,128,128]{2,1,0:T(8,128)S(1)} %get-tuple-element.32, bf16[128,128]{1,0:T(8,128)(2,1)S(1)} %collective-permute-done.9, bf16[128,128]{1,0:T(8,128)(2,1)S(1)} %collective-permute-done.8, bf16[128,128]{1,0:T(8,128)(2,1)S(1)} %collective-permute-done.7), kind=kLoop, calls=%fused_computation.10 | loop fusion | flops 98304 | bytes 229376 | tf_op jit(solution)/shard_map/broadcast_in_dim | solution.py:356
  (9 shorter events, 0.2 us)
Async XLA Ops:
  0.0 9.4 %collective-permute-start = (bf16[1,128,128]{2,1,0:T(8,128)(2,1)}, bf16[1,128,128]{2,1,0:T(8,128)(2,1)S(1)}, u32[]{:S(2)}, u32[]{:S(2)}) collective-permute-start(bf16[1,128,128]{2,1,0:T(8,128)(2,1)} %psi_ref.1), channel_id=1, source_target_pairs={{0,4},{1,5},{2,6},{3,7},{4,0},{5,1},{6,2},{7,3},{8,12},{9,13},{10,... | collective-permute-start | bytes 98312 | tf_op jit(solution)/shard_map/ppermute | solution.py:46
  3.0 6.4 %collective-permute-start.2 = (bf16[1,128,128]{2,1,0:T(8,128)(2,1)}, bf16[1,128,128]{2,1,0:T(8,128)(2,1)S(1)}, u32[]{:S(2)}, u32[]{:S(2)}) collective-permute-start(bf16[1,128,128]{2,1,0:T(8,128)(2,1)} %psi_ref.1), channel_id=1, source_target_pairs={{0,12},{1,13},{2,14},{3,15},{4,8},{5,9},{6,10},{7,11},{8,4},{9,5},... | collective-permute-start | bytes 98312 | tf_op jit(solution)/shard_map/ppermute | solution.py:46
  5.5 5.4 %collective-permute-start.1 = (bf16[1,128,128]{2,1,0:T(8,128)(2,1)}, bf16[1,128,128]{2,1,0:T(8,128)(2,1)S(1)}, u32[]{:S(2)}, u32[]{:S(2)}) collective-permute-start(bf16[1,128,128]{2,1,0:T(8,128)(2,1)} %psi_ref.1), channel_id=1, source_target_pairs={{0,8},{1,9},{2,10},{3,11},{4,12},{5,13},{6,14},{7,15},{8,0},{9,1},... | collective-permute-start | bytes 98312 | tf_op jit(solution)/shard_map/ppermute | solution.py:46
  6.3 1.0 %copy-start = (bf16[16,128,128]{2,1,0:T(8,128)(2,1)S(1)}, bf16[16,128,128]{2,1,0:T(8,128)(2,1)}, u32[]{:S(2)}) copy-start(bf16[16,128,128]{2,1,0:T(8,128)(2,1)} %left_ref.1) | copy-start | bytes 1572868
  7.3 0.8 %copy-start.2 = (bf16[1,128,128]{2,1,0:T(8,128)(2,1)S(1)}, bf16[1,128,128]{2,1,0:T(8,128)(2,1)}, u32[]{:S(2)}) copy-start(bf16[1,128,128]{2,1,0:T(8,128)(2,1)} %psi_ref.1) | copy-start | bytes 98308
  10.9 5.0 %collective-permute-start.3 = (bf16[4,128,128]{2,1,0:T(8,128)(2,1)S(1)}, bf16[4,128,128]{2,1,0:T(8,128)(2,1)S(1)}, u32[]{:S(2)}, u32[]{:S(2)}) collective-permute-start(bf16[4,128,128]{2,1,0:T(8,128)(2,1)S(1)} %pad_maximum_fusion.1.psi_ref), channel_id=1, source_target_pairs={{0,2},{1,3},{2,0},{3,1},{4,6},{5,7},{6,4},{7,5},{8,10},{9,11},{10,... | collective-permute-start | bytes 393224 | tf_op jit(solution)/shard_map/ppermute | solution.py:46
  12.5 1.0 %copy-start.1 = (bf16[16,128,128]{2,1,0:T(8,128)(2,1)S(1)}, bf16[16,128,128]{2,1,0:T(8,128)(2,1)}, u32[]{:S(2)}) copy-start(bf16[16,128,128]{2,1,0:T(8,128)(2,1)} %right_ref.1) | copy-start | bytes 1572868
  16.0 1.6 %collective-permute-start.4 = (bf16[8,128,128]{2,1,0:T(8,128)(2,1)S(1)}, bf16[8,128,128]{2,1,0:T(8,128)(2,1)S(1)}, u32[]{:S(2)}, u32[]{:S(2)}) collective-permute-start(bf16[8,128,128]{2,1,0:T(8,128)(2,1)S(1)} %pad_maximum_fusion), channel_id=1, source_target_pairs={{0,1},{1,0},{2,3},{3,2},{4,5},{5,4},{6,7},{7,6},{8,9},{9,8},{10,11... | collective-permute-start | bytes 786440 | tf_op jit(solution)/shard_map/ppermute | solution.py:46
  20.1 2.7 %collective-permute-start.5 = (f32[8,128,128]{2,1,0:T(8,128)S(1)}, f32[8,128,128]{2,1,0:T(8,128)S(1)}, u32[]{:S(2)}, u32[]{:S(2)}) collective-permute-start(f32[8,128,128]{2,1,0:T(8,128)S(1)} %get-tuple-element.29), channel_id=1, source_target_pairs={{0,1},{1,0},{2,3},{3,2},{4,5},{5,4},{6,7},{7,6},{8,9},{9,8},{10,11... | collective-permute-start | bytes 1572872 | tf_op jit(solution)/shard_map/ppermute | solution.py:46
  22.9 5.8 %collective-permute-start.6 = (bf16[4,128,128]{2,1,0:T(8,128)(2,1)S(1)}, bf16[4,128,128]{2,1,0:T(8,128)(2,1)S(1)}, u32[]{:S(2)}, u32[]{:S(2)}) collective-permute-start(bf16[4,128,128]{2,1,0:T(8,128)(2,1)S(1)} %fusion), channel_id=1, source_target_pairs={{0,2},{1,3},{2,0},{3,1},{4,6},{5,7},{6,4},{7,5},{8,10},{9,11},{10,... | collective-permute-start | bytes 393224 | tf_op jit(solution)/shard_map/ppermute | solution.py:46
  28.8 6.0 %collective-permute-start.7 = (bf16[128,128]{1,0:T(8,128)(2,1)S(1)}, bf16[128,128]{1,0:T(8,128)(2,1)S(1)}, u32[]{:S(2)}, u32[]{:S(2)}) collective-permute-start(bf16[128,128]{1,0:T(8,128)(2,1)S(1)} %get-tuple-element.33), channel_id=1, source_target_pairs={{0,12},{1,13},{2,14},{3,15},{4,8},{5,9},{6,10},{7,11},{8,4},{9,5},... | collective-permute-start | bytes 98312 | tf_op jit(solution)/shard_map/ppermute | solution.py:46
  30.2 5.3 %collective-permute-start.9 = (bf16[128,128]{1,0:T(8,128)(2,1)S(1)}, bf16[128,128]{1,0:T(8,128)(2,1)S(1)}, u32[]{:S(2)}, u32[]{:S(2)}) collective-permute-start(bf16[128,128]{1,0:T(8,128)(2,1)S(1)} %get-tuple-element.34), channel_id=1, source_target_pairs={{0,8},{1,9},{2,10},{3,11},{4,12},{5,13},{6,14},{7,15},{8,0},{9,1},... | collective-permute-start | bytes 98312 | tf_op jit(solution)/shard_map/ppermute | solution.py:46
  30.7 4.8 %collective-permute-start.8 = (bf16[128,128]{1,0:T(8,128)(2,1)S(1)}, bf16[128,128]{1,0:T(8,128)(2,1)S(1)}, u32[]{:S(2)}, u32[]{:S(2)}) collective-permute-start(bf16[128,128]{1,0:T(8,128)(2,1)S(1)} %get-tuple-element.35), channel_id=1, source_target_pairs={{0,4},{1,5},{2,6},{3,7},{4,0},{5,1},{6,2},{7,3},{8,12},{9,13},{10,... | collective-permute-start | bytes 98312 | tf_op jit(solution)/shard_map/ppermute | solution.py:46

commit v8 on v7

--- a/solution.py
+++ b/solution.py
@@ -48,7 +48,9 @@
 
 def place(sector, me):
     near = sector ^ me
-    return (near >> 2) | ((near & 2) << 1) | ((near & 1) << 3)
+    along_z = near >> 2
+    spot = jnp.where(along_z == 3, 1, jnp.where(along_z == 0, 0, along_z + 1))
+    return spot | ((near & 2) << 1) | ((near & 1) << 3)
 
 
 def order_kernel(nops, coup_ref, out_ref):
@@ -73,8 +75,9 @@
     number = count(here, 0)
     only = picked(here, block_col, 0)
     few = (number <= 4).astype(jnp.int32) + (number <= 2).astype(jnp.int32)
-    group = (lane < cells // 2).astype(jnp.int32) + (lane < cells // 4).astype(jnp.int32)
-    kind = jnp.where(number < 2, 9, few + 3 * group)
+    stays = jnp.where(lane & (cells // 4) == 0, 2, 0)
+    group = stays + jnp.where(lane < cells // 2, 1, 0)
+    kind = jnp.where(number < 2, 12, few + 3 * group)
     square = (cells, cells)
     kind_col = as_column(kind)
     ahead = (kind_col < kind) | ((kind_col == kind) & (iota(square, 0) < iota(square, 1)))
@@ -86,7 +89,7 @@
     out_ref[:, SUM : SUM + cells] = (firsts << COUNT_BITS) + picked(chosen, as_column(number), 0)
     small = iota((1, 128), 1)
     ends = jnp.zeros((1, 128), jnp.int32)
-    for k in range(9):
+    for k in range(12):
         ends = jnp.where(small == k, count(kind <= k, 1), ends)
     out_ref[:, ENDS : ENDS + 128] = ends
 
@@ -95,8 +98,7 @@
     return pltpu.CompilerParams(vmem_limit_bytes=limit * 1024 * 1024)
 
 
-def cost(flops):
-    return pl.CostEstimate(flops=flops, bytes_accessed=1 << 20, transcendentals=0)
+COST = pl.CostEstimate(flops=0, bytes_accessed=1 << 16, transcendentals=0)
 
 
 def order_slots(nops, couplings, live):
@@ -108,7 +110,7 @@
         in_specs=[VMEM],
         out_specs=VMEM,
         compiler_params=params(16),
-        cost_estimate=cost(20 * slots * slots),
+        cost_estimate=COST,
         name="order",
     )(rows)
 
@@ -125,7 +127,7 @@
         in_specs=[VMEM] * 2,
         out_specs=[VMEM] * 2,
         compiler_params=params(4),
-        cost_estimate=cost(0),
+        cost_estimate=COST,
         name="hold",
     )(psi, left_ops)
 
@@ -144,7 +146,7 @@
         in_specs=[VMEM],
         out_specs=VMEM,
         compiler_params=params(4),
-        cost_estimate=cost(0),
+        cost_estimate=COST,
         name="turn",
     )(right_ops)
 
@@ -246,7 +248,7 @@
         in_specs=[VMEM] * 2,
         out_specs=VMEM,
         compiler_params=params(24),
-        cost_estimate=cost(2 * psi.shape[0] * nops * m**3),
+        cost_estimate=COST,
         name="early",
     )(psi, left)
 
@@ -264,12 +266,13 @@
         out_specs=VMEM,
         input_output_aliases={2: 0},
         compiler_params=params(24),
-        cost_estimate=cost(2 * psi.shape[0] * nops * m**3),
+        cost_estimate=COST,
         name="more",
     )(psi, left, blocks)
 
 
-def terms(order, turned, blocks, group, offset, number, psi=None, left=None):
+def terms(order, turned, blocks, group, offset, psi=None, left=None):
+    number = 4
     m = blocks.shape[1]
     nops = turned.shape[0] // m
     cells = OPS * nops
@@ -280,7 +283,7 @@
         copy = pltpu.make_async_copy(order_in, order_ref, sem)
         copy.start()
         if extra:
-            fill(refs[0], refs[1], block_ref, OPS // 2)
+            fill(refs[0], refs[1], block_ref, OPS - psi.shape[0])
         copy.wait()
 
         def order(i):
@@ -302,7 +305,7 @@
         scratch_shapes=[pltpu.SMEM(order.shape, jnp.int32), pltpu.SemaphoreType.DMA],
         input_output_aliases={2 + len(extra): 0},
         compiler_params=params(24),
-        cost_estimate=cost(2 * (number + len(extra) * 4) * nops * m**3),
+        cost_estimate=COST,
         name=f"terms_{group}",
     )(order, turned, *extra, blocks)
 
@@ -334,24 +337,29 @@
     psi, left = hold(psi, left_ops)
     order = order_slots(left_ops.shape[0], couplings, live)
     four, left, order = lax.optimization_barrier(
-        (jnp.concatenate([psi, came[4], came[8], came[12]], axis=0), left, order)
+        (jnp.concatenate([psi, *came.values()], axis=0), left, order)
     )
     came = exchange(four, ALONG_X)
-    blocks = early(four, left, slots)
+    four, blocks = lax.optimization_barrier((four, early(four, left, slots)))
+    far_four = exchange(four, OTHER_CORE)
     turned = turn(right_ops)
-    eight, turned, blocks = lax.optimization_barrier(
-        (jnp.concatenate([four, came], axis=0), turned, blocks)
-    )
-    far = exchange(eight, OTHER_CORE)
+    came, turned, blocks = lax.optimization_barrier((came, turned, blocks))
+    far = exchange(came, OTHER_CORE)
     blocks = more(came, left, blocks, 4)
-    blocks, send = terms(order, turned, blocks, 0, 8, 8, far, left)
+    blocks, far_four = lax.optimization_barrier((blocks, far_four))
+    blocks = more(far_four, left, blocks, 8)
+    blocks, send = terms(order, turned, blocks, 0, 12, far, left)
     came = exchange(send, OTHER_CORE)
-    blocks, next_four = terms(order, turned, blocks, 1, 4, 4)
-    arrived = exchange((next_four + came[4:]).astype(jnp.bfloat16), ALONG_X)
-    _, last_four = terms(order, turned, blocks, 2, 0, 4)
-    total = last_four + came[:4] + arrived.astype(jnp.float32)
+    blocks, keep = terms(order, turned, blocks, 1, 4)
+    leaving, blocks = lax.optimization_barrier(((keep + came).astype(jnp.bfloat16), blocks))
+    arrived = exchange(leaving, ALONG_X)
+    blocks, send = terms(order, turned, blocks, 2, 8)
+    came = exchange(send, OTHER_CORE)
+    _, keep = terms(order, turned, blocks, 3, 0)
+    keep, came = lax.optimization_barrier((keep + arrived.astype(jnp.float32), came))
+    total = keep + came
     parts = [
-        exchange(total[apart // 4].astype(jnp.bfloat16), apart) for apart in ALONG_Z
+        exchange(total[k + 1].astype(jnp.bfloat16), apart) for k, apart in enumerate(ALONG_Z)
     ]
     return sum((part.astype(jnp.float32) for part in parts), total[0])[None]
 

time: 36.3 us -> 35.2 us (0.970)
  waiting for transfers between devices: 9.01 us -> 6.94 us
  Pallas kernels: 7.54 us -> 9.13 us
  starting transfers between devices: 14.5 us -> 13.7 us
    ppermute x10 -> x12, waiting for transfers between devices: 9.01 us -> 6.94 us  [exchange(): return lax.ppermute(x, 'ops', [(i, i ^ apart) for i in range(OPS)])]
    pallas_call x3 -> x4, Pallas kernels: 5.31 us -> 6.21 us  [terms(): pl.pallas_call(kernel, out_shape=[jax.ShapeDtypeStruct(blocks.shape, bloc...]
    ppermute x10 -> x12, starting transfers between devices: 14.5 us -> 13.7 us  [exchange(): return lax.ppermute(x, 'ops', [(i, i ^ apart) for i in range(OPS)])]
    pallas_call x1 -> x2, Pallas kernels: 0.69 us -> 1.38 us  [more(): pl.pallas_call(kernel, out_shape=jax.ShapeDtypeStruct(blocks.shape, block...]
  transfers between devices with their start and end apart: 10 -> 12, of which waited for: 7 -> 5; matrix products, arithmetic and copies ran while one was open for 2% -> 2% of each run, Pallas kernels for 14% -> 22%
where the time goes in v8:
time: 35.2 us; the launch traced here: 34.9 us
  starting transfers between devices  13.7 us (39%)
  Pallas kernels  9.13 us (26%)
  waiting for transfers between devices  6.94 us (20%)
  local copies, waits for them, and re-layouts  3.54 us (10%)
  between operations  0.83 us (2%)
  other arithmetic  0.76 us (2%)
    ppermute x12, starting transfers between devices, exchange(): return lax.ppermute(x, 'ops', [(i, i ^ apart) for i in range(OPS)])  13.7 us
    ppermute x12, waiting for transfers between devices, exchange(): return lax.ppermute(x, 'ops', [(i, i ^ apart) for i in range(OPS)])  6.94 us
    pallas_call x4, Pallas kernels, terms(): pl.pallas_call(kernel, out_shape=[jax.ShapeDtypeStruct(blocks.shape, bloc...  6.21 us
    unnamed x6, local copies, waits for them, and re-layouts  2.84 us
    pallas_call x2, Pallas kernels, more(): pl.pallas_call(kernel, out_shape=jax.ShapeDtypeStruct(blocks.shape, block...  1.38 us
  transfers between devices with their start and end apart: 12, of which 5 were waited for; matrix products, arithmetic and copies ran while one was open for 2% of the time, Pallas kernels for 22%

profile of v8, /device:TPU:0, one launch (start us, length us, event | category | flops | bytes accessed | tf_op | source)
XLA Modules:
  0.0 34.9 jit_solution(9788884070677668336)
XLA Ops:
  0.0 5.0 %collective-permute-start = (bf16[1,128,128]{2,1,0:T(8,128)(2,1)}, bf16[1,128,128]{2,1,0:T(8,128)(2,1)S(1)}, u32[]{:S(2)}, u32[]{:S(2)}) collective-permute-start(bf16[1,128,128]{2,1,0:T(8,128)(2,1)} %psi_ref.1), channel_id=1, source_target_pairs={{0,12},{1,13},{2,14},{3,15},{4,8},{5,9},{6,10},{7,11},{8,4},{9,5},... | collective-permute-start | bytes 98312 | tf_op jit(solution)/shard_map/ppermute | solution.py:46
  5.1 0.6 %collective-permute-start.1 = (bf16[1,128,128]{2,1,0:T(8,128)(2,1)}, bf16[1,128,128]{2,1,0:T(8,128)(2,1)S(1)}, u32[]{:S(2)}, u32[]{:S(2)}) collective-permute-start(bf16[1,128,128]{2,1,0:T(8,128)(2,1)} %psi_ref.1), channel_id=1, source_target_pairs={{0,4},{1,5},{2,6},{3,7},{4,0},{5,1},{6,2},{7,3},{8,12},{9,13},{10,... | collective-permute-start | bytes 98312 | tf_op jit(solution)/shard_map/ppermute | solution.py:46
  6.3 0.7 %concatenate.7.refs_0_ = s32[4,384]{1,0:T(4,128)S(1)} pad(s32[3,384]{1,0:T(4,128)} %param.8, s32[]{:T(128)} %bitcast.19), padding=0_1x0_0 | pad | bytes 10756 | tf_op jit(solution)/shard_map/concatenate | solution.py:106
  7.0 0.6 %order.1.order_in = s32[1,1024]{1,0:T(1,128)S(1)} custom-call(s32[4,384]{1,0:T(4,128)S(1)} %concatenate.7.refs_0_), custom_call_target="tpu_custom_call" | custom-call | bytes 65536 | tf_op jit(solution)/shard_map/order/pallas_call | solution.py:107
  7.6 0.0 copy-start
  7.6 1.0 %copy-done = bf16[16,128,128]{2,1,0:T(8,128)(2,1)S(1)} copy-done((bf16[16,128,128]{2,1,0:T(8,128)(2,1)S(1)}, bf16[16,128,128]{2,1,0:T(8,128)(2,1)}, u32[]{:S(2)}) %copy-start) | copy-done | bytes 524312
  8.6 0.8 %copy-done.2 = bf16[1,128,128]{2,1,0:T(8,128)(2,1)S(1)} copy-done((bf16[1,128,128]{2,1,0:T(8,128)(2,1)S(1)}, bf16[1,128,128]{2,1,0:T(8,128)(2,1)}, u32[]{:S(2)}) %copy-start.2) | copy-done | bytes 32792
  9.4 0.0 collective-permute-done
  9.5 0.6 %collective-permute-done.2 = bf16[1,128,128]{2,1,0:T(8,128)(2,1)S(1)} collective-permute-done((bf16[1,128,128]{2,1,0:T(8,128)(2,1)}, bf16[1,128,128]{2,1,0:T(8,128)(2,1)S(1)}, u32[]{:S(2)}, u32[]{:S(2)}) %collective-permute-start.2) | collective-permute-done | bytes 32800 | tf_op jit(solution)/shard_map/ppermute | solution.py:46
  10.1 1.6 %collective-permute-start.3 = (bf16[4,128,128]{2,1,0:T(8,128)(2,1)S(1)}, bf16[4,128,128]{2,1,0:T(8,128)(2,1)S(1)}, u32[]{:S(2)}, u32[]{:S(2)}) collective-permute-start(bf16[4,128,128]{2,1,0:T(8,128)(2,1)S(1)} %pad_maximum_fusion.psi_ref), channel_id=1, source_target_pairs={{0,2},{1,3},{2,0},{3,1},{4,6},{5,7},{6,4},{7,5},{8,10},{9,11},{10,... | collective-permute-start | bytes 393224 | tf_op jit(solution)/shard_map/ppermute | solution.py:46
  11.7 1.0 %copy-done.1 = bf16[16,128,128]{2,1,0:T(8,128)(2,1)S(1)} copy-done((bf16[16,128,128]{2,1,0:T(8,128)(2,1)S(1)}, bf16[16,128,128]{2,1,0:T(8,128)(2,1)}, u32[]{:S(2)}) %copy-start.1) | copy-done | bytes 524312
  12.7 0.2 turn.1.turned_ref
  12.9 0.7 %early.1._ = bf16[449,128,128]{2,1,0:T(8,128)(2,1)S(1)} custom-call(bf16[4,128,128]{2,1,0:T(8,128)(2,1)S(1)} %pad_maximum_fusion.psi_ref, bf16[16,128,128]{2,1,0:T(8,128)(2,1)S(1)} %get-tuple-element.32.left_ref.refs_1_), custom_call_target="tpu_custom_call" | custom-call | bytes 65536 | tf_op jit(solution)/shard_map/early/pallas_call | solution.py:245
  13.6 0.1 collective-permute-start.5
  13.7 1.5 %collective-permute-done.3.psi_ref = bf16[4,128,128]{2,1,0:T(8,128)(2,1)S(1)} collective-permute-done((bf16[4,128,128]{2,1,0:T(8,128)(2,1)S(1)}, bf16[4,128,128]{2,1,0:T(8,128)(2,1)S(1)}, u32[]{:S(2)}, u32[]{:S(2)}) %collective-permute-start.3) | collective-permute-done | bytes 131104 | tf_op jit(solution)/shard_map/ppermute | solution.py:46
  15.1 0.0 collective-permute-start.4
  15.1 0.7 %more.2._ = bf16[449,128,128]{2,1,0:T(8,128)(2,1)S(1)} custom-call(bf16[4,128,128]{2,1,0:T(8,128)(2,1)S(1)} %collective-permute-done.3.psi_ref, bf16[16,128,128]{2,1,0:T(8,128)(2,1)S(1)} %get-tuple-element.32.left_ref.refs_1_, bf16[449,128,128]{2,1,0:T(8,128)(2,1)S(1)} %early.1._), custom_call_target="tpu_custom_call", output_to_operand_aliasing={{}: (2, {})} | custom-call | bytes 65536 | tf_op jit(solution)/shard_map/more/pallas_call | solution.py:262
  15.8 0.0 collective-permute-done.5.psi_ref
  15.8 0.7 %more.3.refs_2_ = bf16[449,128,128]{2,1,0:T(8,128)(2,1)S(1)} custom-call(bf16[4,128,128]{2,1,0:T(8,128)(2,1)S(1)} %collective-permute-done.5.psi_ref, bf16[16,128,128]{2,1,0:T(8,128)(2,1)S(1)} %get-tuple-element.32.left_ref.refs_1_, bf16[449,128,128]{2,1,0:T(8,128)(2,1)S(1)} %more.2._), custom_call_target="tpu_custom_call", output_to_operand_aliasing={{}: (2, {})} | custom-call | bytes 65536 | tf_op jit(solution)/shard_map/more/pallas_call | solution.py:262
  16.6 1.6 %terms_0.1 = (bf16[449,128,128]{2,1,0:T(8,128)(2,1)S(1)}, f32[4,128,128]{2,1,0:T(8,128)S(1)}) custom-call(s32[1,1024]{1,0:T(1,128)S(1)} %order.1.order_in, bf16[2048,128]{1,0:T(8,128)(2,1)S(1)} %turn.1.turned_ref, bf16[4,128,128]{2,1,0:T(8,128)(2,1)S(1)} %collective-permute-done.4.refs_0_, ...), custom_call_target="tpu_custom_call", output_to_operand_aliasing={{0}: (4, {})} | custom-call | bytes 65536 | tf_op jit(solution)/shard_map/terms_0/pallas_call | solution.py:297
  18.2 0.7 %collective-permute-start.6 = (f32[4,128,128]{2,1,0:T(8,128)S(1)}, f32[4,128,128]{2,1,0:T(8,128)S(1)}, u32[]{:S(2)}, u32[]{:S(2)}) collective-permute-start(f32[4,128,128]{2,1,0:T(8,128)S(1)} %get-tuple-element.42), channel_id=1, source_target_pairs={{0,1},{1,0},{2,3},{3,2},{4,5},{5,4},{6,7},{7,6},{8,9},{9,8},{10,11... | collective-permute-start | bytes 786440 | tf_op jit(solution)/shard_map/ppermute | solution.py:46
  18.9 1.6 %terms_1.1 = (bf16[449,128,128]{2,1,0:T(8,128)(2,1)S(1)}, f32[4,128,128]{2,1,0:T(8,128)S(1)}) custom-call(s32[1,1024]{1,0:T(1,128)S(1)} %order.1.order_in, bf16[2048,128]{1,0:T(8,128)(2,1)S(1)} %turn.1.turned_ref, bf16[449,128,128]{2,1,0:T(8,128)(2,1)S(1)} %get-tuple-element.40.refs_0_), custom_call_target="tpu_custom_call", output_to_operand_aliasing={{0}: (2, {})} | custom-call | bytes 65536 | tf_op jit(solution)/shard_map/terms_1/pallas_call | solution.py:297
  20.6 1.2 %collective-permute-start.7 = (bf16[4,128,128]{2,1,0:T(8,128)(2,1)S(1)}, bf16[4,128,128]{2,1,0:T(8,128)(2,1)S(1)}, u32[]{:S(2)}, u32[]{:S(2)}) collective-permute-start(bf16[4,128,128]{2,1,0:T(8,128)(2,1)S(1)} %add_convert_fusion), channel_id=1, source_target_pairs={{0,2},{1,3},{2,0},{3,1},{4,6},{5,7},{6,4},{7,5},{8,10},{9,11},{10,... | collective-permute-start | bytes 393224 | tf_op jit(solution)/shard_map/ppermute | solution.py:46
  21.8 1.5 %terms_2.1 = (bf16[449,128,128]{2,1,0:T(8,128)(2,1)S(1)}, f32[4,128,128]{2,1,0:T(8,128)S(1)}) custom-call(s32[1,1024]{1,0:T(1,128)S(1)} %order.1.order_in, bf16[2048,128]{1,0:T(8,128)(2,1)S(1)} %turn.1.turned_ref, bf16[449,128,128]{2,1,0:T(8,128)(2,1)S(1)} %get-tuple-element.44.refs_0_), custom_call_target="tpu_custom_call", output_to_operand_aliasing={{0}: (2, {})} | custom-call | bytes 65536 | tf_op jit(solution)/shard_map/terms_2/pallas_call | solution.py:297
  23.3 0.1 collective-permute-start.8
  23.4 1.5 %terms_3.1 = (bf16[449,128,128]{2,1,0:T(8,128)(2,1)S(1)}, f32[4,128,128]{2,1,0:T(8,128)S(1)}) custom-call(s32[1,1024]{1,0:T(1,128)S(1)} %order.1.order_in, bf16[2048,128]{1,0:T(8,128)(2,1)S(1)} %turn.1.turned_ref, bf16[449,128,128]{2,1,0:T(8,128)(2,1)S(1)} %get-tuple-element.45.refs_0_), custom_call_target="tpu_custom_call", output_to_operand_aliasing={{0}: (2, {})} | custom-call | bytes 65536 | tf_op jit(solution)/shard_map/terms_3/pallas_call | solution.py:297
  24.9 1.2 %collective-permute-done.7 = bf16[4,128,128]{2,1,0:T(8,128)(2,1)S(1)} collective-permute-done((bf16[4,128,128]{2,1,0:T(8,128)(2,1)S(1)}, bf16[4,128,128]{2,1,0:T(8,128)(2,1)S(1)}, u32[]{:S(2)}, u32[]{:S(2)}) %collective-permute-start.7) | collective-permute-done | bytes 131104 | tf_op jit(solution)/shard_map/ppermute | solution.py:46
  26.2 3.3 %collective-permute-start.9 = (bf16[128,128]{1,0:T(8,128)(2,1)S(1)}, bf16[128,128]{1,0:T(8,128)(2,1)S(1)}, u32[]{:S(2)}, u32[]{:S(2)}) collective-permute-start(bf16[128,128]{1,0:T(8,128)(2,1)S(1)} %get-tuple-element.53), channel_id=1, source_target_pairs={{0,12},{1,13},{2,14},{3,15},{4,8},{5,9},{6,10},{7,11},{8,4},{9,5},... | collective-permute-start | bytes 98312 | tf_op jit(solution)/shard_map/ppermute | solution.py:46
  29.4 1.2 %collective-permute-start.10 = (bf16[128,128]{1,0:T(8,128)(2,1)S(1)}, bf16[128,128]{1,0:T(8,128)(2,1)S(1)}, u32[]{:S(2)}, u32[]{:S(2)}) collective-permute-start(bf16[128,128]{1,0:T(8,128)(2,1)S(1)} %get-tuple-element.55), channel_id=1, source_target_pairs={{0,4},{1,5},{2,6},{3,7},{4,0},{5,1},{6,2},{7,3},{8,12},{9,13},{10,... | collective-permute-start | bytes 98312 | tf_op jit(solution)/shard_map/ppermute | solution.py:46
  30.6 1.6 %collective-permute-done.9 = bf16[128,128]{1,0:T(8,128)(2,1)S(1)} collective-permute-done((bf16[128,128]{1,0:T(8,128)(2,1)S(1)}, bf16[128,128]{1,0:T(8,128)(2,1)S(1)}, u32[]{:S(2)}, u32[]{:S(2)}) %collective-permute-start.9) | collective-permute-done | bytes 32800 | tf_op jit(solution)/shard_map/ppermute | solution.py:46
  32.2 2.1 %collective-permute-done.11 = bf16[128,128]{1,0:T(8,128)(2,1)S(1)} collective-permute-done((bf16[128,128]{1,0:T(8,128)(2,1)S(1)}, bf16[128,128]{1,0:T(8,128)(2,1)S(1)}, u32[]{:S(2)}, u32[]{:S(2)}) %collective-permute-start.11) | collective-permute-done | bytes 32800 | tf_op jit(solution)/shard_map/ppermute | solution.py:46
  34.3 0.6 %fusion.3 = f32[1,128,128]{2,1,0:T(8,128)} fusion(f32[4,128,128]{2,1,0:T(8,128)S(1)} %get-tuple-element.52, bf16[128,128]{1,0:T(8,128)(2,1)S(1)} %collective-permute-done.11, bf16[128,128]{1,0:T(8,128)(2,1)S(1)} %collective-permute-done.10, bf16[128,128]{1,0:T(8,128)(2,1)S(1)} %collective-permute-done.9), kind=kLoop, calls=%fused_computation.7 | loop fusion | flops 98304 | bytes 229376 | tf_op jit(solution)/shard_map/broadcast_in_dim | solution.py:364
  (15 shorter events, 0.2 us)
Async XLA Ops:
  0.0 9.4 %collective-permute-start = (bf16[1,128,128]{2,1,0:T(8,128)(2,1)}, bf16[1,128,128]{2,1,0:T(8,128)(2,1)S(1)}, u32[]{:S(2)}, u32[]{:S(2)}) collective-permute-start(bf16[1,128,128]{2,1,0:T(8,128)(2,1)} %psi_ref.1), channel_id=1, source_target_pairs={{0,12},{1,13},{2,14},{3,15},{4,8},{5,9},{6,10},{7,11},{8,4},{9,5},... | collective-permute-start | bytes 98312 | tf_op jit(solution)/shard_map/ppermute | solution.py:46
  5.0 5.0 %collective-permute-start.2 = (bf16[1,128,128]{2,1,0:T(8,128)(2,1)}, bf16[1,128,128]{2,1,0:T(8,128)(2,1)S(1)}, u32[]{:S(2)}, u32[]{:S(2)}) collective-permute-start(bf16[1,128,128]{2,1,0:T(8,128)(2,1)} %psi_ref.1), channel_id=1, source_target_pairs={{0,8},{1,9},{2,10},{3,11},{4,12},{5,13},{6,14},{7,15},{8,0},{9,1},... | collective-permute-start | bytes 98312 | tf_op jit(solution)/shard_map/ppermute | solution.py:46
  5.1 5.0 %collective-permute-start.1 = (bf16[1,128,128]{2,1,0:T(8,128)(2,1)}, bf16[1,128,128]{2,1,0:T(8,128)(2,1)S(1)}, u32[]{:S(2)}, u32[]{:S(2)}) collective-permute-start(bf16[1,128,128]{2,1,0:T(8,128)(2,1)} %psi_ref.1), channel_id=1, source_target_pairs={{0,4},{1,5},{2,6},{3,7},{4,0},{5,1},{6,2},{7,3},{8,12},{9,13},{10,... | collective-permute-start | bytes 98312 | tf_op jit(solution)/shard_map/ppermute | solution.py:46
  7.6 1.0 %copy-start = (bf16[16,128,128]{2,1,0:T(8,128)(2,1)S(1)}, bf16[16,128,128]{2,1,0:T(8,128)(2,1)}, u32[]{:S(2)}) copy-start(bf16[16,128,128]{2,1,0:T(8,128)(2,1)} %left_ref.1) | copy-start | bytes 1572868
  8.6 0.8 %copy-start.2 = (bf16[1,128,128]{2,1,0:T(8,128)(2,1)S(1)}, bf16[1,128,128]{2,1,0:T(8,128)(2,1)}, u32[]{:S(2)}) copy-start(bf16[1,128,128]{2,1,0:T(8,128)(2,1)} %psi_ref.1) | copy-start | bytes 98308
  10.1 5.0 %collective-permute-start.3 = (bf16[4,128,128]{2,1,0:T(8,128)(2,1)S(1)}, bf16[4,128,128]{2,1,0:T(8,128)(2,1)S(1)}, u32[]{:S(2)}, u32[]{:S(2)}) collective-permute-start(bf16[4,128,128]{2,1,0:T(8,128)(2,1)S(1)} %pad_maximum_fusion.psi_ref), channel_id=1, source_target_pairs={{0,2},{1,3},{2,0},{3,1},{4,6},{5,7},{6,4},{7,5},{8,10},{9,11},{10,... | collective-permute-start | bytes 393224 | tf_op jit(solution)/shard_map/ppermute | solution.py:46
  11.7 1.0 %copy-start.1 = (bf16[16,128,128]{2,1,0:T(8,128)(2,1)S(1)}, bf16[16,128,128]{2,1,0:T(8,128)(2,1)}, u32[]{:S(2)}) copy-start(bf16[16,128,128]{2,1,0:T(8,128)(2,1)} %right_ref.1) | copy-start | bytes 1572868
  13.6 2.3 %collective-permute-start.5 = (bf16[4,128,128]{2,1,0:T(8,128)(2,1)S(1)}, bf16[4,128,128]{2,1,0:T(8,128)(2,1)S(1)}, u32[]{:S(2)}, u32[]{:S(2)}) collective-permute-start(bf16[4,128,128]{2,1,0:T(8,128)(2,1)S(1)} %pad_maximum_fusion.psi_ref), channel_id=1, source_target_pairs={{0,1},{1,0},{2,3},{3,2},{4,5},{5,4},{6,7},{7,6},{8,9},{9,8},{10,11... | collective-permute-start | bytes 393224 | tf_op jit(solution)/shard_map/ppermute | solution.py:46
  15.1 1.4 %collective-permute-start.4 = (bf16[4,128,128]{2,1,0:T(8,128)(2,1)S(1)}, bf16[4,128,128]{2,1,0:T(8,128)(2,1)S(1)}, u32[]{:S(2)}, u32[]{:S(2)}) collective-permute-start(bf16[4,128,128]{2,1,0:T(8,128)(2,1)S(1)} %collective-permute-done.3.psi_ref), channel_id=1, source_target_pairs={{0,1},{1,0},{2,3},{3,2},{4,5},{5,4},{6,7},{7,6},{8,9},{9,8},{10,11... | collective-permute-start | bytes 393224 | tf_op jit(solution)/shard_map/ppermute | solution.py:46
  18.2 2.4 %collective-permute-start.6 = (f32[4,128,128]{2,1,0:T(8,128)S(1)}, f32[4,128,128]{2,1,0:T(8,128)S(1)}, u32[]{:S(2)}, u32[]{:S(2)}) collective-permute-start(f32[4,128,128]{2,1,0:T(8,128)S(1)} %get-tuple-element.42), channel_id=1, source_target_pairs={{0,1},{1,0},{2,3},{3,2},{4,5},{5,4},{6,7},{7,6},{8,9},{9,8},{10,11... | collective-permute-start | bytes 786440 | tf_op jit(solution)/shard_map/ppermute | solution.py:46
  20.6 5.5 %collective-permute-start.7 = (bf16[4,128,128]{2,1,0:T(8,128)(2,1)S(1)}, bf16[4,128,128]{2,1,0:T(8,128)(2,1)S(1)}, u32[]{:S(2)}, u32[]{:S(2)}) collective-permute-start(bf16[4,128,128]{2,1,0:T(8,128)(2,1)S(1)} %add_convert_fusion), channel_id=1, source_target_pairs={{0,2},{1,3},{2,0},{3,1},{4,6},{5,7},{6,4},{7,5},{8,10},{9,11},{10,... | collective-permute-start | bytes 393224 | tf_op jit(solution)/shard_map/ppermute | solution.py:46
  23.3 2.8 %collective-permute-start.8 = (f32[4,128,128]{2,1,0:T(8,128)S(1)}, f32[4,128,128]{2,1,0:T(8,128)S(1)}, u32[]{:S(2)}, u32[]{:S(2)}) collective-permute-start(f32[4,128,128]{2,1,0:T(8,128)S(1)} %get-tuple-element.48), channel_id=1, source_target_pairs={{0,1},{1,0},{2,3},{3,2},{4,5},{5,4},{6,7},{7,6},{8,9},{9,8},{10,11... | collective-permute-start | bytes 786440 | tf_op jit(solution)/shard_map/ppermute | solution.py:46
  26.2 6.0 %collective-permute-start.9 = (bf16[128,128]{1,0:T(8,128)(2,1)S(1)}, bf16[128,128]{1,0:T(8,128)(2,1)S(1)}, u32[]{:S(2)}, u32[]{:S(2)}) collective-permute-start(bf16[128,128]{1,0:T(8,128)(2,1)S(1)} %get-tuple-element.53), channel_id=1, source_target_pairs={{0,12},{1,13},{2,14},{3,15},{4,8},{5,9},{6,10},{7,11},{8,4},{9,5},... | collective-permute-start | bytes 98312 | tf_op jit(solution)/shard_map/ppermute | solution.py:46
  29.4 4.8 %collective-permute-start.11 = (bf16[128,128]{1,0:T(8,128)(2,1)S(1)}, bf16[128,128]{1,0:T(8,128)(2,1)S(1)}, u32[]{:S(2)}, u32[]{:S(2)}) collective-permute-start(bf16[128,128]{1,0:T(8,128)(2,1)S(1)} %get-tuple-element.54), channel_id=1, source_target_pairs={{0,8},{1,9},{2,10},{3,11},{4,12},{5,13},{6,14},{7,15},{8,0},{9,1},... | collective-permute-start | bytes 98312 | tf_op jit(solution)/shard_map/ppermute | solution.py:46
  29.4 4.8 %collective-permute-start.10 = (bf16[128,128]{1,0:T(8,128)(2,1)S(1)}, bf16[128,128]{1,0:T(8,128)(2,1)S(1)}, u32[]{:S(2)}, u32[]{:S(2)}) collective-permute-start(bf16[128,128]{1,0:T(8,128)(2,1)S(1)} %get-tuple-element.55), channel_id=1, source_target_pairs={{0,4},{1,5},{2,6},{3,7},{4,0},{5,1},{6,2},{7,3},{8,12},{9,13},{10,... | collective-permute-start | bytes 98312 | tf_op jit(solution)/shard_map/ppermute | solution.py:46

commit v9 on v8

--- a/solution.py
+++ b/solution.py
@@ -59,7 +59,7 @@
     me = lax.axis_index("ops").astype(jnp.int32)
 
     g = coup_ref[0:1, :]
-    alive = iota((1, slots), 1) < coup_ref[3:4, :]
+    alive = iota((1, slots), 1) < coup_ref[3:4, 0:1]
     cell = jnp.where(alive, place(coup_ref[2:3, :], me) * nops + g, cells)
     block = place(coup_ref[1:2, :], me) * nops + g
     cell_col = as_column(cell)
@@ -103,7 +103,7 @@
 
 def order_slots(nops, couplings, live):
     slots = couplings.shape[1]
-    rows = jnp.concatenate([couplings, jnp.broadcast_to(live[None], (1, slots))], axis=0)
+    rows = jnp.concatenate([couplings, jnp.pad(live[None], ((0, 0), (0, slots - 1)))], axis=0)
     return pl.pallas_call(
         lambda *refs: order_kernel(nops, *refs),
         out_shape=jax.ShapeDtypeStruct((1, ORDER_SIZE), jnp.int32),
@@ -115,21 +115,20 @@
     )(rows)
 
 
-def hold_kernel(psi_ref, left_ref, psi_out, left_out):
-    psi_out[...] = psi_ref[...]
-    left_out[...] = left_ref[...]
-
-
-def hold(psi, left_ops):
+def hold_kernel(in_ref, out_ref):
+    out_ref[...] = in_ref[...]
+
+
+def hold(x):
     return pl.pallas_call(
         hold_kernel,
-        out_shape=[jax.ShapeDtypeStruct(x.shape, x.dtype) for x in (psi, left_ops)],
-        in_specs=[VMEM] * 2,
-        out_specs=[VMEM] * 2,
+        out_shape=jax.ShapeDtypeStruct(x.shape, x.dtype),
+        in_specs=[VMEM],
+        out_specs=VMEM,
         compiler_params=params(4),
         cost_estimate=COST,
         name="hold",
-    )(psi, left_ops)
+    )(x)
 
 
 def turn_kernel(right_ref, turned_ref):
@@ -334,12 +333,12 @@
 def shards_small(psi, left_ops, right_ops, couplings, live):
     slots = couplings.shape[1]
     came = {apart: exchange(psi, apart) for apart in ALONG_Z}
-    psi, left = hold(psi, left_ops)
     order = order_slots(left_ops.shape[0], couplings, live)
-    four, left, order = lax.optimization_barrier(
-        (jnp.concatenate([psi, *came.values()], axis=0), left, order)
+    four, order = lax.optimization_barrier(
+        (jnp.concatenate([hold(psi), *came.values()], axis=0), order)
     )
     came = exchange(four, ALONG_X)
+    left = hold(left_ops)
     four, blocks = lax.optimization_barrier((four, early(four, left, slots)))
     far_four = exchange(four, OTHER_CORE)
     turned = turn(right_ops)

time: 35.2 us -> 34.7 us (0.986)
  waiting for transfers between devices: 6.94 us -> 6.23 us
  local copies, waits for them, and re-layouts: 3.54 us -> 2.84 us
  other arithmetic: 0.76 us -> 1.46 us
  Pallas kernels: 9.13 us -> 9.71 us
    ppermute x12, waiting for transfers between devices: 6.94 us -> 6.23 us  [exchange(): return lax.ppermute(x, 'ops', [(i, i ^ apart) for i in range(OPS)])]
    concatenate x1 -> x2, other arithmetic: 0.02 us -> 0.72 us  [the longest x1 0.7 us: order_slots(): jnp.concatenate([couplings, jnp.pad(live[None], ((0, 0), (0, slots - 1)))...]
    concatenate x1 -> x0, local copies, waits for them, and re-layouts: 0.7 us -> none  [order_slots(): jnp.concatenate([couplings, jnp.broadcast_to(live[None], (1, slots))], ax...]
    pallas_call x4, Pallas kernels: 6.21 us -> 6.73 us  [terms(): pl.pallas_call(kernel, out_shape=[jax.ShapeDtypeStruct(blocks.shape, bloc...]
  transfers between devices with their start and end apart: 12 -> 12, of which waited for: 5 -> 6; matrix products, arithmetic and copies ran while one was open for 2% -> 2% of each run, Pallas kernels for 22% -> 23%
where the time goes in v9:
time: 34.7 us; the launch traced here: 34.5 us
  starting transfers between devices  13.4 us (39%)
  Pallas kernels  9.71 us (28%)
  waiting for transfers between devices  6.23 us (18%)
  local copies, waits for them, and re-layouts  2.84 us (8%)
  other arithmetic  1.46 us (4%)
  between operations  0.82 us (2%)
    ppermute x12, starting transfers between devices, exchange(): return lax.ppermute(x, 'ops', [(i, i ^ apart) for i in range(OPS)])  13.4 us
    pallas_call x4, Pallas kernels, terms(): pl.pallas_call(kernel, out_shape=[jax.ShapeDtypeStruct(blocks.shape, bloc...  6.73 us
    ppermute x12, waiting for transfers between devices, exchange(): return lax.ppermute(x, 'ops', [(i, i ^ apart) for i in range(OPS)])  6.23 us
    unnamed x6, local copies, waits for them, and re-layouts  2.84 us
    pallas_call x2, Pallas kernels, more(): pl.pallas_call(kernel, out_shape=jax.ShapeDtypeStruct(blocks.shape, block...  1.37 us
    concatenate x1, other arithmetic, order_slots(): jnp.concatenate([couplings, jnp.pad(live[None], ((0, 0), (0, slots - 1)))...  0.7 us
    pallas_call x1, Pallas kernels, order_slots(): pl.pallas_call(lambda *refs: order_kernel(nops, *refs), out_shape=jax.Sha...  0.7 us
  transfers between devices with their start and end apart: 12, of which 6 were waited for; matrix products, arithmetic and copies ran while one was open for 2% of the time, Pallas kernels for 23%

profile of v9, /device:TPU:0, one launch (start us, length us, event | category | flops | bytes accessed | tf_op | source)
XLA Modules:
  0.0 34.5 jit_solution(5201348816893723942)
XLA Ops:
  0.0 5.0 %collective-permute-start = (bf16[1,128,128]{2,1,0:T(8,128)(2,1)}, bf16[1,128,128]{2,1,0:T(8,128)(2,1)S(1)}, u32[]{:S(2)}, u32[]{:S(2)}) collective-permute-start(bf16[1,128,128]{2,1,0:T(8,128)(2,1)} %in_ref.2), channel_id=1, source_target_pairs={{0,12},{1,13},{2,14},{3,15},{4,8},{5,9},{6,10},{7,11},{8,4},{9,5},... | collective-permute-start | bytes 98312 | tf_op jit(solution)/shard_map/ppermute | solution.py:46
  5.1 0.6 %collective-permute-start.1 = (bf16[1,128,128]{2,1,0:T(8,128)(2,1)}, bf16[1,128,128]{2,1,0:T(8,128)(2,1)S(1)}, u32[]{:S(2)}, u32[]{:S(2)}) collective-permute-start(bf16[1,128,128]{2,1,0:T(8,128)(2,1)} %in_ref.2), channel_id=1, source_target_pairs={{0,4},{1,5},{2,6},{3,7},{4,0},{5,1},{6,2},{7,3},{8,12},{9,13},{10,... | collective-permute-start | bytes 98312 | tf_op jit(solution)/shard_map/ppermute | solution.py:46
  6.3 0.7 %pad_add_fusion.refs_0_ = s32[4,384]{1,0:T(4,128)S(1)} fusion(s32[1,1]{1,0:T(1,128)} %bitcast.19, s32[3,384]{1,0:T(4,128)} %param.8), kind=kLoop, calls=%fused_computation.11 | loop fusion | flops 1536 | bytes 10756 | tf_op jit(solution)/shard_map/concatenate | solution.py:106
  7.0 0.8 %copy-done.2 = bf16[1,128,128]{2,1,0:T(8,128)(2,1)S(1)} copy-done((bf16[1,128,128]{2,1,0:T(8,128)(2,1)S(1)}, bf16[1,128,128]{2,1,0:T(8,128)(2,1)}, u32[]{:S(2)}) %copy-start.2) | copy-done | bytes 32792
  7.7 0.7 %order.1.order_in = s32[1,1024]{1,0:T(1,128)S(1)} custom-call(s32[4,384]{1,0:T(4,128)S(1)} %pad_add_fusion.refs_0_), custom_call_target="tpu_custom_call" | custom-call | bytes 65536 | tf_op jit(solution)/shard_map/order/pallas_call | solution.py:107
  8.4 1.6 %collective-permute-done.2 = bf16[1,128,128]{2,1,0:T(8,128)(2,1)S(1)} collective-permute-done((bf16[1,128,128]{2,1,0:T(8,128)(2,1)}, bf16[1,128,128]{2,1,0:T(8,128)(2,1)S(1)}, u32[]{:S(2)}, u32[]{:S(2)}) %collective-permute-start.2) | collective-permute-done | bytes 32800 | tf_op jit(solution)/shard_map/ppermute | solution.py:46
  10.1 1.6 %collective-permute-start.3 = (bf16[4,128,128]{2,1,0:T(8,128)(2,1)S(1)}, bf16[4,128,128]{2,1,0:T(8,128)(2,1)S(1)}, u32[]{:S(2)}, u32[]{:S(2)}) collective-permute-start(bf16[4,128,128]{2,1,0:T(8,128)(2,1)S(1)} %pad_maximum_fusion.psi_ref), channel_id=1, source_target_pairs={{0,2},{1,3},{2,0},{3,1},{4,6},{5,7},{6,4},{7,5},{8,10},{9,11},{10,... | collective-permute-start | bytes 393224 | tf_op jit(solution)/shard_map/ppermute | solution.py:46
  11.7 1.0 %copy-done = bf16[16,128,128]{2,1,0:T(8,128)(2,1)S(1)} copy-done((bf16[16,128,128]{2,1,0:T(8,128)(2,1)S(1)}, bf16[16,128,128]{2,1,0:T(8,128)(2,1)}, u32[]{:S(2)}) %copy-start) | copy-done | bytes 524312
  12.7 0.0 copy-start.1
  12.8 1.0 %copy-done.1 = bf16[16,128,128]{2,1,0:T(8,128)(2,1)S(1)} copy-done((bf16[16,128,128]{2,1,0:T(8,128)(2,1)S(1)}, bf16[16,128,128]{2,1,0:T(8,128)(2,1)}, u32[]{:S(2)}) %copy-start.1) | copy-done | bytes 524312
  13.8 0.2 turn.1.turned_ref
  14.0 0.7 %early.1._ = bf16[449,128,128]{2,1,0:T(8,128)(2,1)S(1)} custom-call(bf16[4,128,128]{2,1,0:T(8,128)(2,1)S(1)} %pad_maximum_fusion.psi_ref, bf16[16,128,128]{2,1,0:T(8,128)(2,1)S(1)} %hold.3.left_ref.refs_1_), custom_call_target="tpu_custom_call" | custom-call | bytes 65536 | tf_op jit(solution)/shard_map/early/pallas_call | solution.py:244
  14.7 0.1 collective-permute-start.5
  14.8 0.4 %collective-permute-done.3.psi_ref = bf16[4,128,128]{2,1,0:T(8,128)(2,1)S(1)} collective-permute-done((bf16[4,128,128]{2,1,0:T(8,128)(2,1)S(1)}, bf16[4,128,128]{2,1,0:T(8,128)(2,1)S(1)}, u32[]{:S(2)}, u32[]{:S(2)}) %collective-permute-start.3) | collective-permute-done | bytes 131104 | tf_op jit(solution)/shard_map/ppermute | solution.py:46
  15.1 0.1 collective-permute-start.4
  15.3 0.7 %more.2._ = bf16[449,128,128]{2,1,0:T(8,128)(2,1)S(1)} custom-call(bf16[4,128,128]{2,1,0:T(8,128)(2,1)S(1)} %collective-permute-done.3.psi_ref, bf16[16,128,128]{2,1,0:T(8,128)(2,1)S(1)} %hold.3.left_ref.refs_1_, bf16[449,128,128]{2,1,0:T(8,128)(2,1)S(1)} %early.1._), custom_call_target="tpu_custom_call", output_to_operand_aliasing={{}: (2, {})} | custom-call | bytes 65536 | tf_op jit(solution)/shard_map/more/pallas_call | solution.py:261
  15.9 0.1 collective-permute-done.5.psi_ref
  16.1 0.7 %more.3.refs_2_ = bf16[449,128,128]{2,1,0:T(8,128)(2,1)S(1)} custom-call(bf16[4,128,128]{2,1,0:T(8,128)(2,1)S(1)} %collective-permute-done.5.psi_ref, bf16[16,128,128]{2,1,0:T(8,128)(2,1)S(1)} %hold.3.left_ref.refs_1_, bf16[449,128,128]{2,1,0:T(8,128)(2,1)S(1)} %more.2._), custom_call_target="tpu_custom_call", output_to_operand_aliasing={{}: (2, {})} | custom-call | bytes 65536 | tf_op jit(solution)/shard_map/more/pallas_call | solution.py:261
  16.8 1.7 %terms_0.1 = (bf16[449,128,128]{2,1,0:T(8,128)(2,1)S(1)}, f32[4,128,128]{2,1,0:T(8,128)S(1)}) custom-call(s32[1,1024]{1,0:T(1,128)S(1)} %order.1.order_in, bf16[2048,128]{1,0:T(8,128)(2,1)S(1)} %turn.1.turned_ref, bf16[4,128,128]{2,1,0:T(8,128)(2,1)S(1)} %collective-permute-done.4.refs_0_, ...), custom_call_target="tpu_custom_call", output_to_operand_aliasing={{0}: (4, {})} | custom-call | bytes 65536 | tf_op jit(solution)/shard_map/terms_0/pallas_call | solution.py:296
  18.5 0.1 collective-permute-start.6
  18.6 1.7 %terms_1.1 = (bf16[449,128,128]{2,1,0:T(8,128)(2,1)S(1)}, f32[4,128,128]{2,1,0:T(8,128)S(1)}) custom-call(s32[1,1024]{1,0:T(1,128)S(1)} %order.1.order_in, bf16[2048,128]{1,0:T(8,128)(2,1)S(1)} %turn.1.turned_ref, bf16[449,128,128]{2,1,0:T(8,128)(2,1)S(1)} %get-tuple-element.34.refs_0_), custom_call_target="tpu_custom_call", output_to_operand_aliasing={{0}: (2, {})} | custom-call | bytes 65536 | tf_op jit(solution)/shard_map/terms_1/pallas_call | solution.py:296
  20.4 1.4 %collective-permute-start.7 = (bf16[4,128,128]{2,1,0:T(8,128)(2,1)S(1)}, bf16[4,128,128]{2,1,0:T(8,128)(2,1)S(1)}, u32[]{:S(2)}, u32[]{:S(2)}) collective-permute-start(bf16[4,128,128]{2,1,0:T(8,128)(2,1)S(1)} %add_convert_fusion), channel_id=1, source_target_pairs={{0,2},{1,3},{2,0},{3,1},{4,6},{5,7},{6,4},{7,5},{8,10},{9,11},{10,... | collective-permute-start | bytes 393224 | tf_op jit(solution)/shard_map/ppermute | solution.py:46
  21.8 1.6 %terms_2.1 = (bf16[449,128,128]{2,1,0:T(8,128)(2,1)S(1)}, f32[4,128,128]{2,1,0:T(8,128)S(1)}) custom-call(s32[1,1024]{1,0:T(1,128)S(1)} %order.1.order_in, bf16[2048,128]{1,0:T(8,128)(2,1)S(1)} %turn.1.turned_ref, bf16[449,128,128]{2,1,0:T(8,128)(2,1)S(1)} %get-tuple-element.38.refs_0_), custom_call_target="tpu_custom_call", output_to_operand_aliasing={{0}: (2, {})} | custom-call | bytes 65536 | tf_op jit(solution)/shard_map/terms_2/pallas_call | solution.py:296
  23.4 0.1 collective-permute-start.8
  23.5 1.7 %terms_3.1 = (bf16[449,128,128]{2,1,0:T(8,128)(2,1)S(1)}, f32[4,128,128]{2,1,0:T(8,128)S(1)}) custom-call(s32[1,1024]{1,0:T(1,128)S(1)} %order.1.order_in, bf16[2048,128]{1,0:T(8,128)(2,1)S(1)} %turn.1.turned_ref, bf16[449,128,128]{2,1,0:T(8,128)(2,1)S(1)} %get-tuple-element.39.refs_0_), custom_call_target="tpu_custom_call", output_to_operand_aliasing={{0}: (2, {})} | custom-call | bytes 65536 | tf_op jit(solution)/shard_map/terms_3/pallas_call | solution.py:296
  25.2 0.8 %collective-permute-done.7 = bf16[4,128,128]{2,1,0:T(8,128)(2,1)S(1)} collective-permute-done((bf16[4,128,128]{2,1,0:T(8,128)(2,1)S(1)}, bf16[4,128,128]{2,1,0:T(8,128)(2,1)S(1)}, u32[]{:S(2)}, u32[]{:S(2)}) %collective-permute-start.7) | collective-permute-done | bytes 131104 | tf_op jit(solution)/shard_map/ppermute | solution.py:46
  26.1 2.6 %collective-permute-start.9 = (bf16[128,128]{1,0:T(8,128)(2,1)S(1)}, bf16[128,128]{1,0:T(8,128)(2,1)S(1)}, u32[]{:S(2)}, u32[]{:S(2)}) collective-permute-start(bf16[128,128]{1,0:T(8,128)(2,1)S(1)} %get-tuple-element.47), channel_id=1, source_target_pairs={{0,12},{1,13},{2,14},{3,15},{4,8},{5,9},{6,10},{7,11},{8,4},{9,5},... | collective-permute-start | bytes 98312 | tf_op jit(solution)/shard_map/ppermute | solution.py:46
  28.6 0.1 collective-permute-start.11
  28.7 1.8 %collective-permute-start.10 = (bf16[128,128]{1,0:T(8,128)(2,1)S(1)}, bf16[128,128]{1,0:T(8,128)(2,1)S(1)}, u32[]{:S(2)}, u32[]{:S(2)}) collective-permute-start(bf16[128,128]{1,0:T(8,128)(2,1)S(1)} %get-tuple-element.49), channel_id=1, source_target_pairs={{0,4},{1,5},{2,6},{3,7},{4,0},{5,1},{6,2},{7,3},{8,12},{9,13},{10,... | collective-permute-start | bytes 98312 | tf_op jit(solution)/shard_map/ppermute | solution.py:46
  30.5 1.5 %collective-permute-done.9 = bf16[128,128]{1,0:T(8,128)(2,1)S(1)} collective-permute-done((bf16[128,128]{1,0:T(8,128)(2,1)S(1)}, bf16[128,128]{1,0:T(8,128)(2,1)S(1)}, u32[]{:S(2)}, u32[]{:S(2)}) %collective-permute-start.9) | collective-permute-done | bytes 32800 | tf_op jit(solution)/shard_map/ppermute | solution.py:46
  32.0 1.8 %collective-permute-done.11 = bf16[128,128]{1,0:T(8,128)(2,1)S(1)} collective-permute-done((bf16[128,128]{1,0:T(8,128)(2,1)S(1)}, bf16[128,128]{1,0:T(8,128)(2,1)S(1)}, u32[]{:S(2)}, u32[]{:S(2)}) %collective-permute-start.11) | collective-permute-done | bytes 32800 | tf_op jit(solution)/shard_map/ppermute | solution.py:46
  33.8 0.6 %fusion.3 = f32[1,128,128]{2,1,0:T(8,128)} fusion(f32[4,128,128]{2,1,0:T(8,128)S(1)} %get-tuple-element.46, bf16[128,128]{1,0:T(8,128)(2,1)S(1)} %collective-permute-done.11, bf16[128,128]{1,0:T(8,128)(2,1)S(1)} %collective-permute-done.10, bf16[128,128]{1,0:T(8,128)(2,1)S(1)} %collective-permute-done.9), kind=kLoop, calls=%fused_computation.7 | loop fusion | flops 98304 | bytes 229376 | tf_op jit(solution)/shard_map/broadcast_in_dim | solution.py:363
  (16 shorter events, 0.2 us)
Async XLA Ops:
  0.0 8.4 %collective-permute-start = (bf16[1,128,128]{2,1,0:T(8,128)(2,1)}, bf16[1,128,128]{2,1,0:T(8,128)(2,1)S(1)}, u32[]{:S(2)}, u32[]{:S(2)}) collective-permute-start(bf16[1,128,128]{2,1,0:T(8,128)(2,1)} %in_ref.2), channel_id=1, source_target_pairs={{0,12},{1,13},{2,14},{3,15},{4,8},{5,9},{6,10},{7,11},{8,4},{9,5},... | collective-permute-start | bytes 98312 | tf_op jit(solution)/shard_map/ppermute | solution.py:46
  5.0 5.0 %collective-permute-start.2 = (bf16[1,128,128]{2,1,0:T(8,128)(2,1)}, bf16[1,128,128]{2,1,0:T(8,128)(2,1)S(1)}, u32[]{:S(2)}, u32[]{:S(2)}) collective-permute-start(bf16[1,128,128]{2,1,0:T(8,128)(2,1)} %in_ref.2), channel_id=1, source_target_pairs={{0,8},{1,9},{2,10},{3,11},{4,12},{5,13},{6,14},{7,15},{8,0},{9,1},... | collective-permute-start | bytes 98312 | tf_op jit(solution)/shard_map/ppermute | solution.py:46
  5.1 5.0 %collective-permute-start.1 = (bf16[1,128,128]{2,1,0:T(8,128)(2,1)}, bf16[1,128,128]{2,1,0:T(8,128)(2,1)S(1)}, u32[]{:S(2)}, u32[]{:S(2)}) collective-permute-start(bf16[1,128,128]{2,1,0:T(8,128)(2,1)} %in_ref.2), channel_id=1, source_target_pairs={{0,4},{1,5},{2,6},{3,7},{4,0},{5,1},{6,2},{7,3},{8,12},{9,13},{10,... | collective-permute-start | bytes 98312 | tf_op jit(solution)/shard_map/ppermute | solution.py:46
  7.0 0.8 %copy-start.2 = (bf16[1,128,128]{2,1,0:T(8,128)(2,1)S(1)}, bf16[1,128,128]{2,1,0:T(8,128)(2,1)}, u32[]{:S(2)}) copy-start(bf16[1,128,128]{2,1,0:T(8,128)(2,1)} %in_ref.2) | copy-start | bytes 98308
  10.1 5.0 %collective-permute-start.3 = (bf16[4,128,128]{2,1,0:T(8,128)(2,1)S(1)}, bf16[4,128,128]{2,1,0:T(8,128)(2,1)S(1)}, u32[]{:S(2)}, u32[]{:S(2)}) collective-permute-start(bf16[4,128,128]{2,1,0:T(8,128)(2,1)S(1)} %pad_maximum_fusion.psi_ref), channel_id=1, source_target_pairs={{0,2},{1,3},{2,0},{3,1},{4,6},{5,7},{6,4},{7,5},{8,10},{9,11},{10,... | collective-permute-start | bytes 393224 | tf_op jit(solution)/shard_map/ppermute | solution.py:46
  11.7 1.0 %copy-start = (bf16[16,128,128]{2,1,0:T(8,128)(2,1)S(1)}, bf16[16,128,128]{2,1,0:T(8,128)(2,1)}, u32[]{:S(2)}) copy-start(bf16[16,128,128]{2,1,0:T(8,128)(2,1)} %in_ref.3) | copy-start | bytes 1572868
  12.7 1.0 %copy-start.1 = (bf16[16,128,128]{2,1,0:T(8,128)(2,1)S(1)}, bf16[16,128,128]{2,1,0:T(8,128)(2,1)}, u32[]{:S(2)}) copy-start(bf16[16,128,128]{2,1,0:T(8,128)(2,1)} %right_ref.1) | copy-start | bytes 1572868
  14.7 1.4 %collective-permute-start.5 = (bf16[4,128,128]{2,1,0:T(8,128)(2,1)S(1)}, bf16[4,128,128]{2,1,0:T(8,128)(2,1)S(1)}, u32[]{:S(2)}, u32[]{:S(2)}) collective-permute-start(bf16[4,128,128]{2,1,0:T(8,128)(2,1)S(1)} %pad_maximum_fusion.psi_ref), channel_id=1, source_target_pairs={{0,1},{1,0},{2,3},{3,2},{4,5},{5,4},{6,7},{7,6},{8,9},{9,8},{10,11... | collective-permute-start | bytes 393224 | tf_op jit(solution)/shard_map/ppermute | solution.py:46
  15.1 1.6 %collective-permute-start.4 = (bf16[4,128,128]{2,1,0:T(8,128)(2,1)S(1)}, bf16[4,128,128]{2,1,0:T(8,128)(2,1)S(1)}, u32[]{:S(2)}, u32[]{:S(2)}) collective-permute-start(bf16[4,128,128]{2,1,0:T(8,128)(2,1)S(1)} %collective-permute-done.3.psi_ref), channel_id=1, source_target_pairs={{0,1},{1,0},{2,3},{3,2},{4,5},{5,4},{6,7},{7,6},{8,9},{9,8},{10,11... | collective-permute-start | bytes 393224 | tf_op jit(solution)/shard_map/ppermute | solution.py:46
  18.5 1.9 %collective-permute-start.6 = (f32[4,128,128]{2,1,0:T(8,128)S(1)}, f32[4,128,128]{2,1,0:T(8,128)S(1)}, u32[]{:S(2)}, u32[]{:S(2)}) collective-permute-start(f32[4,128,128]{2,1,0:T(8,128)S(1)} %get-tuple-element.36), channel_id=1, source_target_pairs={{0,1},{1,0},{2,3},{3,2},{4,5},{5,4},{6,7},{7,6},{8,9},{9,8},{10,11... | collective-permute-start | bytes 786440 | tf_op jit(solution)/shard_map/ppermute | solution.py:46
  20.4 5.6 %collective-permute-start.7 = (bf16[4,128,128]{2,1,0:T(8,128)(2,1)S(1)}, bf16[4,128,128]{2,1,0:T(8,128)(2,1)S(1)}, u32[]{:S(2)}, u32[]{:S(2)}) collective-permute-start(bf16[4,128,128]{2,1,0:T(8,128)(2,1)S(1)} %add_convert_fusion), channel_id=1, source_target_pairs={{0,2},{1,3},{2,0},{3,1},{4,6},{5,7},{6,4},{7,5},{8,10},{9,11},{10,... | collective-permute-start | bytes 393224 | tf_op jit(solution)/shard_map/ppermute | solution.py:46
  23.4 2.6 %collective-permute-start.8 = (f32[4,128,128]{2,1,0:T(8,128)S(1)}, f32[4,128,128]{2,1,0:T(8,128)S(1)}, u32[]{:S(2)}, u32[]{:S(2)}) collective-permute-start(f32[4,128,128]{2,1,0:T(8,128)S(1)} %get-tuple-element.42), channel_id=1, source_target_pairs={{0,1},{1,0},{2,3},{3,2},{4,5},{5,4},{6,7},{7,6},{8,9},{9,8},{10,11... | collective-permute-start | bytes 786440 | tf_op jit(solution)/shard_map/ppermute | solution.py:46
  26.1 6.0 %collective-permute-start.9 = (bf16[128,128]{1,0:T(8,128)(2,1)S(1)}, bf16[128,128]{1,0:T(8,128)(2,1)S(1)}, u32[]{:S(2)}, u32[]{:S(2)}) collective-permute-start(bf16[128,128]{1,0:T(8,128)(2,1)S(1)} %get-tuple-element.47), channel_id=1, source_target_pairs={{0,12},{1,13},{2,14},{3,15},{4,8},{5,9},{6,10},{7,11},{8,4},{9,5},... | collective-permute-start | bytes 98312 | tf_op jit(solution)/shard_map/ppermute | solution.py:46
  28.6 5.2 %collective-permute-start.11 = (bf16[128,128]{1,0:T(8,128)(2,1)S(1)}, bf16[128,128]{1,0:T(8,128)(2,1)S(1)}, u32[]{:S(2)}, u32[]{:S(2)}) collective-permute-start(bf16[128,128]{1,0:T(8,128)(2,1)S(1)} %get-tuple-element.48), channel_id=1, source_target_pairs={{0,8},{1,9},{2,10},{3,11},{4,12},{5,13},{6,14},{7,15},{8,0},{9,1},... | collective-permute-start | bytes 98312 | tf_op jit(solution)/shard_map/ppermute | solution.py:46
  28.7 5.1 %collective-permute-start.10 = (bf16[128,128]{1,0:T(8,128)(2,1)S(1)}, bf16[128,128]{1,0:T(8,128)(2,1)S(1)}, u32[]{:S(2)}, u32[]{:S(2)}) collective-permute-start(bf16[128,128]{1,0:T(8,128)(2,1)S(1)} %get-tuple-element.49), channel_id=1, source_target_pairs={{0,4},{1,5},{2,6},{3,7},{4,0},{5,1},{6,2},{7,3},{8,12},{9,13},{10,... | collective-permute-start | bytes 98312 | tf_op jit(solution)/shard_map/ppermute | solution.py:46

commit v10 on v9

--- a/solution.py
+++ b/solution.py
@@ -48,9 +48,7 @@
 
 def place(sector, me):
     near = sector ^ me
-    along_z = near >> 2
-    spot = jnp.where(along_z == 3, 1, jnp.where(along_z == 0, 0, along_z + 1))
-    return spot | ((near & 2) << 1) | ((near & 1) << 3)
+    return (near >> 2) | ((near & 2) << 1) | ((near & 1) << 3)
 
 
 def order_kernel(nops, coup_ref, out_ref):
@@ -335,7 +333,7 @@
     came = {apart: exchange(psi, apart) for apart in ALONG_Z}
     order = order_slots(left_ops.shape[0], couplings, live)
     four, order = lax.optimization_barrier(
-        (jnp.concatenate([hold(psi), *came.values()], axis=0), order)
+        (jnp.concatenate([hold(psi), came[4], came[8], came[12]], axis=0), order)
     )
     came = exchange(four, ALONG_X)
     left = hold(left_ops)
@@ -358,7 +356,7 @@
     keep, came = lax.optimization_barrier((keep + arrived.astype(jnp.float32), came))
     total = keep + came
     parts = [
-        exchange(total[k + 1].astype(jnp.bfloat16), apart) for k, apart in enumerate(ALONG_Z)
+        exchange(total[apart // 4].astype(jnp.bfloat16), apart) for apart in ALONG_Z
     ]
     return sum((part.astype(jnp.float32) for part in parts), total[0])[None]
 

time: 34.7 us -> 34.8 us (level)
  starting transfers between devices: 13.4 us -> 14.1 us
  Pallas kernels: 9.71 us -> 9.1 us
    ppermute x12, starting transfers between devices: 13.4 us -> 14.1 us  [exchange(): return lax.ppermute(x, 'ops', [(i, i ^ apart) for i in range(OPS)])]
    pallas_call x4, Pallas kernels: 6.73 us -> 6.12 us  [terms(): pl.pallas_call(kernel, out_shape=[jax.ShapeDtypeStruct(blocks.shape, bloc...]
  transfers between devices with their start and end apart: 12 -> 12, of which waited for: 6 -> 8; matrix products, arithmetic and copies ran while one was open for 2% -> 2% of each run, Pallas kernels for 23% -> 22%
where the time goes in v10:
time: 34.8 us; the launch traced here: 34.3 us
  starting transfers between devices  14.1 us (41%)
  Pallas kernels  9.1 us (26%)
  waiting for transfers between devices  5.97 us (17%)
  local copies, waits for them, and re-layouts  2.84 us (8%)
  other arithmetic  1.46 us (4%)
  between operations  0.82 us (2%)
    ppermute x12, starting transfers between devices, exchange(): return lax.ppermute(x, 'ops', [(i, i ^ apart) for i in range(OPS)])  14.1 us
    pallas_call x4, Pallas kernels, terms(): pl.pallas_call(kernel, out_shape=[jax.ShapeDtypeStruct(blocks.shape, bloc...  6.12 us
    ppermute x12, waiting for transfers between devices, exchange(): return lax.ppermute(x, 'ops', [(i, i ^ apart) for i in range(OPS)])  5.97 us
    unnamed x6, local copies, waits for them, and re-layouts  2.84 us
    pallas_call x2, Pallas kernels, more(): pl.pallas_call(kernel, out_shape=jax.ShapeDtypeStruct(blocks.shape, block...  1.38 us
    concatenate x1, other arithmetic, order_slots(): jnp.concatenate([couplings, jnp.pad(live[None], ((0, 0), (0, slots - 1)))...  0.7 us
    pallas_call x1, Pallas kernels, order_slots(): pl.pallas_call(lambda *refs: order_kernel(nops, *refs), out_shape=jax.Sha...  0.7 us
  transfers between devices with their start and end apart: 12, of which 8 were waited for; matrix products, arithmetic and copies ran while one was open for 2% of the time, Pallas kernels for 22%

profile of v10, /device:TPU:0, one launch (start us, length us, event | category | flops | bytes accessed | tf_op | source)
XLA Modules:
  0.0 34.3 jit_solution(8580776158616386915)
XLA Ops:
  0.0 3.0 %collective-permute-start = (bf16[1,128,128]{2,1,0:T(8,128)(2,1)}, bf16[1,128,128]{2,1,0:T(8,128)(2,1)S(1)}, u32[]{:S(2)}, u32[]{:S(2)}) collective-permute-start(bf16[1,128,128]{2,1,0:T(8,128)(2,1)} %in_ref.2), channel_id=1, source_target_pairs={{0,4},{1,5},{2,6},{3,7},{4,0},{5,1},{6,2},{7,3},{8,12},{9,13},{10,... | collective-permute-start | bytes 98312 | tf_op jit(solution)/shard_map/ppermute | solution.py:46
  3.0 2.5 %collective-permute-start.2 = (bf16[1,128,128]{2,1,0:T(8,128)(2,1)}, bf16[1,128,128]{2,1,0:T(8,128)(2,1)S(1)}, u32[]{:S(2)}, u32[]{:S(2)}) collective-permute-start(bf16[1,128,128]{2,1,0:T(8,128)(2,1)} %in_ref.2), channel_id=1, source_target_pairs={{0,12},{1,13},{2,14},{3,15},{4,8},{5,9},{6,10},{7,11},{8,4},{9,5},... | collective-permute-start | bytes 98312 | tf_op jit(solution)/shard_map/ppermute | solution.py:46
  5.5 0.1 collective-permute-start.1
  6.3 0.7 %pad_add_fusion.refs_0_ = s32[4,384]{1,0:T(4,128)S(1)} fusion(s32[1,1]{1,0:T(1,128)} %bitcast.19, s32[3,384]{1,0:T(4,128)} %param.8), kind=kLoop, calls=%fused_computation.11 | loop fusion | flops 1536 | bytes 10756 | tf_op jit(solution)/shard_map/concatenate | solution.py:104
  7.0 0.8 %copy-done.2 = bf16[1,128,128]{2,1,0:T(8,128)(2,1)S(1)} copy-done((bf16[1,128,128]{2,1,0:T(8,128)(2,1)S(1)}, bf16[1,128,128]{2,1,0:T(8,128)(2,1)}, u32[]{:S(2)}) %copy-start.2) | copy-done | bytes 32792
  7.7 0.7 %order.1.order_in = s32[1,1024]{1,0:T(1,128)S(1)} custom-call(s32[4,384]{1,0:T(4,128)S(1)} %pad_add_fusion.refs_0_), custom_call_target="tpu_custom_call" | custom-call | bytes 65536 | tf_op jit(solution)/shard_map/order/pallas_call | solution.py:105
  8.4 0.9 %collective-permute-done.2 = bf16[1,128,128]{2,1,0:T(8,128)(2,1)S(1)} collective-permute-done((bf16[1,128,128]{2,1,0:T(8,128)(2,1)}, bf16[1,128,128]{2,1,0:T(8,128)(2,1)S(1)}, u32[]{:S(2)}, u32[]{:S(2)}) %collective-permute-start.2) | collective-permute-done | bytes 32800 | tf_op jit(solution)/shard_map/ppermute | solution.py:46
  9.4 1.5 %collective-permute-done.1 = bf16[1,128,128]{2,1,0:T(8,128)(2,1)S(1)} collective-permute-done((bf16[1,128,128]{2,1,0:T(8,128)(2,1)}, bf16[1,128,128]{2,1,0:T(8,128)(2,1)S(1)}, u32[]{:S(2)}, u32[]{:S(2)}) %collective-permute-start.1) | collective-permute-done | bytes 32800 | tf_op jit(solution)/shard_map/ppermute | solution.py:46
  10.9 1.6 %collective-permute-start.3 = (bf16[4,128,128]{2,1,0:T(8,128)(2,1)S(1)}, bf16[4,128,128]{2,1,0:T(8,128)(2,1)S(1)}, u32[]{:S(2)}, u32[]{:S(2)}) collective-permute-start(bf16[4,128,128]{2,1,0:T(8,128)(2,1)S(1)} %pad_maximum_fusion.psi_ref), channel_id=1, source_target_pairs={{0,2},{1,3},{2,0},{3,1},{4,6},{5,7},{6,4},{7,5},{8,10},{9,11},{10,... | collective-permute-start | bytes 393224 | tf_op jit(solution)/shard_map/ppermute | solution.py:46
  12.5 1.0 %copy-done = bf16[16,128,128]{2,1,0:T(8,128)(2,1)S(1)} copy-done((bf16[16,128,128]{2,1,0:T(8,128)(2,1)S(1)}, bf16[16,128,128]{2,1,0:T(8,128)(2,1)}, u32[]{:S(2)}) %copy-start) | copy-done | bytes 524312
  13.5 1.0 %copy-done.1 = bf16[16,128,128]{2,1,0:T(8,128)(2,1)S(1)} copy-done((bf16[16,128,128]{2,1,0:T(8,128)(2,1)S(1)}, bf16[16,128,128]{2,1,0:T(8,128)(2,1)}, u32[]{:S(2)}) %copy-start.1) | copy-done | bytes 524312
  14.6 0.2 turn.1.turned_ref
  14.8 0.7 %early.1._ = bf16[449,128,128]{2,1,0:T(8,128)(2,1)S(1)} custom-call(bf16[4,128,128]{2,1,0:T(8,128)(2,1)S(1)} %pad_maximum_fusion.psi_ref, bf16[16,128,128]{2,1,0:T(8,128)(2,1)S(1)} %hold.3.left_ref.refs_1_), custom_call_target="tpu_custom_call" | custom-call | bytes 65536 | tf_op jit(solution)/shard_map/early/pallas_call | solution.py:242
  15.5 0.4 %collective-permute-done.3.psi_ref = bf16[4,128,128]{2,1,0:T(8,128)(2,1)S(1)} collective-permute-done((bf16[4,128,128]{2,1,0:T(8,128)(2,1)S(1)}, bf16[4,128,128]{2,1,0:T(8,128)(2,1)S(1)}, u32[]{:S(2)}, u32[]{:S(2)}) %collective-permute-start.3) | collective-permute-done | bytes 131104 | tf_op jit(solution)/shard_map/ppermute | solution.py:46
  15.9 0.1 collective-permute-start.4
  16.0 0.7 %more.2._ = bf16[449,128,128]{2,1,0:T(8,128)(2,1)S(1)} custom-call(bf16[4,128,128]{2,1,0:T(8,128)(2,1)S(1)} %collective-permute-done.3.psi_ref, bf16[16,128,128]{2,1,0:T(8,128)(2,1)S(1)} %hold.3.left_ref.refs_1_, bf16[449,128,128]{2,1,0:T(8,128)(2,1)S(1)} %early.1._), custom_call_target="tpu_custom_call", output_to_operand_aliasing={{}: (2, {})} | custom-call | bytes 65536 | tf_op jit(solution)/shard_map/more/pallas_call | solution.py:259
  16.7 0.1 collective-permute-done.5.psi_ref
  16.9 0.7 %more.3.refs_2_ = bf16[449,128,128]{2,1,0:T(8,128)(2,1)S(1)} custom-call(bf16[4,128,128]{2,1,0:T(8,128)(2,1)S(1)} %collective-permute-done.5.psi_ref, bf16[16,128,128]{2,1,0:T(8,128)(2,1)S(1)} %hold.3.left_ref.refs_1_, bf16[449,128,128]{2,1,0:T(8,128)(2,1)S(1)} %more.2._), custom_call_target="tpu_custom_call", output_to_operand_aliasing={{}: (2, {})} | custom-call | bytes 65536 | tf_op jit(solution)/shard_map/more/pallas_call | solution.py:259
  17.6 1.6 %terms_0.1 = (bf16[449,128,128]{2,1,0:T(8,128)(2,1)S(1)}, f32[4,128,128]{2,1,0:T(8,128)S(1)}) custom-call(s32[1,1024]{1,0:T(1,128)S(1)} %order.1.order_in, bf16[2048,128]{1,0:T(8,128)(2,1)S(1)} %turn.1.turned_ref, bf16[4,128,128]{2,1,0:T(8,128)(2,1)S(1)} %collective-permute-done.4.refs_0_, ...), custom_call_target="tpu_custom_call", output_to_operand_aliasing={{0}: (4, {})} | custom-call | bytes 65536 | tf_op jit(solution)/shard_map/terms_0/pallas_call | solution.py:294
  19.2 0.2 collective-permute-start.6
  19.4 1.5 %terms_1.1 = (bf16[449,128,128]{2,1,0:T(8,128)(2,1)S(1)}, f32[4,128,128]{2,1,0:T(8,128)S(1)}) custom-call(s32[1,1024]{1,0:T(1,128)S(1)} %order.1.order_in, bf16[2048,128]{1,0:T(8,128)(2,1)S(1)} %turn.1.turned_ref, bf16[449,128,128]{2,1,0:T(8,128)(2,1)S(1)} %get-tuple-element.34.refs_0_), custom_call_target="tpu_custom_call", output_to_operand_aliasing={{0}: (2, {})} | custom-call | bytes 65536 | tf_op jit(solution)/shard_map/terms_1/pallas_call | solution.py:294
  21.0 2.0 %collective-permute-start.7 = (bf16[4,128,128]{2,1,0:T(8,128)(2,1)S(1)}, bf16[4,128,128]{2,1,0:T(8,128)(2,1)S(1)}, u32[]{:S(2)}, u32[]{:S(2)}) collective-permute-start(bf16[4,128,128]{2,1,0:T(8,128)(2,1)S(1)} %add_convert_fusion), channel_id=1, source_target_pairs={{0,2},{1,3},{2,0},{3,1},{4,6},{5,7},{6,4},{7,5},{8,10},{9,11},{10,... | collective-permute-start | bytes 393224 | tf_op jit(solution)/shard_map/ppermute | solution.py:46
  22.9 1.4 %terms_2.1 = (bf16[449,128,128]{2,1,0:T(8,128)(2,1)S(1)}, f32[4,128,128]{2,1,0:T(8,128)S(1)}) custom-call(s32[1,1024]{1,0:T(1,128)S(1)} %order.1.order_in, bf16[2048,128]{1,0:T(8,128)(2,1)S(1)} %turn.1.turned_ref, bf16[449,128,128]{2,1,0:T(8,128)(2,1)S(1)} %get-tuple-element.38.refs_0_), custom_call_target="tpu_custom_call", output_to_operand_aliasing={{0}: (2, {})} | custom-call | bytes 65536 | tf_op jit(solution)/shard_map/terms_2/pallas_call | solution.py:294
  24.4 1.6 %terms_3.1 = (bf16[449,128,128]{2,1,0:T(8,128)(2,1)S(1)}, f32[4,128,128]{2,1,0:T(8,128)S(1)}) custom-call(s32[1,1024]{1,0:T(1,128)S(1)} %order.1.order_in, bf16[2048,128]{1,0:T(8,128)(2,1)S(1)} %turn.1.turned_ref, bf16[449,128,128]{2,1,0:T(8,128)(2,1)S(1)} %get-tuple-element.39.refs_0_), custom_call_target="tpu_custom_call", output_to_operand_aliasing={{0}: (2, {})} | custom-call | bytes 65536 | tf_op jit(solution)/shard_map/terms_3/pallas_call | solution.py:294
  26.0 0.6 %collective-permute-done.7 = bf16[4,128,128]{2,1,0:T(8,128)(2,1)S(1)} collective-permute-done((bf16[4,128,128]{2,1,0:T(8,128)(2,1)S(1)}, bf16[4,128,128]{2,1,0:T(8,128)(2,1)S(1)}, u32[]{:S(2)}, u32[]{:S(2)}) %collective-permute-start.7) | collective-permute-done | bytes 131104 | tf_op jit(solution)/shard_map/ppermute | solution.py:46
  26.7 1.7 %collective-permute-start.9 = (bf16[128,128]{1,0:T(8,128)(2,1)S(1)}, bf16[128,128]{1,0:T(8,128)(2,1)S(1)}, u32[]{:S(2)}, u32[]{:S(2)}) collective-permute-start(bf16[128,128]{1,0:T(8,128)(2,1)S(1)} %get-tuple-element.47), channel_id=1, source_target_pairs={{0,12},{1,13},{2,14},{3,15},{4,8},{5,9},{6,10},{7,11},{8,4},{9,5},... | collective-permute-start | bytes 98312 | tf_op jit(solution)/shard_map/ppermute | solution.py:46
  28.4 1.0 %collective-permute-start.11 = (bf16[128,128]{1,0:T(8,128)(2,1)S(1)}, bf16[128,128]{1,0:T(8,128)(2,1)S(1)}, u32[]{:S(2)}, u32[]{:S(2)}) collective-permute-start(bf16[128,128]{1,0:T(8,128)(2,1)S(1)} %get-tuple-element.48), channel_id=1, source_target_pairs={{0,8},{1,9},{2,10},{3,11},{4,12},{5,13},{6,14},{7,15},{8,0},{9,1},... | collective-permute-start | bytes 98312 | tf_op jit(solution)/shard_map/ppermute | solution.py:46
  29.4 1.8 %collective-permute-start.10 = (bf16[128,128]{1,0:T(8,128)(2,1)S(1)}, bf16[128,128]{1,0:T(8,128)(2,1)S(1)}, u32[]{:S(2)}, u32[]{:S(2)}) collective-permute-start(bf16[128,128]{1,0:T(8,128)(2,1)S(1)} %get-tuple-element.49), channel_id=1, source_target_pairs={{0,4},{1,5},{2,6},{3,7},{4,0},{5,1},{6,2},{7,3},{8,12},{9,13},{10,... | collective-permute-start | bytes 98312 | tf_op jit(solution)/shard_map/ppermute | solution.py:46
  31.2 1.4 %collective-permute-done.9 = bf16[128,128]{1,0:T(8,128)(2,1)S(1)} collective-permute-done((bf16[128,128]{1,0:T(8,128)(2,1)S(1)}, bf16[128,128]{1,0:T(8,128)(2,1)S(1)}, u32[]{:S(2)}, u32[]{:S(2)}) %collective-permute-start.9) | collective-permute-done | bytes 32800 | tf_op jit(solution)/shard_map/ppermute | solution.py:46
  32.6 0.8 %collective-permute-done.11 = bf16[128,128]{1,0:T(8,128)(2,1)S(1)} collective-permute-done((bf16[128,128]{1,0:T(8,128)(2,1)S(1)}, bf16[128,128]{1,0:T(8,128)(2,1)S(1)}, u32[]{:S(2)}, u32[]{:S(2)}) %collective-permute-start.11) | collective-permute-done | bytes 32800 | tf_op jit(solution)/shard_map/ppermute | solution.py:46
  33.4 0.2 collective-permute-done.10
  33.6 0.6 %fusion.3 = f32[1,128,128]{2,1,0:T(8,128)} fusion(f32[4,128,128]{2,1,0:T(8,128)S(1)} %get-tuple-element.46, bf16[128,128]{1,0:T(8,128)(2,1)S(1)} %collective-permute-done.11, bf16[128,128]{1,0:T(8,128)(2,1)S(1)} %collective-permute-done.10, bf16[128,128]{1,0:T(8,128)(2,1)S(1)} %collective-permute-done.9), kind=kLoop, calls=%fused_computation.7 | loop fusion | flops 98304 | bytes 229376 | tf_op jit(solution)/shard_map/broadcast_in_dim | solution.py:361
  (16 shorter events, 0.3 us)
Async XLA Ops:
  0.0 8.4 %collective-permute-start = (bf16[1,128,128]{2,1,0:T(8,128)(2,1)}, bf16[1,128,128]{2,1,0:T(8,128)(2,1)S(1)}, u32[]{:S(2)}, u32[]{:S(2)}) collective-permute-start(bf16[1,128,128]{2,1,0:T(8,128)(2,1)} %in_ref.2), channel_id=1, source_target_pairs={{0,4},{1,5},{2,6},{3,7},{4,0},{5,1},{6,2},{7,3},{8,12},{9,13},{10,... | collective-permute-start | bytes 98312 | tf_op jit(solution)/shard_map/ppermute | solution.py:46
  3.0 6.4 %collective-permute-start.2 = (bf16[1,128,128]{2,1,0:T(8,128)(2,1)}, bf16[1,128,128]{2,1,0:T(8,128)(2,1)S(1)}, u32[]{:S(2)}, u32[]{:S(2)}) collective-permute-start(bf16[1,128,128]{2,1,0:T(8,128)(2,1)} %in_ref.2), channel_id=1, source_target_pairs={{0,12},{1,13},{2,14},{3,15},{4,8},{5,9},{6,10},{7,11},{8,4},{9,5},... | collective-permute-start | bytes 98312 | tf_op jit(solution)/shard_map/ppermute | solution.py:46
  5.5 5.4 %collective-permute-start.1 = (bf16[1,128,128]{2,1,0:T(8,128)(2,1)}, bf16[1,128,128]{2,1,0:T(8,128)(2,1)S(1)}, u32[]{:S(2)}, u32[]{:S(2)}) collective-permute-start(bf16[1,128,128]{2,1,0:T(8,128)(2,1)} %in_ref.2), channel_id=1, source_target_pairs={{0,8},{1,9},{2,10},{3,11},{4,12},{5,13},{6,14},{7,15},{8,0},{9,1},... | collective-permute-start | bytes 98312 | tf_op jit(solution)/shard_map/ppermute | solution.py:46
  7.0 0.8 %copy-start.2 = (bf16[1,128,128]{2,1,0:T(8,128)(2,1)S(1)}, bf16[1,128,128]{2,1,0:T(8,128)(2,1)}, u32[]{:S(2)}) copy-start(bf16[1,128,128]{2,1,0:T(8,128)(2,1)} %in_ref.2) | copy-start | bytes 98308
  10.9 5.0 %collective-permute-start.3 = (bf16[4,128,128]{2,1,0:T(8,128)(2,1)S(1)}, bf16[4,128,128]{2,1,0:T(8,128)(2,1)S(1)}, u32[]{:S(2)}, u32[]{:S(2)}) collective-permute-start(bf16[4,128,128]{2,1,0:T(8,128)(2,1)S(1)} %pad_maximum_fusion.psi_ref), channel_id=1, source_target_pairs={{0,2},{1,3},{2,0},{3,1},{4,6},{5,7},{6,4},{7,5},{8,10},{9,11},{10,... | collective-permute-start | bytes 393224 | tf_op jit(solution)/shard_map/ppermute | solution.py:46
  12.5 1.0 %copy-start = (bf16[16,128,128]{2,1,0:T(8,128)(2,1)S(1)}, bf16[16,128,128]{2,1,0:T(8,128)(2,1)}, u32[]{:S(2)}) copy-start(bf16[16,128,128]{2,1,0:T(8,128)(2,1)} %in_ref.3) | copy-start | bytes 1572868
  13.5 1.0 %copy-start.1 = (bf16[16,128,128]{2,1,0:T(8,128)(2,1)S(1)}, bf16[16,128,128]{2,1,0:T(8,128)(2,1)}, u32[]{:S(2)}) copy-start(bf16[16,128,128]{2,1,0:T(8,128)(2,1)} %right_ref.1) | copy-start | bytes 1572868
  15.5 1.4 %collective-permute-start.5 = (bf16[4,128,128]{2,1,0:T(8,128)(2,1)S(1)}, bf16[4,128,128]{2,1,0:T(8,128)(2,1)S(1)}, u32[]{:S(2)}, u32[]{:S(2)}) collective-permute-start(bf16[4,128,128]{2,1,0:T(8,128)(2,1)S(1)} %pad_maximum_fusion.psi_ref), channel_id=1, source_target_pairs={{0,1},{1,0},{2,3},{3,2},{4,5},{5,4},{6,7},{7,6},{8,9},{9,8},{10,11... | collective-permute-start | bytes 393224 | tf_op jit(solution)/shard_map/ppermute | solution.py:46
  15.9 1.7 %collective-permute-start.4 = (bf16[4,128,128]{2,1,0:T(8,128)(2,1)S(1)}, bf16[4,128,128]{2,1,0:T(8,128)(2,1)S(1)}, u32[]{:S(2)}, u32[]{:S(2)}) collective-permute-start(bf16[4,128,128]{2,1,0:T(8,128)(2,1)S(1)} %collective-permute-done.3.psi_ref), channel_id=1, source_target_pairs={{0,1},{1,0},{2,3},{3,2},{4,5},{5,4},{6,7},{7,6},{8,9},{9,8},{10,11... | collective-permute-start | bytes 393224 | tf_op jit(solution)/shard_map/ppermute | solution.py:46
  19.2 1.8 %collective-permute-start.6 = (f32[4,128,128]{2,1,0:T(8,128)S(1)}, f32[4,128,128]{2,1,0:T(8,128)S(1)}, u32[]{:S(2)}, u32[]{:S(2)}) collective-permute-start(f32[4,128,128]{2,1,0:T(8,128)S(1)} %get-tuple-element.36), channel_id=1, source_target_pairs={{0,1},{1,0},{2,3},{3,2},{4,5},{5,4},{6,7},{7,6},{8,9},{9,8},{10,11... | collective-permute-start | bytes 786440 | tf_op jit(solution)/shard_map/ppermute | solution.py:46
  21.0 5.7 %collective-permute-start.7 = (bf16[4,128,128]{2,1,0:T(8,128)(2,1)S(1)}, bf16[4,128,128]{2,1,0:T(8,128)(2,1)S(1)}, u32[]{:S(2)}, u32[]{:S(2)}) collective-permute-start(bf16[4,128,128]{2,1,0:T(8,128)(2,1)S(1)} %add_convert_fusion), channel_id=1, source_target_pairs={{0,2},{1,3},{2,0},{3,1},{4,6},{5,7},{6,4},{7,5},{8,10},{9,11},{10,... | collective-permute-start | bytes 393224 | tf_op jit(solution)/shard_map/ppermute | solution.py:46
  24.4 2.3 %collective-permute-start.8 = (f32[4,128,128]{2,1,0:T(8,128)S(1)}, f32[4,128,128]{2,1,0:T(8,128)S(1)}, u32[]{:S(2)}, u32[]{:S(2)}) collective-permute-start(f32[4,128,128]{2,1,0:T(8,128)S(1)} %get-tuple-element.42), channel_id=1, source_target_pairs={{0,1},{1,0},{2,3},{3,2},{4,5},{5,4},{6,7},{7,6},{8,9},{9,8},{10,11... | collective-permute-start | bytes 786440 | tf_op jit(solution)/shard_map/ppermute | solution.py:46
  26.7 5.9 %collective-permute-start.9 = (bf16[128,128]{1,0:T(8,128)(2,1)S(1)}, bf16[128,128]{1,0:T(8,128)(2,1)S(1)}, u32[]{:S(2)}, u32[]{:S(2)}) collective-permute-start(bf16[128,128]{1,0:T(8,128)(2,1)S(1)} %get-tuple-element.47), channel_id=1, source_target_pairs={{0,12},{1,13},{2,14},{3,15},{4,8},{5,9},{6,10},{7,11},{8,4},{9,5},... | collective-permute-start | bytes 98312 | tf_op jit(solution)/shard_map/ppermute | solution.py:46
  28.4 5.0 %collective-permute-start.11 = (bf16[128,128]{1,0:T(8,128)(2,1)S(1)}, bf16[128,128]{1,0:T(8,128)(2,1)S(1)}, u32[]{:S(2)}, u32[]{:S(2)}) collective-permute-start(bf16[128,128]{1,0:T(8,128)(2,1)S(1)} %get-tuple-element.48), channel_id=1, source_target_pairs={{0,8},{1,9},{2,10},{3,11},{4,12},{5,13},{6,14},{7,15},{8,0},{9,1},... | collective-permute-start | bytes 98312 | tf_op jit(solution)/shard_map/ppermute | solution.py:46
  29.4 4.2 %collective-permute-start.10 = (bf16[128,128]{1,0:T(8,128)(2,1)S(1)}, bf16[128,128]{1,0:T(8,128)(2,1)S(1)}, u32[]{:S(2)}, u32[]{:S(2)}) collective-permute-start(bf16[128,128]{1,0:T(8,128)(2,1)S(1)} %get-tuple-element.49), channel_id=1, source_target_pairs={{0,4},{1,5},{2,6},{3,7},{4,0},{5,1},{6,2},{7,3},{8,12},{9,13},{10,... | collective-permute-start | bytes 98312 | tf_op jit(solution)/shard_map/ppermute | solution.py:46

commit v11 on v9

--- a/solution.py
+++ b/solution.py
@@ -202,7 +202,8 @@
 
 def multiply(order, block_ref, turned_ref, out_ref, offset, nops):
     half, m, _ = out_ref.shape
-    for t in range(0, half, 2):
+    step = 4
+    for t in range(0, half, step):
         rows = [
             jnp.concatenate(
                 [
@@ -211,12 +212,12 @@
                 ],
                 axis=1,
             )
-            for i in range(2)
+            for i in range(step)
         ]
         out = jnp.dot(
             jnp.concatenate(rows, axis=0), turned_ref[...], preferred_element_type=jnp.float32
         )
-        out_ref[t : t + 2] = out.reshape(2, m, m)
+        out_ref[t : t + step] = out.reshape(step, m, m)
 
 
 def fill(psi_ref, left_ref, block_ref, offset):

time: 34.7 us -> 35.3 us (1.017)
  Pallas kernels: 9.71 us -> 10.1 us
    pallas_call x4, Pallas kernels: 6.73 us -> 7.09 us  [terms(): pl.pallas_call(kernel, out_shape=[jax.ShapeDtypeStruct(blocks.shape, bloc...]
  transfers between devices with their start and end apart: 12 -> 12, of which waited for: 6 -> 6; matrix products, arithmetic and copies ran while one was open for 2% -> 2% of each run, Pallas kernels for 23% -> 22%
where the time goes in v11:
time: 35.3 us; the launch traced here: 35.1 us
  starting transfers between devices  13.6 us (39%)
  Pallas kernels  10.1 us (29%)
  waiting for transfers between devices  6.32 us (18%)
  local copies, waits for them, and re-layouts  2.84 us (8%)
  other arithmetic  1.46 us (4%)
  between operations  0.82 us (2%)
    ppermute x12, starting transfers between devices, exchange(): return lax.ppermute(x, 'ops', [(i, i ^ apart) for i in range(OPS)])  13.6 us
    pallas_call x4, Pallas kernels, terms(): pl.pallas_call(kernel, out_shape=[jax.ShapeDtypeStruct(blocks.shape, bloc...  7.09 us
    ppermute x12, waiting for transfers between devices, exchange(): return lax.ppermute(x, 'ops', [(i, i ^ apart) for i in range(OPS)])  6.32 us
    unnamed x6, local copies, waits for them, and re-layouts  2.84 us
    pallas_call x2, Pallas kernels, more(): pl.pallas_call(kernel, out_shape=jax.ShapeDtypeStruct(blocks.shape, block...  1.37 us
  transfers between devices with their start and end apart: 12, of which 6 were waited for; matrix products, arithmetic and copies ran while one was open for 2% of the time, Pallas kernels for 22%

profile of v11, /device:TPU:0, one launch (start us, length us, event | category | flops | bytes accessed | tf_op | source)
XLA Modules:
  0.0 35.1 jit_solution(11563213555274127426)
XLA Ops:
  0.0 5.0 %collective-permute-start = (bf16[1,128,128]{2,1,0:T(8,128)(2,1)}, bf16[1,128,128]{2,1,0:T(8,128)(2,1)S(1)}, u32[]{:S(2)}, u32[]{:S(2)}) collective-permute-start(bf16[1,128,128]{2,1,0:T(8,128)(2,1)} %in_ref.2), channel_id=1, source_target_pairs={{0,12},{1,13},{2,14},{3,15},{4,8},{5,9},{6,10},{7,11},{8,4},{9,5},... | collective-permute-start | bytes 98312 | tf_op jit(solution)/shard_map/ppermute | solution.py:46
  5.0 0.0 collective-permute-start.2
  5.1 0.6 %collective-permute-start.1 = (bf16[1,128,128]{2,1,0:T(8,128)(2,1)}, bf16[1,128,128]{2,1,0:T(8,128)(2,1)S(1)}, u32[]{:S(2)}, u32[]{:S(2)}) collective-permute-start(bf16[1,128,128]{2,1,0:T(8,128)(2,1)} %in_ref.2), channel_id=1, source_target_pairs={{0,4},{1,5},{2,6},{3,7},{4,0},{5,1},{6,2},{7,3},{8,12},{9,13},{10,... | collective-permute-start | bytes 98312 | tf_op jit(solution)/shard_map/ppermute | solution.py:46
  6.3 0.7 %pad_add_fusion.refs_0_ = s32[4,384]{1,0:T(4,128)S(1)} fusion(s32[1,1]{1,0:T(1,128)} %bitcast.19, s32[3,384]{1,0:T(4,128)} %param.8), kind=kLoop, calls=%fused_computation.11 | loop fusion | flops 1536 | bytes 10756 | tf_op jit(solution)/shard_map/concatenate | solution.py:106
  7.0 0.8 %copy-done.2 = bf16[1,128,128]{2,1,0:T(8,128)(2,1)S(1)} copy-done((bf16[1,128,128]{2,1,0:T(8,128)(2,1)S(1)}, bf16[1,128,128]{2,1,0:T(8,128)(2,1)}, u32[]{:S(2)}) %copy-start.2) | copy-done | bytes 32792
  7.7 0.7 %order.1.order_in = s32[1,1024]{1,0:T(1,128)S(1)} custom-call(s32[4,384]{1,0:T(4,128)S(1)} %pad_add_fusion.refs_0_), custom_call_target="tpu_custom_call" | custom-call | bytes 65536 | tf_op jit(solution)/shard_map/order/pallas_call | solution.py:107
  8.4 1.6 %collective-permute-done.2 = bf16[1,128,128]{2,1,0:T(8,128)(2,1)S(1)} collective-permute-done((bf16[1,128,128]{2,1,0:T(8,128)(2,1)}, bf16[1,128,128]{2,1,0:T(8,128)(2,1)S(1)}, u32[]{:S(2)}, u32[]{:S(2)}) %collective-permute-start.2) | collective-permute-done | bytes 32800 | tf_op jit(solution)/shard_map/ppermute | solution.py:46
  10.1 1.6 %collective-permute-start.3 = (bf16[4,128,128]{2,1,0:T(8,128)(2,1)S(1)}, bf16[4,128,128]{2,1,0:T(8,128)(2,1)S(1)}, u32[]{:S(2)}, u32[]{:S(2)}) collective-permute-start(bf16[4,128,128]{2,1,0:T(8,128)(2,1)S(1)} %pad_maximum_fusion.psi_ref), channel_id=1, source_target_pairs={{0,2},{1,3},{2,0},{3,1},{4,6},{5,7},{6,4},{7,5},{8,10},{9,11},{10,... | collective-permute-start | bytes 393224 | tf_op jit(solution)/shard_map/ppermute | solution.py:46
  11.7 1.0 %copy-done = bf16[16,128,128]{2,1,0:T(8,128)(2,1)S(1)} copy-done((bf16[16,128,128]{2,1,0:T(8,128)(2,1)S(1)}, bf16[16,128,128]{2,1,0:T(8,128)(2,1)}, u32[]{:S(2)}) %copy-start) | copy-done | bytes 524312
  12.7 0.0 copy-start.1
  12.8 1.0 %copy-done.1 = bf16[16,128,128]{2,1,0:T(8,128)(2,1)S(1)} copy-done((bf16[16,128,128]{2,1,0:T(8,128)(2,1)S(1)}, bf16[16,128,128]{2,1,0:T(8,128)(2,1)}, u32[]{:S(2)}) %copy-start.1) | copy-done | bytes 524312
  13.8 0.2 turn.1.turned_ref
  14.0 0.7 %early.1._ = bf16[449,128,128]{2,1,0:T(8,128)(2,1)S(1)} custom-call(bf16[4,128,128]{2,1,0:T(8,128)(2,1)S(1)} %pad_maximum_fusion.psi_ref, bf16[16,128,128]{2,1,0:T(8,128)(2,1)S(1)} %hold.3.left_ref.refs_1_), custom_call_target="tpu_custom_call" | custom-call | bytes 65536 | tf_op jit(solution)/shard_map/early/pallas_call | solution.py:245
  14.7 0.1 collective-permute-start.5
  14.8 0.4 %collective-permute-done.3.psi_ref = bf16[4,128,128]{2,1,0:T(8,128)(2,1)S(1)} collective-permute-done((bf16[4,128,128]{2,1,0:T(8,128)(2,1)S(1)}, bf16[4,128,128]{2,1,0:T(8,128)(2,1)S(1)}, u32[]{:S(2)}, u32[]{:S(2)}) %collective-permute-start.3) | collective-permute-done | bytes 131104 | tf_op jit(solution)/shard_map/ppermute | solution.py:46
  15.1 0.1 collective-permute-start.4
  15.3 0.7 %more.2._ = bf16[449,128,128]{2,1,0:T(8,128)(2,1)S(1)} custom-call(bf16[4,128,128]{2,1,0:T(8,128)(2,1)S(1)} %collective-permute-done.3.psi_ref, bf16[16,128,128]{2,1,0:T(8,128)(2,1)S(1)} %hold.3.left_ref.refs_1_, bf16[449,128,128]{2,1,0:T(8,128)(2,1)S(1)} %early.1._), custom_call_target="tpu_custom_call", output_to_operand_aliasing={{}: (2, {})} | custom-call | bytes 65536 | tf_op jit(solution)/shard_map/more/pallas_call | solution.py:262
  15.9 0.1 collective-permute-done.5.psi_ref
  16.1 0.7 %more.3.refs_2_ = bf16[449,128,128]{2,1,0:T(8,128)(2,1)S(1)} custom-call(bf16[4,128,128]{2,1,0:T(8,128)(2,1)S(1)} %collective-permute-done.5.psi_ref, bf16[16,128,128]{2,1,0:T(8,128)(2,1)S(1)} %hold.3.left_ref.refs_1_, bf16[449,128,128]{2,1,0:T(8,128)(2,1)S(1)} %more.2._), custom_call_target="tpu_custom_call", output_to_operand_aliasing={{}: (2, {})} | custom-call | bytes 65536 | tf_op jit(solution)/shard_map/more/pallas_call | solution.py:262
  16.8 2.4 %terms_0.1 = (bf16[449,128,128]{2,1,0:T(8,128)(2,1)S(1)}, f32[4,128,128]{2,1,0:T(8,128)S(1)}) custom-call(s32[1,1024]{1,0:T(1,128)S(1)} %order.1.order_in, bf16[2048,128]{1,0:T(8,128)(2,1)S(1)} %turn.1.turned_ref, bf16[4,128,128]{2,1,0:T(8,128)(2,1)S(1)} %collective-permute-done.4.refs_0_, ...), custom_call_target="tpu_custom_call", output_to_operand_aliasing={{0}: (4, {})} | custom-call | bytes 65536 | tf_op jit(solution)/shard_map/terms_0/pallas_call | solution.py:297
  19.2 0.3 collective-permute-start.6
  19.5 1.6 %terms_1.1 = (bf16[449,128,128]{2,1,0:T(8,128)(2,1)S(1)}, f32[4,128,128]{2,1,0:T(8,128)S(1)}) custom-call(s32[1,1024]{1,0:T(1,128)S(1)} %order.1.order_in, bf16[2048,128]{1,0:T(8,128)(2,1)S(1)} %turn.1.turned_ref, bf16[449,128,128]{2,1,0:T(8,128)(2,1)S(1)} %get-tuple-element.34.refs_0_), custom_call_target="tpu_custom_call", output_to_operand_aliasing={{0}: (2, {})} | custom-call | bytes 65536 | tf_op jit(solution)/shard_map/terms_1/pallas_call | solution.py:297
  21.2 1.3 %collective-permute-start.7 = (bf16[4,128,128]{2,1,0:T(8,128)(2,1)S(1)}, bf16[4,128,128]{2,1,0:T(8,128)(2,1)S(1)}, u32[]{:S(2)}, u32[]{:S(2)}) collective-permute-start(bf16[4,128,128]{2,1,0:T(8,128)(2,1)S(1)} %add_convert_fusion), channel_id=1, source_target_pairs={{0,2},{1,3},{2,0},{3,1},{4,6},{5,7},{6,4},{7,5},{8,10},{9,11},{10,... | collective-permute-start | bytes 393224 | tf_op jit(solution)/shard_map/ppermute | solution.py:46
  22.5 1.6 %terms_2.1 = (bf16[449,128,128]{2,1,0:T(8,128)(2,1)S(1)}, f32[4,128,128]{2,1,0:T(8,128)S(1)}) custom-call(s32[1,1024]{1,0:T(1,128)S(1)} %order.1.order_in, bf16[2048,128]{1,0:T(8,128)(2,1)S(1)} %turn.1.turned_ref, bf16[449,128,128]{2,1,0:T(8,128)(2,1)S(1)} %get-tuple-element.38.refs_0_), custom_call_target="tpu_custom_call", output_to_operand_aliasing={{0}: (2, {})} | custom-call | bytes 65536 | tf_op jit(solution)/shard_map/terms_2/pallas_call | solution.py:297
  24.1 0.1 collective-permute-start.8
  24.1 1.6 %terms_3.1 = (bf16[449,128,128]{2,1,0:T(8,128)(2,1)S(1)}, f32[4,128,128]{2,1,0:T(8,128)S(1)}) custom-call(s32[1,1024]{1,0:T(1,128)S(1)} %order.1.order_in, bf16[2048,128]{1,0:T(8,128)(2,1)S(1)} %turn.1.turned_ref, bf16[449,128,128]{2,1,0:T(8,128)(2,1)S(1)} %get-tuple-element.39.refs_0_), custom_call_target="tpu_custom_call", output_to_operand_aliasing={{0}: (2, {})} | custom-call | bytes 65536 | tf_op jit(solution)/shard_map/terms_3/pallas_call | solution.py:297
  25.7 1.0 %collective-permute-done.7 = bf16[4,128,128]{2,1,0:T(8,128)(2,1)S(1)} collective-permute-done((bf16[4,128,128]{2,1,0:T(8,128)(2,1)S(1)}, bf16[4,128,128]{2,1,0:T(8,128)(2,1)S(1)}, u32[]{:S(2)}, u32[]{:S(2)}) %collective-permute-start.7) | collective-permute-done | bytes 131104 | tf_op jit(solution)/shard_map/ppermute | solution.py:46
  26.8 2.6 %collective-permute-start.9 = (bf16[128,128]{1,0:T(8,128)(2,1)S(1)}, bf16[128,128]{1,0:T(8,128)(2,1)S(1)}, u32[]{:S(2)}, u32[]{:S(2)}) collective-permute-start(bf16[128,128]{1,0:T(8,128)(2,1)S(1)} %get-tuple-element.47), channel_id=1, source_target_pairs={{0,12},{1,13},{2,14},{3,15},{4,8},{5,9},{6,10},{7,11},{8,4},{9,5},... | collective-permute-start | bytes 98312 | tf_op jit(solution)/shard_map/ppermute | solution.py:46
  29.4 1.9 %collective-permute-start.10 = (bf16[128,128]{1,0:T(8,128)(2,1)S(1)}, bf16[128,128]{1,0:T(8,128)(2,1)S(1)}, u32[]{:S(2)}, u32[]{:S(2)}) collective-permute-start(bf16[128,128]{1,0:T(8,128)(2,1)S(1)} %get-tuple-element.49), channel_id=1, source_target_pairs={{0,4},{1,5},{2,6},{3,7},{4,0},{5,1},{6,2},{7,3},{8,12},{9,13},{10,... | collective-permute-start | bytes 98312 | tf_op jit(solution)/shard_map/ppermute | solution.py:46
  31.3 1.5 %collective-permute-done.9 = bf16[128,128]{1,0:T(8,128)(2,1)S(1)} collective-permute-done((bf16[128,128]{1,0:T(8,128)(2,1)S(1)}, bf16[128,128]{1,0:T(8,128)(2,1)S(1)}, u32[]{:S(2)}, u32[]{:S(2)}) %collective-permute-start.9) | collective-permute-done | bytes 32800 | tf_op jit(solution)/shard_map/ppermute | solution.py:46
  32.8 1.6 %collective-permute-done.11 = bf16[128,128]{1,0:T(8,128)(2,1)S(1)} collective-permute-done((bf16[128,128]{1,0:T(8,128)(2,1)S(1)}, bf16[128,128]{1,0:T(8,128)(2,1)S(1)}, u32[]{:S(2)}, u32[]{:S(2)}) %collective-permute-start.11) | collective-permute-done | bytes 32800 | tf_op jit(solution)/shard_map/ppermute | solution.py:46
  34.4 0.6 %fusion.3 = f32[1,128,128]{2,1,0:T(8,128)} fusion(f32[4,128,128]{2,1,0:T(8,128)S(1)} %get-tuple-element.46, bf16[128,128]{1,0:T(8,128)(2,1)S(1)} %collective-permute-done.11, bf16[128,128]{1,0:T(8,128)(2,1)S(1)} %collective-permute-done.10, bf16[128,128]{1,0:T(8,128)(2,1)S(1)} %collective-permute-done.9), kind=kLoop, calls=%fused_computation.7 | loop fusion | flops 98304 | bytes 229376 | tf_op jit(solution)/shard_map/broadcast_in_dim | solution.py:364
  (16 shorter events, 0.2 us)
Async XLA Ops:
  0.0 8.4 %collective-permute-start = (bf16[1,128,128]{2,1,0:T(8,128)(2,1)}, bf16[1,128,128]{2,1,0:T(8,128)(2,1)S(1)}, u32[]{:S(2)}, u32[]{:S(2)}) collective-permute-start(bf16[1,128,128]{2,1,0:T(8,128)(2,1)} %in_ref.2), channel_id=1, source_target_pairs={{0,12},{1,13},{2,14},{3,15},{4,8},{5,9},{6,10},{7,11},{8,4},{9,5},... | collective-permute-start | bytes 98312 | tf_op jit(solution)/shard_map/ppermute | solution.py:46
  5.0 5.0 %collective-permute-start.2 = (bf16[1,128,128]{2,1,0:T(8,128)(2,1)}, bf16[1,128,128]{2,1,0:T(8,128)(2,1)S(1)}, u32[]{:S(2)}, u32[]{:S(2)}) collective-permute-start(bf16[1,128,128]{2,1,0:T(8,128)(2,1)} %in_ref.2), channel_id=1, source_target_pairs={{0,8},{1,9},{2,10},{3,11},{4,12},{5,13},{6,14},{7,15},{8,0},{9,1},... | collective-permute-start | bytes 98312 | tf_op jit(solution)/shard_map/ppermute | solution.py:46
  5.1 5.0 %collective-permute-start.1 = (bf16[1,128,128]{2,1,0:T(8,128)(2,1)}, bf16[1,128,128]{2,1,0:T(8,128)(2,1)S(1)}, u32[]{:S(2)}, u32[]{:S(2)}) collective-permute-start(bf16[1,128,128]{2,1,0:T(8,128)(2,1)} %in_ref.2), channel_id=1, source_target_pairs={{0,4},{1,5},{2,6},{3,7},{4,0},{5,1},{6,2},{7,3},{8,12},{9,13},{10,... | collective-permute-start | bytes 98312 | tf_op jit(solution)/shard_map/ppermute | solution.py:46
  7.0 0.8 %copy-start.2 = (bf16[1,128,128]{2,1,0:T(8,128)(2,1)S(1)}, bf16[1,128,128]{2,1,0:T(8,128)(2,1)}, u32[]{:S(2)}) copy-start(bf16[1,128,128]{2,1,0:T(8,128)(2,1)} %in_ref.2) | copy-start | bytes 98308
  10.1 5.0 %collective-permute-start.3 = (bf16[4,128,128]{2,1,0:T(8,128)(2,1)S(1)}, bf16[4,128,128]{2,1,0:T(8,128)(2,1)S(1)}, u32[]{:S(2)}, u32[]{:S(2)}) collective-permute-start(bf16[4,128,128]{2,1,0:T(8,128)(2,1)S(1)} %pad_maximum_fusion.psi_ref), channel_id=1, source_target_pairs={{0,2},{1,3},{2,0},{3,1},{4,6},{5,7},{6,4},{7,5},{8,10},{9,11},{10,... | collective-permute-start | bytes 393224 | tf_op jit(solution)/shard_map/ppermute | solution.py:46
  11.7 1.0 %copy-start = (bf16[16,128,128]{2,1,0:T(8,128)(2,1)S(1)}, bf16[16,128,128]{2,1,0:T(8,128)(2,1)}, u32[]{:S(2)}) copy-start(bf16[16,128,128]{2,1,0:T(8,128)(2,1)} %in_ref.3) | copy-start | bytes 1572868
  12.7 1.0 %copy-start.1 = (bf16[16,128,128]{2,1,0:T(8,128)(2,1)S(1)}, bf16[16,128,128]{2,1,0:T(8,128)(2,1)}, u32[]{:S(2)}) copy-start(bf16[16,128,128]{2,1,0:T(8,128)(2,1)} %right_ref.1) | copy-start | bytes 1572868
  14.7 1.4 %collective-permute-start.5 = (bf16[4,128,128]{2,1,0:T(8,128)(2,1)S(1)}, bf16[4,128,128]{2,1,0:T(8,128)(2,1)S(1)}, u32[]{:S(2)}, u32[]{:S(2)}) collective-permute-start(bf16[4,128,128]{2,1,0:T(8,128)(2,1)S(1)} %pad_maximum_fusion.psi_ref), channel_id=1, source_target_pairs={{0,1},{1,0},{2,3},{3,2},{4,5},{5,4},{6,7},{7,6},{8,9},{9,8},{10,11... | collective-permute-start | bytes 393224 | tf_op jit(solution)/shard_map/ppermute | solution.py:46
  15.1 1.6 %collective-permute-start.4 = (bf16[4,128,128]{2,1,0:T(8,128)(2,1)S(1)}, bf16[4,128,128]{2,1,0:T(8,128)(2,1)S(1)}, u32[]{:S(2)}, u32[]{:S(2)}) collective-permute-start(bf16[4,128,128]{2,1,0:T(8,128)(2,1)S(1)} %collective-permute-done.3.psi_ref), channel_id=1, source_target_pairs={{0,1},{1,0},{2,3},{3,2},{4,5},{5,4},{6,7},{7,6},{8,9},{9,8},{10,11... | collective-permute-start | bytes 393224 | tf_op jit(solution)/shard_map/ppermute | solution.py:46
  19.2 1.9 %collective-permute-start.6 = (f32[4,128,128]{2,1,0:T(8,128)S(1)}, f32[4,128,128]{2,1,0:T(8,128)S(1)}, u32[]{:S(2)}, u32[]{:S(2)}) collective-permute-start(f32[4,128,128]{2,1,0:T(8,128)S(1)} %get-tuple-element.36), channel_id=1, source_target_pairs={{0,1},{1,0},{2,3},{3,2},{4,5},{5,4},{6,7},{7,6},{8,9},{9,8},{10,11... | collective-permute-start | bytes 786440 | tf_op jit(solution)/shard_map/ppermute | solution.py:46
  21.2 5.6 %collective-permute-start.7 = (bf16[4,128,128]{2,1,0:T(8,128)(2,1)S(1)}, bf16[4,128,128]{2,1,0:T(8,128)(2,1)S(1)}, u32[]{:S(2)}, u32[]{:S(2)}) collective-permute-start(bf16[4,128,128]{2,1,0:T(8,128)(2,1)S(1)} %add_convert_fusion), channel_id=1, source_target_pairs={{0,2},{1,3},{2,0},{3,1},{4,6},{5,7},{6,4},{7,5},{8,10},{9,11},{10,... | collective-permute-start | bytes 393224 | tf_op jit(solution)/shard_map/ppermute | solution.py:46
  24.1 2.7 %collective-permute-start.8 = (f32[4,128,128]{2,1,0:T(8,128)S(1)}, f32[4,128,128]{2,1,0:T(8,128)S(1)}, u32[]{:S(2)}, u32[]{:S(2)}) collective-permute-start(f32[4,128,128]{2,1,0:T(8,128)S(1)} %get-tuple-element.42), channel_id=1, source_target_pairs={{0,1},{1,0},{2,3},{3,2},{4,5},{5,4},{6,7},{7,6},{8,9},{9,8},{10,11... | collective-permute-start | bytes 786440 | tf_op jit(solution)/shard_map/ppermute | solution.py:46
  26.8 6.0 %collective-permute-start.9 = (bf16[128,128]{1,0:T(8,128)(2,1)S(1)}, bf16[128,128]{1,0:T(8,128)(2,1)S(1)}, u32[]{:S(2)}, u32[]{:S(2)}) collective-permute-start(bf16[128,128]{1,0:T(8,128)(2,1)S(1)} %get-tuple-element.47), channel_id=1, source_target_pairs={{0,12},{1,13},{2,14},{3,15},{4,8},{5,9},{6,10},{7,11},{8,4},{9,5},... | collective-permute-start | bytes 98312 | tf_op jit(solution)/shard_map/ppermute | solution.py:46
  29.4 5.0 %collective-permute-start.11 = (bf16[128,128]{1,0:T(8,128)(2,1)S(1)}, bf16[128,128]{1,0:T(8,128)(2,1)S(1)}, u32[]{:S(2)}, u32[]{:S(2)}) collective-permute-start(bf16[128,128]{1,0:T(8,128)(2,1)S(1)} %get-tuple-element.48), channel_id=1, source_target_pairs={{0,8},{1,9},{2,10},{3,11},{4,12},{5,13},{6,14},{7,15},{8,0},{9,1},... | collective-permute-start | bytes 98312 | tf_op jit(solution)/shard_map/ppermute | solution.py:46
  29.4 5.0 %collective-permute-start.10 = (bf16[128,128]{1,0:T(8,128)(2,1)S(1)}, bf16[128,128]{1,0:T(8,128)(2,1)S(1)}, u32[]{:S(2)}, u32[]{:S(2)}) collective-permute-start(bf16[128,128]{1,0:T(8,128)(2,1)S(1)} %get-tuple-element.49), channel_id=1, source_target_pairs={{0,4},{1,5},{2,6},{3,7},{4,0},{5,1},{6,2},{7,3},{8,12},{9,13},{10,... | collective-permute-start | bytes 98312 | tf_op jit(solution)/shard_map/ppermute | solution.py:46
